TPU v7x, 32 devices: a whole 2x2x4 slice. The times are simulated.
32 devices in a mesh: tm: 16 (over z, x, core), freq: 2 (over y).
Axes of the slice: x: 2, y: 2, z: 4, core: 2. Of those that a mesh axis runs over, the one named last changes fastest.
Arguments:
- features: bfloat16 [128, 256, 256], P('tm', 'freq'), may hold values from -6 to 6
- upstream: bfloat16 [128, 256, 256], P('tm', 'freq'), may hold values from -6 to 6
- weights: bfloat16 [8, 256, 256], replicated, may hold values from -8 to 8
- gains: float32 [2, 256], replicated, may hold values from 0.5 to 1.5
Outputs:
- grad_input: bfloat16 [128, 256, 256], P('tm', 'freq')
- weight_grads: float32 [8, 256, 256], replicated
- gain_grads: float32 [2, 256], replicated
All inputs are finite; a program needn't handle non-finite values.
Results may differ from a plain program's by a relative error of at most 0.02.
Values may be sent and summed in bfloat16 or wider, within the bound.
No kernel may reach another device: no remote copies, remote signals or barrier semaphores. Data moves between devices by JAX's collectives and lax.ppermute only.
A program may use at most 128 MiB of HBM per device.

v0:
```python
import jax
import jax.numpy as jnp
from jax import lax
from jax.sharding import PartitionSpec as P

HEADS = 4
WINDOW = 128


epsilon = 1e-06
masked_score = -1e30


def passed_along(block, axis, distance):
    devices = range(lax.axis_size(axis))
    route = [(i - distance, i) for i in devices if i - distance in devices]
    return lax.ppermute(block, axis, route)


def norm_forward(inputs, gain):
    widened = inputs.astype(jnp.float32)
    inverse = lax.rsqrt(jnp.mean(widened * widened, axis=-1, keepdims=True) + epsilon)
    unit_rows = widened * inverse
    return ((unit_rows * gain).astype(jnp.bfloat16), inverse, unit_rows)


def norm_backward(incoming, inverse, unit_rows, gain):
    scaled = incoming * gain
    result = inverse * (scaled - unit_rows * jnp.mean(scaled * unit_rows, axis=-1, keepdims=True))
    gain_grad = jnp.sum((incoming * unit_rows).reshape(-1, unit_rows.shape[-1]), axis=0)
    return (result, gain_grad)


def project(inputs, matrix):
    flat_rows = inputs.reshape(-1, inputs.shape[-1])
    product = jnp.dot(flat_rows, matrix, preferred_element_type=jnp.float32)
    return product.reshape(inputs.shape[:-1] + (matrix.shape[1],))


def project_back(grads, matrices):
    running = jnp.zeros((grads[0].size // grads[0].shape[-1], matrices[0].shape[0]), jnp.float32)
    for grad_part, matrix in zip(grads, matrices):
        flat_rows = grad_part.reshape(-1, grad_part.shape[-1])
        running = running + lax.dot_general(
            flat_rows, matrix, (((1,), (1,)), ((), ())), preferred_element_type=jnp.float32
        )
    return running.reshape(grads[0].shape[:-1] + (matrices[0].shape[0],))


def weight_grad(inputs, grads):
    return lax.dot_general(
        inputs.reshape(-1, inputs.shape[-1]),
        grads.reshape(-1, grads.shape[-1]),
        (((0,), (0,)), ((), ())),
        preferred_element_type=jnp.float32,
    )


def channel_masks(width, ndim, dtype):
    owner = jnp.arange(width, dtype=jnp.int32)[None, :] // (width // HEADS)
    chosen = (owner == jnp.arange(HEADS, dtype=jnp.int32)[:, None]).astype(dtype)
    return chosen.reshape((HEADS,) + (1,) * ndim + (width,))


def spread_heads(rows):
    return rows[None] * channel_masks(rows.shape[-1], rows.ndim - 1, rows.dtype)


def collect_heads(stacked):
    return jnp.sum(
        stacked * channel_masks(stacked.shape[-1], stacked.ndim - 2, jnp.float32), axis=0
    )


def head_scale(rows):
    return (rows.shape[-1] // HEADS) ** (-0.5)


def attend(queries, key_rows, value_rows, allowed, query_form, key_form):
    scaling = head_scale(queries)
    scores = (
        jnp.einsum(
            "h" + query_form + "," + key_form + "->bhqk",
            spread_heads(queries),
            key_rows,
            preferred_element_type=jnp.float32,
        )
        * scaling
    )
    scores = jnp.where(allowed, scores, masked_score)
    largest = jnp.max(scores, axis=-1, keepdims=True)
    log_total = largest + jnp.log(jnp.sum(jnp.exp(scores - largest), axis=-1, keepdims=True))
    attention = jnp.exp(scores - log_total)
    stacked = jnp.einsum(
        "bhqk," + key_form + "->h" + query_form,
        attention.astype(jnp.bfloat16),
        value_rows,
        preferred_element_type=jnp.float32,
    )
    mixed_rows = collect_heads(stacked).astype(jnp.bfloat16)
    return (mixed_rows, log_total[..., 0], attention)


def query_backward(attention, grad_out, key_rows, value_rows, query_form, key_form):
    scaling = head_scale(key_rows)
    grad_attention = jnp.einsum(
        "h" + query_form + "," + key_form + "->bhqk",
        spread_heads(grad_out),
        value_rows,
        preferred_element_type=jnp.float32,
    )
    row_dot = jnp.sum(grad_attention * attention, axis=-1, keepdims=True)
    grad_scores = (attention * (grad_attention - row_dot) * scaling).astype(jnp.bfloat16)
    stacked = jnp.einsum(
        "bhqk," + key_form + "->h" + query_form,
        grad_scores,
        key_rows,
        preferred_element_type=jnp.float32,
    )
    grad_queries = collect_heads(stacked).astype(jnp.bfloat16)
    return (grad_queries, row_dot[..., 0], grad_scores)


def key_terms(attention, grad_scores, queries, grad_out, query_form, key_form):
    grad_keys = collect_heads(
        jnp.einsum(
            "bhqk," + query_form + "->h" + key_form,
            grad_scores,
            queries,
            preferred_element_type=jnp.float32,
        )
    )
    grad_values = collect_heads(
        jnp.einsum(
            "bhqk," + query_form + "->h" + key_form,
            attention.astype(jnp.bfloat16),
            grad_out,
            preferred_element_type=jnp.float32,
        )
    )
    return (grad_keys, grad_values)


def key_backward(
    queries, grad_out, log_total, row_dot, key_rows, value_rows, allowed, query_form, key_form
):
    scaling = head_scale(key_rows)
    scores = (
        jnp.einsum(
            query_form + ",h" + key_form + "->bhqk",
            queries,
            spread_heads(key_rows),
            preferred_element_type=jnp.float32,
        )
        * scaling
    )
    scores = jnp.where(allowed, scores, masked_score)
    attention = jnp.exp(scores - log_total[..., None])
    grad_attention = jnp.einsum(
        query_form + ",h" + key_form + "->bhqk",
        grad_out,
        spread_heads(value_rows),
        preferred_element_type=jnp.float32,
    )
    grad_scores = (attention * (grad_attention - row_dot[..., None]) * scaling).astype(jnp.bfloat16)
    return key_terms(attention, grad_scores, queries, grad_out, query_form, key_form)


def window_masks(first_frame, frames_dev, window, total_frames):
    half_window = window // 2
    row_ids = jnp.arange(frames_dev, dtype=jnp.int32)[:, None]
    col_ids = jnp.arange(frames_dev + window, dtype=jnp.int32)[None, :]
    frame_ids = first_frame - half_window + col_ids
    inside = (frame_ids >= 0) & (frame_ids < total_frames)
    distance = col_ids - row_ids
    ahead_mask = (distance >= 0) & (distance < window) & inside
    behind_mask = (distance.T >= 1) & (distance.T <= window) & inside.T
    return (ahead_mask, behind_mask)


def per_device(features, upstream, weights, gains):
    frames_dev = features.shape[0]
    bins_dev = features.shape[1]
    total_frames = frames_dev * lax.axis_size("tm")
    hops = WINDOW // 2 // frames_dev
    lower_rows = hops * frames_dev
    first_frame = lax.axis_index("tm") * frames_dev
    ahead_mask, behind_mask = window_masks(first_frame, frames_dev, WINDOW, total_frames)
    window_offsets = [offset for offset in range(-hops, hops + 1) if offset != 0]
    norm_one, inverse_one, unit_one = norm_forward(features, gains[0])
    query_one = project(norm_one, weights[0]).astype(jnp.bfloat16)
    key_one = project(norm_one, weights[1]).astype(jnp.bfloat16)
    value_one = project(norm_one, weights[2]).astype(jnp.bfloat16)
    moved = (
        lax.all_to_all(query_one, "freq", split_axis=0, concat_axis=1, tiled=True),
        lax.all_to_all(key_one, "freq", split_axis=0, concat_axis=1, tiled=True),
        lax.all_to_all(value_one, "freq", split_axis=0, concat_axis=1, tiled=True),
    )
    frame_query = moved[0]
    frame_key = moved[1]
    frame_value = moved[2]
    freq_out, _, freq_attention = attend(frame_query, frame_key, frame_value, True, "bqc", "bkc")
    mixed_one = lax.all_to_all(freq_out, "freq", split_axis=1, concat_axis=0, tiled=True)
    hidden = (features.astype(jnp.float32) + project(mixed_one, weights[3])).astype(jnp.bfloat16)
    norm_two, inverse_two, unit_two = norm_forward(hidden, gains[1])
    query_two = project(norm_two, weights[4]).astype(jnp.bfloat16)
    key_two = project(norm_two, weights[5]).astype(jnp.bfloat16)
    value_two = project(norm_two, weights[6]).astype(jnp.bfloat16)
    arrived = [passed_along(norm_two, "tm", -offset) for offset in window_offsets]
    remote_norm = jnp.concatenate(arrived, axis=0)
    remote_query = project(remote_norm, weights[4]).astype(jnp.bfloat16)
    remote_key = project(remote_norm, weights[5]).astype(jnp.bfloat16)
    remote_value = project(remote_norm, weights[6]).astype(jnp.bfloat16)

    def windowed(remote_rows, local_rows):
        return jnp.concatenate(
            [remote_rows[:lower_rows], local_rows, remote_rows[lower_rows:]], axis=0
        )

    window_query = windowed(remote_query, query_two)
    window_key = windowed(remote_key, key_two)
    window_value = windowed(remote_value, value_two)
    mixed_two, log_two, time_attention = attend(
        query_two, window_key, window_value, ahead_mask[None, None], "qbc", "kbc"
    )
    grad_mixed_two = project_back([upstream], [weights[7]]).astype(jnp.bfloat16)
    grad_query_two, row_two, _ = query_backward(
        time_attention, grad_mixed_two, window_key, window_value, "qbc", "kbc"
    )
    grad_arrived = [passed_along(grad_mixed_two, "tm", -offset) for offset in window_offsets]
    stats_arrived = [passed_along((log_two, row_two), "tm", -offset) for offset in window_offsets]
    remote_grad = jnp.concatenate(grad_arrived, axis=0)
    remote_log = jnp.concatenate([piece[0] for piece in stats_arrived], axis=2)
    remote_row = jnp.concatenate([piece[1] for piece in stats_arrived], axis=2)
    window_grad = windowed(remote_grad, grad_mixed_two)
    window_log = jnp.concatenate(
        [remote_log[:, :, :lower_rows], log_two, remote_log[:, :, lower_rows:]], axis=2
    )
    window_row = jnp.concatenate(
        [remote_row[:, :, :lower_rows], row_two, remote_row[:, :, lower_rows:]], axis=2
    )
    grad_key_two, grad_value_two = key_backward(
        window_query,
        window_grad,
        window_log,
        window_row,
        key_two,
        value_two,
        behind_mask[None, None],
        "qbc",
        "kbc",
    )
    grad_key_two = grad_key_two.astype(jnp.bfloat16)
    grad_value_two = grad_value_two.astype(jnp.bfloat16)
    grad_norm_two = project_back(
        [grad_query_two, grad_key_two, grad_value_two], [weights[4], weights[5], weights[6]]
    )
    hidden_part, gain_two = norm_backward(grad_norm_two, inverse_two, unit_two, gains[1])
    grad_hidden = (upstream.astype(jnp.float32) + hidden_part).astype(jnp.bfloat16)
    time_stack = jnp.stack(
        [
            weight_grad(norm_two, grad_query_two),
            weight_grad(norm_two, grad_key_two),
            weight_grad(norm_two, grad_value_two),
            weight_grad(mixed_two, upstream),
        ]
    )
    grad_mixed_one = project_back([grad_hidden], [weights[3]]).astype(jnp.bfloat16)
    frame_grad = lax.all_to_all(grad_mixed_one, "freq", split_axis=0, concat_axis=1, tiled=True)
    grad_frame_query, _, grad_scores = query_backward(
        freq_attention, frame_grad, frame_key, frame_value, "bqc", "bkc"
    )
    grad_frame_key, grad_frame_value = key_terms(
        freq_attention, grad_scores, frame_query, frame_grad, "bqc", "bkc"
    )
    returned = (
        lax.all_to_all(grad_frame_query, "freq", split_axis=1, concat_axis=0, tiled=True),
        lax.all_to_all(
            grad_frame_key.astype(jnp.bfloat16), "freq", split_axis=1, concat_axis=0, tiled=True
        ),
        lax.all_to_all(
            grad_frame_value.astype(jnp.bfloat16), "freq", split_axis=1, concat_axis=0, tiled=True
        ),
    )
    grad_norm_one = project_back(
        [returned[0], returned[1], returned[2]], [weights[0], weights[1], weights[2]]
    )
    input_part, gain_one = norm_backward(grad_norm_one, inverse_one, unit_one, gains[0])
    grad_input = (grad_hidden.astype(jnp.float32) + input_part).astype(jnp.bfloat16)
    freq_stack = jnp.stack(
        [
            weight_grad(norm_one, returned[0]),
            weight_grad(norm_one, returned[1]),
            weight_grad(norm_one, returned[2]),
            weight_grad(mixed_one, grad_hidden),
        ]
    )
    summed = lax.psum(
        (jnp.concatenate([freq_stack, time_stack], axis=0), jnp.stack([gain_one, gain_two])),
        ("tm", "freq"),
    )
    weight_grads = summed[0]
    gain_grads = summed[1]
    inv_root = (total_frames * bins_dev * lax.axis_size("freq")) ** (-0.5)
    return (grad_input, weight_grads * inv_root, gain_grads * inv_root)


def solution(mesh):
    return jax.shard_map(
        per_device,
        mesh=mesh,
        in_specs=(P("tm", "freq", None), P("tm", "freq", None), P(), P()),
        out_specs=(P("tm", "freq", None), P(), P()),
        check_vma=False,
    )
```

profile of v0, /device:TPU:0, one launch (start us, length us, event | category | flops | bytes accessed | tf_op | source)
XLA Modules:
  0.0 932.9 jit_solution(8629153750614957040)
XLA Ops:
  82.7 20.3 %collective-permute-start.38 = (bf16[8,128,256]{2,1,0:T(8,128)(2,1)}, bf16[8,128,256]{2,1,0:T(8,128)(2,1)S(1)}, u32[]{:S(2)}, u32[]{:S(2)}) collective-permute-start(bf16[8,128,256]{2,1,0:T(8,128)(2,1)} %convolution_convert_fusion.5), channel_id=1, source_target_pairs={{0,4},{2,6},{4,8},{6,10},{8,12},{10,14},{12,16},{14,18},{16,20},{1... | collective-permute-start | bytes 1572872 | tf_op jit(solution)/shard_map/ppermute | solution.py:17
  104.1 25.7 %collective-permute-start.39 = (bf16[8,128,256]{2,1,0:T(8,128)(2,1)}, bf16[8,128,256]{2,1,0:T(8,128)(2,1)S(1)}, u32[]{:S(2)}, u32[]{:S(2)}) collective-permute-start(bf16[8,128,256]{2,1,0:T(8,128)(2,1)} %convolution_convert_fusion.5), channel_id=1, source_target_pairs={{0,2},{2,4},{4,6},{6,8},{8,10},{10,12},{12,14},{14,16},{16,18},{18... | collective-permute-start | bytes 1572872 | tf_op jit(solution)/shard_map/ppermute | solution.py:17
  142.2 22.6 %collective-permute-done.41 = bf16[8,128,256]{2,1,0:T(8,128)(2,1)S(1)} collective-permute-done((bf16[8,128,256]{2,1,0:T(8,128)(2,1)}, bf16[8,128,256]{2,1,0:T(8,128)(2,1)S(1)}, u32[]{:S(2)}, u32[]{:S(2)}) %collective-permute-start.41) | collective-permute-done | bytes 524320 | tf_op jit(solution)/shard_map/ppermute | solution.py:17
  167.5 19.0 %collective-permute-done.43 = bf16[8,128,256]{2,1,0:T(8,128)(2,1)S(1)} collective-permute-done((bf16[8,128,256]{2,1,0:T(8,128)(2,1)}, bf16[8,128,256]{2,1,0:T(8,128)(2,1)S(1)}, u32[]{:S(2)}, u32[]{:S(2)}) %collective-permute-start.43) | collective-permute-done | bytes 524320 | tf_op jit(solution)/shard_map/ppermute | solution.py:17
  186.5 46.9 %collective-permute-start = (bf16[8,128,256]{2,1,0:T(8,128)(2,1)S(1)}, bf16[8,128,256]{2,1,0:T(8,128)(2,1)S(1)}, u32[]{:S(2)}, u32[]{:S(2)}) collective-permute-start(bf16[8,128,256]{2,1,0:T(8,128)(2,1)S(1)} %fusion.119), channel_id=1, source_target_pairs={{0,16},{2,18},{4,20},{6,22},{8,24},{10,26},{12,28},{14,30},{1,17},... | collective-permute-start | bytes 1572872 | tf_op jit(solution)/shard_map/ppermute | solution.py:17
  237.7 22.2 %collective-permute-done.47 = bf16[8,128,256]{2,1,0:T(8,128)(2,1)S(1)} collective-permute-done((bf16[8,128,256]{2,1,0:T(8,128)(2,1)}, bf16[8,128,256]{2,1,0:T(8,128)(2,1)S(1)}, u32[]{:S(2)}, u32[]{:S(2)}) %collective-permute-start.47) | collective-permute-done | bytes 524320 | tf_op jit(solution)/shard_map/ppermute | solution.py:17
  269.8 8.9 collective-permute-done.3
  280.1 9.9 %collective-permute-done.4 = bf16[8,128,256]{2,1,0:T(8,128)(2,1)S(1)} collective-permute-done((bf16[8,128,256]{2,1,0:T(8,128)(2,1)S(1)}, bf16[8,128,256]{2,1,0:T(8,128)(2,1)S(1)}, u32[]{:S(2)}, u32[]{:S(2)}) %collective-permute-start.4) | collective-permute-done | bytes 524320 | tf_op jit(solution)/shard_map/ppermute | solution.py:17
  292.7 15.3 %collective-permute-done.6 = bf16[8,128,256]{2,1,0:T(8,128)(2,1)S(1)} collective-permute-done((bf16[8,128,256]{2,1,0:T(8,128)(2,1)S(1)}, bf16[8,128,256]{2,1,0:T(8,128)(2,1)S(1)}, u32[]{:S(2)}, u32[]{:S(2)}) %collective-permute-start.6) | collective-permute-done | bytes 524320 | tf_op jit(solution)/shard_map/ppermute | solution.py:17
  315.1 12.1 %collective-permute-done.11 = bf16[8,128,256]{2,1,0:T(8,128)(2,1)S(1)} collective-permute-done((bf16[8,128,256]{2,1,0:T(8,128)(2,1)S(1)}, bf16[8,128,256]{2,1,0:T(8,128)(2,1)S(1)}, u32[]{:S(2)}, u32[]{:S(2)}) %collective-permute-start.11) | collective-permute-done | bytes 524320 | tf_op jit(solution)/shard_map/ppermute | solution.py:17
  330.6 18.9 %collective-permute-done.13 = bf16[8,128,256]{2,1,0:T(8,128)(2,1)S(1)} collective-permute-done((bf16[8,128,256]{2,1,0:T(8,128)(2,1)S(1)}, bf16[8,128,256]{2,1,0:T(8,128)(2,1)S(1)}, u32[]{:S(2)}, u32[]{:S(2)}) %collective-permute-start.13) | collective-permute-done | bytes 524320 | tf_op jit(solution)/shard_map/ppermute | solution.py:17
  355.4 57.4 %collective-permute-done.15 = bf16[8,128,256]{2,1,0:T(8,128)(2,1)S(1)} collective-permute-done((bf16[8,128,256]{2,1,0:T(8,128)(2,1)S(1)}, bf16[8,128,256]{2,1,0:T(8,128)(2,1)S(1)}, u32[]{:S(2)}, u32[]{:S(2)}) %collective-permute-start.15) | collective-permute-done | bytes 524320 | tf_op jit(solution)/shard_map/ppermute | solution.py:17
  432.3 11.2 %fusion.30 = (f32[128,4,8]{2,1,0:T(4,128)S(1)}, f32[128,4,8,136]{3,2,1,0:T(8,128)}) fusion(pred[8,136]{1,0:T(8,128)(4,1)S(1)} %fusion.199, bf16[136,128,256,1]{2,1,0,3:T(8,128)(2,1)} %maximum_bitcast_fusion, bf16[4,256]{1,0:T(4,128)(2,1)S(1)} %get-tuple-element.17, bf16[8,128,256]{2,0,1:T(8,128)(2,1)S(1)} %copy.142), kind=kOutput, calls=%fused_computation.56 | convolution fusion | flops 287928320 | bytes 11684928 | tf_op jit(solution)/shard_map/hqbc,kbc->bhqk/dot_general | solution.py:82
  462.4 12.2 %multiply_reduce_fusion.1 = (f32[128,4,8]{2,1,0:T(4,128)}, f32[128,4,8,136]{3,2,1,0:T(8,128)}) fusion(f32[128,4,8,136]{3,2,1,0:T(8,128)S(1)} %copy-done.6, f32[128,4,8]{2,1,0:T(4,128)S(1)} %bitcast.314, pred[8,136]{1,0:T(8,128)(4,1)S(1)} %fusion.199, bf16[136,128,256,1]{2,1,0,3:T(8,128)(2,1)} %maximum_bitcast_fusion.1, ...), kind=kOutput, calls=%fused_computation.49 | convolution fusion | flops 289042432 | bytes 13929536 | tf_op jit(solution)/shard_map/hqbc,kbc->bhqk/dot_general | solution.py:106
  474.6 11.2 %fusion.27 = bf16[8,128,256]{2,0,1:T(8,128)(2,1)S(1)} fusion(bf16[136,128,256,1]{2,1,0,3:T(8,128)(2,1)} %maximum_bitcast_fusion, f32[128,4,8,136]{3,2,1,0:T(8,128)} %get-tuple-element.26, f32[128,4,8,136]{3,2,1,0:T(8,128)S(1)} %copy-done.6, f32[4,256]{1,0:T(4,128)S(1)} %get-tuple-element.18, f32[128,4,8]{2,1,0:T(4,128)} %get-tuple-element.25, ...), kind=kOutput, calls=%fused_computation.42 | convolution fusion | flops 290947072 | bytes 13931584 | tf_op jit(solution)/shard_map/bhqk,kbc->hqbc/dot_general | solution.py:114
  547.9 7.5 fusion.3
  581.8 10.7 %collective-permute-start.53 = (f32[128,4,8]{2,1,0:T(4,128)}, f32[128,4,8]{2,1,0:T(4,128)}, u32[]{:S(2)}, u32[]{:S(2)}) collective-permute-start(f32[128,4,8]{2,1,0:T(4,128)} %get-tuple-element.25), channel_id=1, source_target_pairs={{0,6},{2,8},{4,10},{6,12},{8,14},{10,16},{12,18},{14,20},{16,22},{... | collective-permute-start | bytes 49160 | tf_op jit(solution)/shard_map/ppermute | solution.py:17
  615.3 11.5 %fusion.17 = bf16[8,128,256]{2,0,1:T(8,128)(2,1)} fusion(bf16[136,128,256]{2,1,0:T(8,128)(2,1)} %copy-done.35, f32[128,4,8,136]{3,2,1,0:T(8,128)} %fusion.3, f32[128,4,136]{2,1,0:T(4,128)} %concatenate.40, f32[4,256]{1,0:T(4,128)S(1)} %get-tuple-element.18, pred[136,8]{0,1:T(8,128)(4,1)S(1)} %fusion.201), kind=kOutput, calls=%fused_computation.24 | convolution fusion | flops 289275904 | bytes 11949120
  637.9 20.2 %fusion.18 = bf16[8,128,256]{2,0,1:T(8,128)(2,1)} fusion(bf16[136,128,256]{2,1,0:T(8,128)(2,1)} %get-tuple-element.8, f32[128,4,8,136]{3,2,1,0:T(8,128)} %fusion.3, f32[128,4,136]{2,1,0:T(4,128)} %concatenate.42, f32[128,4,136]{2,1,0:T(4,128)} %concatenate.40, f32[4,256]{1,0:T(4,128)S(1)} %get-tuple-element.18, pred[136,8]{0,1:T(8,128)(4,1)S(1)} %fusion.201, ...), kind=kOutput, calls=%fused_computation.26 | convolution fusion | flops 577208320 | bytes 21666880
  699.5 9.9 %fusion.22 = bf16[4,256,256]{1,2,0:T(8,128)(2,1)} fusion(f32[4,256]{1,0:T(4,128)S(1)} %get-tuple-element.18, bf16[4,256,256,1]{2,1,3,0:T(8,128)(2,1)} %bitcast.334, f32[4,4,256,256]{2,3,1,0:T(8,128)} %fusion.55, f32[4,4,256,256]{2,3,1,0:T(8,128)} %copy-done.5, f32[4,4,256]{2,1,0:T(4,128)S(1)} %bitcast.347), kind=kOutput, calls=%fused_computation.34 | convolution fusion | flops 548147456 | bytes 9457664 | tf_op jit(solution)/shard_map/bhqk,bkc->hbqc/dot_general | solution.py:114
  719.9 9.8 %fusion.21 = bf16[4,256,256]{1,2,0:T(8,128)(2,1)} fusion(f32[4,256]{1,0:T(4,128)S(1)} %get-tuple-element.18, f32[4,4,256,256]{2,3,1,0:T(8,128)} %fusion.55, f32[4,4,256,256]{2,3,1,0:T(8,128)} %copy-done.5, f32[4,4,256]{2,1,0:T(4,128)S(1)} %bitcast.348, bf16[4,256,256,1]{1,2,0,3:T(8,128)(2,1)} %reshape.370), kind=kOutput, calls=%fused_computation.32 | convolution fusion | flops 548147456 | bytes 9457664 | tf_op jit(solution)/shard_map/bhqk,bqc->hbkc/dot_general | solution.py:126
  736.3 12.0 %fusion.19 = bf16[8,128,256]{2,0,1:T(8,128)(2,1)} fusion(bf16[136,128,256,1]{2,1,0,3:T(8,128)(2,1)} %maximum_bitcast_fusion.1, f32[128,4,8,136]{3,2,1,0:T(8,128)} %get-tuple-element.24, f32[4,256]{1,0:T(4,128)S(1)} %get-tuple-element.18, f32[128,4,8]{2,1,0:T(4,128)S(1)} %bitcast.328, pred[8,136]{1,0:T(8,128)(4,1)S(1)} %fusion.199), kind=kOutput, calls=%fused_computation.28 | convolution fusion | flops 289275904 | bytes 11686976 | tf_op jit(solution)/shard_map/bhqk,kbc->hqbc/dot_general | solution.py:94
  766.7 61.1 %psum.15 = f32[2,256]{1,0:T(2,128)S(1)} all-reduce(f32[2,256]{1,0:T(2,128)S(1)} %pad_maximum_fusion.1), channel_id=1, replica_groups=mesh['tm'=16,'freq'=2] {'tm','freq'}, use_global_device_ids=true, to_apply=%region_21.22 | all-reduce | flops 512 | bytes 4096 | tf_op jit(solution)/shard_map/psum | solution.py:298
  829.6 93.0 %all-reduce.2.cloned.1.call-done = f32[8,256,256]{2,1,0:T(8,128)} async-done(((f32[8,256,256]{2,1,0:T(8,128)}), f32[8,256,256]{2,1,0:T(8,128)}) %all-reduce.2.cloned.1.call-update) | async-done | bytes 2097168 | tf_op jit(solution)/shard_map/psum | solution.py:298
  (331 shorter events, 367.1 us)
Async XLA Ops:
  18.9 114.3 %collective-permute-start.36 = (bf16[8,128,256]{2,1,0:T(8,128)(2,1)}, bf16[8,128,256]{2,1,0:T(8,128)(2,1)}, u32[]{:S(2)}, u32[]{:S(2)}) collective-permute-start(bf16[8,128,256]{2,1,0:T(8,128)(2,1)} %convolution_convert_fusion.5), channel_id=1, source_target_pairs={{0,8},{2,10},{4,12},{6,14},{8,16},{10,18},{12,20},{14,22},{16,24},... | collective-permute-start | bytes 1572872 | tf_op jit(solution)/shard_map/ppermute | solution.py:17
  23.9 106.9 %collective-permute-start.35 = (bf16[8,128,256]{2,1,0:T(8,128)(2,1)}, bf16[8,128,256]{2,1,0:T(8,128)(2,1)}, u32[]{:S(2)}, u32[]{:S(2)}) collective-permute-start(bf16[8,128,256]{2,1,0:T(8,128)(2,1)} %convolution_convert_fusion.5), channel_id=1, source_target_pairs={{0,10},{2,12},{4,14},{6,16},{8,18},{10,20},{12,22},{14,24},{16,26}... | collective-permute-start | bytes 1572872 | tf_op jit(solution)/shard_map/ppermute | solution.py:17
  26.6 77.5 %collective-permute-start.34 = (bf16[8,128,256]{2,1,0:T(8,128)(2,1)}, bf16[8,128,256]{2,1,0:T(8,128)(2,1)}, u32[]{:S(2)}, u32[]{:S(2)}) collective-permute-start(bf16[8,128,256]{2,1,0:T(8,128)(2,1)} %convolution_convert_fusion.5), channel_id=1, source_target_pairs={{0,12},{2,14},{4,16},{6,18},{8,20},{10,22},{12,24},{14,26},{16,28}... | collective-permute-start | bytes 1572872 | tf_op jit(solution)/shard_map/ppermute | solution.py:17
  31.0 51.7 %collective-permute-start.33 = (bf16[8,128,256]{2,1,0:T(8,128)(2,1)}, bf16[8,128,256]{2,1,0:T(8,128)(2,1)}, u32[]{:S(2)}, u32[]{:S(2)}) collective-permute-start(bf16[8,128,256]{2,1,0:T(8,128)(2,1)} %convolution_convert_fusion.5), channel_id=1, source_target_pairs={{0,14},{2,16},{4,18},{6,20},{8,22},{10,24},{12,26},{14,28},{16,30}... | collective-permute-start | bytes 1572872 | tf_op jit(solution)/shard_map/ppermute | solution.py:17
  33.1 46.5 %collective-permute-start.32 = (bf16[8,128,256]{2,1,0:T(8,128)(2,1)}, bf16[8,128,256]{2,1,0:T(8,128)(2,1)}, u32[]{:S(2)}, u32[]{:S(2)}) collective-permute-start(bf16[8,128,256]{2,1,0:T(8,128)(2,1)} %convolution_convert_fusion.5), channel_id=1, source_target_pairs={{0,16},{2,18},{4,20},{6,22},{8,24},{10,26},{12,28},{14,30},{1,17},... | collective-permute-start | bytes 1572872 | tf_op jit(solution)/shard_map/ppermute | solution.py:17
  79.6 56.1 %collective-permute-start.37 = (bf16[8,128,256]{2,1,0:T(8,128)(2,1)}, bf16[8,128,256]{2,1,0:T(8,128)(2,1)S(1)}, u32[]{:S(2)}, u32[]{:S(2)}) collective-permute-start(bf16[8,128,256]{2,1,0:T(8,128)(2,1)} %convolution_convert_fusion.5), channel_id=1, source_target_pairs={{0,6},{2,8},{4,10},{6,12},{8,14},{10,16},{12,18},{14,20},{16,22},{... | collective-permute-start | bytes 1572872 | tf_op jit(solution)/shard_map/ppermute | solution.py:17
  82.7 54.3 %collective-permute-start.38 = (bf16[8,128,256]{2,1,0:T(8,128)(2,1)}, bf16[8,128,256]{2,1,0:T(8,128)(2,1)S(1)}, u32[]{:S(2)}, u32[]{:S(2)}) collective-permute-start(bf16[8,128,256]{2,1,0:T(8,128)(2,1)} %convolution_convert_fusion.5), channel_id=1, source_target_pairs={{0,4},{2,6},{4,8},{6,10},{8,12},{10,14},{12,16},{14,18},{16,20},{1... | collective-permute-start | bytes 1572872 | tf_op jit(solution)/shard_map/ppermute | solution.py:17
  130.9 102.6 %collective-permute-start.44 = (bf16[8,128,256]{2,1,0:T(8,128)(2,1)}, bf16[8,128,256]{2,1,0:T(8,128)(2,1)S(1)}, u32[]{:S(2)}, u32[]{:S(2)}) collective-permute-start(bf16[8,128,256]{2,1,0:T(8,128)(2,1)} %convolution_convert_fusion.5), channel_id=1, source_target_pairs={{10,0},{12,2},{14,4},{16,6},{18,8},{20,10},{22,12},{24,14},{26,16}... | collective-permute-start | bytes 1572872 | tf_op jit(solution)/shard_map/ppermute | solution.py:17
  138.4 48.2 %collective-permute-start.43 = (bf16[8,128,256]{2,1,0:T(8,128)(2,1)}, bf16[8,128,256]{2,1,0:T(8,128)(2,1)S(1)}, u32[]{:S(2)}, u32[]{:S(2)}) collective-permute-start(bf16[8,128,256]{2,1,0:T(8,128)(2,1)} %convolution_convert_fusion.5), channel_id=1, source_target_pairs={{8,0},{10,2},{12,4},{14,6},{16,8},{18,10},{20,12},{22,14},{24,16},... | collective-permute-start | bytes 1572872 | tf_op jit(solution)/shard_map/ppermute | solution.py:17
  140.8 94.1 %collective-permute-start.45 = (bf16[8,128,256]{2,1,0:T(8,128)(2,1)}, bf16[8,128,256]{2,1,0:T(8,128)(2,1)S(1)}, u32[]{:S(2)}, u32[]{:S(2)}) collective-permute-start(bf16[8,128,256]{2,1,0:T(8,128)(2,1)} %convolution_convert_fusion.5), channel_id=1, source_target_pairs={{12,0},{14,2},{16,4},{18,6},{20,8},{22,10},{24,12},{26,14},{28,16}... | collective-permute-start | bytes 1572872 | tf_op jit(solution)/shard_map/ppermute | solution.py:17
  164.8 71.5 %collective-permute-start.46 = (bf16[8,128,256]{2,1,0:T(8,128)(2,1)}, bf16[8,128,256]{2,1,0:T(8,128)(2,1)S(1)}, u32[]{:S(2)}, u32[]{:S(2)}) collective-permute-start(bf16[8,128,256]{2,1,0:T(8,128)(2,1)} %convolution_convert_fusion.5), channel_id=1, source_target_pairs={{14,0},{16,2},{18,4},{20,6},{22,8},{24,10},{26,12},{28,14},{30,16}... | collective-permute-start | bytes 1572872 | tf_op jit(solution)/shard_map/ppermute | solution.py:17
  166.2 93.7 %collective-permute-start.47 = (bf16[8,128,256]{2,1,0:T(8,128)(2,1)}, bf16[8,128,256]{2,1,0:T(8,128)(2,1)S(1)}, u32[]{:S(2)}, u32[]{:S(2)}) collective-permute-start(bf16[8,128,256]{2,1,0:T(8,128)(2,1)} %convolution_convert_fusion.5), channel_id=1, source_target_pairs={{16,0},{18,2},{20,4},{22,6},{24,8},{26,10},{28,12},{30,14},{17,1},... | collective-permute-start | bytes 1572872 | tf_op jit(solution)/shard_map/ppermute | solution.py:17
  186.5 77.0 %collective-permute-start = (bf16[8,128,256]{2,1,0:T(8,128)(2,1)S(1)}, bf16[8,128,256]{2,1,0:T(8,128)(2,1)S(1)}, u32[]{:S(2)}, u32[]{:S(2)}) collective-permute-start(bf16[8,128,256]{2,1,0:T(8,128)(2,1)S(1)} %fusion.119), channel_id=1, source_target_pairs={{0,16},{2,18},{4,20},{6,22},{8,24},{10,26},{12,28},{14,30},{1,17},... | collective-permute-start | bytes 1572872 | tf_op jit(solution)/shard_map/ppermute | solution.py:17
  236.3 42.5 %collective-permute-start.3 = (bf16[8,128,256]{2,1,0:T(8,128)(2,1)S(1)}, bf16[8,128,256]{2,1,0:T(8,128)(2,1)S(1)}, u32[]{:S(2)}, u32[]{:S(2)}) collective-permute-start(bf16[8,128,256]{2,1,0:T(8,128)(2,1)S(1)} %fusion.119), channel_id=1, source_target_pairs={{0,10},{2,12},{4,14},{6,16},{8,18},{10,20},{12,22},{14,24},{16,26}... | collective-permute-start | bytes 1572872 | tf_op jit(solution)/shard_map/ppermute | solution.py:17
  264.9 43.1 %collective-permute-start.6 = (bf16[8,128,256]{2,1,0:T(8,128)(2,1)S(1)}, bf16[8,128,256]{2,1,0:T(8,128)(2,1)S(1)}, u32[]{:S(2)}, u32[]{:S(2)}) collective-permute-start(bf16[8,128,256]{2,1,0:T(8,128)(2,1)S(1)} %fusion.119), channel_id=1, source_target_pairs={{0,4},{2,6},{4,8},{6,10},{8,12},{10,14},{12,16},{14,18},{16,20},{1... | collective-permute-start | bytes 1572872 | tf_op jit(solution)/shard_map/ppermute | solution.py:17
  267.5 41.8 %collective-permute-start.7 = (bf16[8,128,256]{2,1,0:T(8,128)(2,1)S(1)}, bf16[8,128,256]{2,1,0:T(8,128)(2,1)S(1)}, u32[]{:S(2)}, u32[]{:S(2)}) collective-permute-start(bf16[8,128,256]{2,1,0:T(8,128)(2,1)S(1)} %fusion.119), channel_id=1, source_target_pairs={{0,2},{2,4},{4,6},{6,8},{8,10},{10,12},{12,14},{14,16},{16,18},{18... | collective-permute-start | bytes 1572872 | tf_op jit(solution)/shard_map/ppermute | solution.py:17
  312.1 43.3 %collective-permute-start.14 = (bf16[8,128,256]{2,1,0:T(8,128)(2,1)S(1)}, bf16[8,128,256]{2,1,0:T(8,128)(2,1)S(1)}, u32[]{:S(2)}, u32[]{:S(2)}) collective-permute-start(bf16[8,128,256]{2,1,0:T(8,128)(2,1)S(1)} %fusion.119), channel_id=1, source_target_pairs={{14,0},{16,2},{18,4},{20,6},{22,8},{24,10},{26,12},{28,14},{30,16}... | collective-permute-start | bytes 1572872 | tf_op jit(solution)/shard_map/ppermute | solution.py:17
  313.4 99.4 %collective-permute-start.15 = (bf16[8,128,256]{2,1,0:T(8,128)(2,1)S(1)}, bf16[8,128,256]{2,1,0:T(8,128)(2,1)S(1)}, u32[]{:S(2)}, u32[]{:S(2)}) collective-permute-start(bf16[8,128,256]{2,1,0:T(8,128)(2,1)S(1)} %fusion.119), channel_id=1, source_target_pairs={{16,0},{18,2},{20,4},{22,6},{24,8},{26,10},{28,12},{30,14},{17,1},... | collective-permute-start | bytes 1572872 | tf_op jit(solution)/shard_map/ppermute | solution.py:17
  449.4 44.7 %collective-permute-start.29 = (f32[128,4,8]{2,1,0:T(4,128)S(1)}, f32[128,4,8]{2,1,0:T(4,128)S(1)}, u32[]{:S(2)}, u32[]{:S(2)}) collective-permute-start(f32[128,4,8]{2,1,0:T(4,128)S(1)} %bitcast.311), channel_id=1, source_target_pairs={{12,0},{14,2},{16,4},{18,6},{20,8},{22,10},{24,12},{26,14},{28,16}... | collective-permute-start | bytes 49160 | tf_op jit(solution)/shard_map/ppermute | solution.py:17
  450.7 44.7 %collective-permute-start.28 = (f32[128,4,8]{2,1,0:T(4,128)S(1)}, f32[128,4,8]{2,1,0:T(4,128)S(1)}, u32[]{:S(2)}, u32[]{:S(2)}) collective-permute-start(f32[128,4,8]{2,1,0:T(4,128)S(1)} %bitcast.312), channel_id=1, source_target_pairs={{10,0},{12,2},{14,4},{16,6},{18,8},{20,10},{22,12},{24,14},{26,16}... | collective-permute-start | bytes 49160 | tf_op jit(solution)/shard_map/ppermute | solution.py:17
  452.0 46.5 %collective-permute-start.27 = (f32[128,4,8]{2,1,0:T(4,128)S(1)}, f32[128,4,8]{2,1,0:T(4,128)S(1)}, u32[]{:S(2)}, u32[]{:S(2)}) collective-permute-start(f32[128,4,8]{2,1,0:T(4,128)S(1)} %bitcast.313), channel_id=1, source_target_pairs={{8,0},{10,2},{12,4},{14,6},{16,8},{18,10},{20,12},{22,14},{24,16},... | collective-permute-start | bytes 49160 | tf_op jit(solution)/shard_map/ppermute | solution.py:17
  559.2 40.5 %collective-permute-start.57 = (f32[128,4,8]{2,1,0:T(4,128)}, f32[128,4,8]{2,1,0:T(4,128)}, u32[]{:S(2)}, u32[]{:S(2)}) collective-permute-start(f32[128,4,8]{2,1,0:T(4,128)} %get-tuple-element.25), channel_id=1, source_target_pairs={{4,0},{6,2},{8,4},{10,6},{12,8},{14,10},{16,12},{18,14},{20,16},{2... | collective-permute-start | bytes 49160 | tf_op jit(solution)/shard_map/ppermute | solution.py:17
  568.6 40.2 %collective-permute-start.55 = (f32[128,4,8]{2,1,0:T(4,128)}, f32[128,4,8]{2,1,0:T(4,128)}, u32[]{:S(2)}, u32[]{:S(2)}) collective-permute-start(f32[128,4,8]{2,1,0:T(4,128)} %get-tuple-element.25), channel_id=1, source_target_pairs={{0,2},{2,4},{4,6},{6,8},{8,10},{10,12},{12,14},{14,16},{16,18},{18... | collective-permute-start | bytes 49160 | tf_op jit(solution)/shard_map/ppermute | solution.py:17
  736.0 186.5 %all-reduce.2.cloned.1.call-start = ((), (), s32[]{:S(2)}) async-start(), calls=%async_computation.8 | async-start | bytes 4194304 | tf_op jit(solution)/shard_map/psum | solution.py:298
  (86 other events, 2324.4 us)
Sparse Core Ops, SparseCore 0:
  766.3 156.2 all-reduce.1
where the time goes:
time: 946 us; the launch traced here: 933 us
  waiting for transfers between devices  335 us (35%)
  starting transfers between devices  265 us (28%)
  matrix products  160 us (17%)
  local copies, waits for them, and re-layouts  69.3 us (7%)
  blocking collectives  61.1 us (6%)
  other arithmetic  26.9 us (3%)
  between operations  16.1 us (2%)
    ppermute x64, starting transfers between devices, passed_along(): return lax.ppermute(block, axis, route)  232 us
    ppermute x64, waiting for transfers between devices, passed_along(): return lax.ppermute(block, axis, route)  218 us
    psum x1, waiting for transfers between devices, per_device(): lax.psum((jnp.concatenate([freq_stack, time_stack], axis=0), jnp.stack([g...  93 us
    psum x1, blocking collectives, per_device(): lax.psum((jnp.concatenate([freq_stack, time_stack], axis=0), jnp.stack([g...  61.1 us
    unnamed x2, matrix products  31.7 us
    dot_general x10, matrix products, project(): product = jnp.dot(flat_rows, matrix, preferred_element_type=jnp.float32)  22.5 us
    dot_general x2, matrix products, query_backward(): jnp.einsum('bhqk,' + key_form + '->h' + query_form, grad_scores, key_rows...  21.1 us
  transfers between devices with their start and end apart: 73, of which 24 were waited for; matrix products, arithmetic and copies ran while one was open for 16% of the time, Pallas kernels for 0%

commit v1 on v0

v1 whole, which is shorter than its diff:
```python
import functools

import jax
import jax.numpy as jnp
from jax import lax
from jax.experimental import pallas as pl
from jax.experimental.pallas import tpu as pltpu
from jax.sharding import PartitionSpec as P

HEADS = 4
WINDOW = 128

epsilon = 1e-06
masked_score = -1e30

f32 = jnp.float32
bf16 = jnp.bfloat16
LANES = 128
VMEM_LIMIT = 48 * 1024 * 1024

CONTRACT_LAST = (((1,), (1,)), ((), ()))
CONTRACT_FIRST = (((0,), (0,)), ((), ()))


def dot(left, right):
    return jnp.dot(left, right, preferred_element_type=f32)


def dot_nt(left, right):
    return lax.dot_general(left, right, CONTRACT_LAST, preferred_element_type=f32)


def dot_tn(left, right):
    return lax.dot_general(left, right, CONTRACT_FIRST, preferred_element_type=f32)


def put(ref, rows, value):
    for c in range(ref.shape[0]):
        ref[c, rows, :] = value[:, c * LANES : (c + 1) * LANES]


def get(ref, rows):
    return jnp.concatenate([ref[c, rows, :] for c in range(ref.shape[0])], axis=1)


def norm_parts(widened):
    inverse = lax.rsqrt(jnp.mean(widened * widened, axis=-1, keepdims=True) + epsilon)
    return inverse, widened * inverse


def norm_backward(incoming, inverse, unit_rows, gain):
    scaled = incoming * gain
    return inverse * (scaled - unit_rows * jnp.mean(scaled * unit_rows, axis=-1, keepdims=True))


def spread(rows, factor):
    width = rows.shape[-1]
    owner = lax.broadcasted_iota(jnp.int32, (1, width), 1) // (width // HEADS)
    return jnp.concatenate(
        [rows * jnp.where(owner == h, factor, 0.0).astype(rows.dtype) for h in range(HEADS)], axis=0
    )


def softmax_heads(scores, keys, allowed):
    parts = []
    for h in range(HEADS):
        s = scores[:, h * keys : (h + 1) * keys]
        if allowed is not None:
            s = jnp.where(allowed, s, masked_score)
        e = jnp.exp(s - jnp.max(s, axis=-1, keepdims=True))
        parts.append(e * (1.0 / jnp.sum(e, axis=-1, keepdims=True)))
    return parts


def attention_backward(probs, grad_out, q, v, k_spread, scale):
    keys = v.shape[0]
    grad_probs = dot_nt(grad_out, spread(v, 1.0))
    grad_scores = []
    for h in range(HEADS):
        gp = grad_probs[:, h * keys : (h + 1) * keys]
        row_dot = jnp.sum(gp * probs[h], axis=-1, keepdims=True)
        grad_scores.append((probs[h] * (gp - row_dot)).astype(bf16))
    g_q = dot(jnp.concatenate(grad_scores, axis=1), k_spread)
    g_k = dot_tn(jnp.concatenate(grad_scores, axis=0), spread(q, scale))
    g_v = dot_tn(
        jnp.concatenate([p.astype(bf16) for p in probs], axis=0), spread(grad_out, 1.0)
    )
    return g_q, g_k, g_v


def freq_forward_kernel(x_ref, w_ref, gain_ref, q_ref, k_ref, v_ref, o_ref, p_ref, h_ref, hold):
    step = pl.program_id(0)
    freq, _, bins_dev, width = x_ref.shape
    bins = freq * bins_dev
    bins_time = hold.shape[2] // pl.num_programs(0)
    scale = (width // HEADS) ** (-0.5)
    x = x_ref[...].reshape(bins, width).astype(f32)
    _, unit = norm_parts(x)
    n = (unit * gain_ref[0:1, :]).astype(bf16)
    q = dot(n, w_ref[0]).astype(bf16)
    k = dot(n, w_ref[1]).astype(bf16)
    v = dot(n, w_ref[2]).astype(bf16)
    probs = softmax_heads(dot_nt(q, spread(k, scale)), bins, None)
    for h in range(HEADS):
        p_ref[0, h] = probs[h]
    o = dot(jnp.concatenate([p.astype(bf16) for p in probs], axis=1), spread(v, 1.0)).astype(bf16)
    hidden = x + dot(o, w_ref[3])
    q_ref[0] = q
    k_ref[0] = k
    v_ref[0] = v
    o_ref[0] = o
    rows = pl.ds(pl.multiple_of(step * bins_time, bins_time), bins_time)
    for f in range(freq):
        part = hidden[f * bins_dev : (f + 1) * bins_dev].reshape(-1, bins_time, width)
        hold[:, f, rows, :] = part

    @pl.when(step == pl.num_programs(0) - 1)
    def _():
        h_ref[...] = hold[...].astype(bf16)


def freq_forward(x, weights, gains, group):
    freq, frames, bins_dev, width = x.shape
    bins = freq * bins_dev
    rows = frames * (bins_dev // group)
    rowspec = pl.BlockSpec((1, bins, width), lambda i: (i, 0, 0))
    rowshape = jax.ShapeDtypeStruct((frames, bins, width), bf16)
    whole = (group, freq, rows, width)
    flops = frames * 2 * bins * (4 * width * width + 2 * HEADS * bins * width)
    return pl.pallas_call(
        freq_forward_kernel,
        grid=(frames,),
        in_specs=[
            pl.BlockSpec((freq, 1, bins_dev, width), lambda i: (0, i, 0, 0)),
            pl.BlockSpec(weights.shape, lambda i: (0, 0, 0)),
            pl.BlockSpec(gains.shape, lambda i: (0, 0)),
        ],
        out_specs=[rowspec] * 4
        + [
            pl.BlockSpec((1, HEADS, bins, bins), lambda i: (i, 0, 0, 0)),
            pl.BlockSpec(whole, lambda i: (0, 0, 0, 0)),
        ],
        out_shape=[rowshape] * 4
        + [
            jax.ShapeDtypeStruct((frames, HEADS, bins, bins), f32),
            jax.ShapeDtypeStruct(whole, bf16),
        ],
        scratch_shapes=[pltpu.VMEM(whole, f32)],
        compiler_params=pltpu.CompilerParams(vmem_limit_bytes=VMEM_LIMIT),
        cost_estimate=pl.CostEstimate(
            flops=flops, bytes_accessed=8 * 1024 * 1024, transcendentals=frames * HEADS * bins * bins
        ),
        name="freq_forward",
    )(x, weights, gains)


def freq_backward_kernel(
    x_ref, q_ref, k_ref, v_ref, o_ref, p_ref, gh_ref, w_ref, gain_ref, gx_ref, dw_ref, dg_ref, hold
):
    step = pl.program_id(0)
    freq, _, bins_dev, width = x_ref.shape
    bins = freq * bins_dev
    group = hold.shape[0]
    bins_time = bins_dev // group
    scale = (width // HEADS) ** (-0.5)

    @pl.when(step == 0)
    def _():
        hold[...] = gh_ref[...].astype(f32)
        dw_ref[...] = jnp.zeros_like(dw_ref)
        dg_ref[...] = jnp.zeros_like(dg_ref)

    rows = pl.ds(pl.multiple_of(step * bins_time, bins_time), bins_time)
    grad_hidden = jnp.concatenate(
        [hold[:, f, rows, :].reshape(bins_dev, width) for f in range(freq)], axis=0
    )
    grad_hidden_low = grad_hidden.astype(bf16)
    grad_out = dot_nt(grad_hidden_low, w_ref[3]).astype(bf16)
    q, k, v = q_ref[0], k_ref[0], v_ref[0]
    probs = [p_ref[0, h] for h in range(HEADS)]
    g_q, g_k, g_v = attention_backward(probs, grad_out, q, v, spread(k, scale), scale)
    g_q, g_k, g_v = g_q.astype(bf16), g_k.astype(bf16), g_v.astype(bf16)
    g_n = dot_nt(g_q, w_ref[0]) + dot_nt(g_k, w_ref[1]) + dot_nt(g_v, w_ref[2])
    x = x_ref[...].reshape(bins, width).astype(f32)
    inverse, unit = norm_parts(x)
    gain = gain_ref[0:1, :]
    n = (unit * gain).astype(bf16)
    grad_x = grad_hidden + norm_backward(g_n, inverse, unit, gain)
    gx_ref[...] = grad_x.astype(bf16).reshape(gx_ref.shape)
    dw_ref[0] += dot_tn(n, g_q)
    dw_ref[1] += dot_tn(n, g_k)
    dw_ref[2] += dot_tn(n, g_v)
    dw_ref[3] += dot_tn(o_ref[0], grad_hidden_low)
    dg_ref[...] += jnp.sum(g_n * unit, axis=0, keepdims=True)


def freq_backward(x, q, k, v, o, probs, grad_hidden, weights, gains):
    freq, frames, bins_dev, width = x.shape
    bins = freq * bins_dev
    rowspec = pl.BlockSpec((1, bins, width), lambda i: (i, 0, 0))
    xspec = pl.BlockSpec((freq, 1, bins_dev, width), lambda i: (0, i, 0, 0))
    flops = frames * 2 * bins * (8 * width * width + 4 * HEADS * bins * width)
    return pl.pallas_call(
        freq_backward_kernel,
        grid=(frames,),
        in_specs=[
            xspec,
            rowspec,
            rowspec,
            rowspec,
            rowspec,
            pl.BlockSpec((1, HEADS, bins, bins), lambda i: (i, 0, 0, 0)),
            pl.BlockSpec(grad_hidden.shape, lambda i: (0, 0, 0, 0)),
            pl.BlockSpec(weights.shape, lambda i: (0, 0, 0)),
            pl.BlockSpec(gains.shape, lambda i: (0, 0)),
        ],
        out_specs=[
            xspec,
            pl.BlockSpec((4, width, width), lambda i: (0, 0, 0)),
            pl.BlockSpec((1, width), lambda i: (0, 0)),
        ],
        out_shape=[
            jax.ShapeDtypeStruct(x.shape, bf16),
            jax.ShapeDtypeStruct((4, width, width), f32),
            jax.ShapeDtypeStruct((1, width), f32),
        ],
        scratch_shapes=[pltpu.VMEM(grad_hidden.shape, f32)],
        compiler_params=pltpu.CompilerParams(vmem_limit_bytes=VMEM_LIMIT),
        cost_estimate=pl.CostEstimate(
            flops=flops, bytes_accessed=8 * 1024 * 1024, transcendentals=0
        ),
        name="freq_backward",
    )(x, q, k, v, o, probs, grad_hidden, weights, gains)


def time_kernel(
    bins, own_start, total_frames, first_ref, h_ref, up_ref, w_ref, gain_ref, gh_ref, dw_ref,
    dg_ref, q_s, k_s, v_s, go_s, o_s, gq_s, gk_s, gv_s
):
    span_rows, width = h_ref.shape
    span = span_rows // bins
    own_rows = gh_ref.shape[0]
    own = own_rows // bins
    scale = (width // HEADS) ** (-0.5)
    gain = gain_ref[1:2, :]
    chunk = own_rows
    while chunk > 256 and chunk % 32 == 0:
        chunk //= 2

    def project(i, carry):
        rows = pl.ds(pl.multiple_of(i * chunk, chunk), chunk)
        _, unit = norm_parts(h_ref[rows, :].astype(f32))
        n = (unit * gain).astype(bf16)
        put(q_s, rows, dot(n, w_ref[4]))
        put(k_s, rows, dot(n, w_ref[5]))
        put(v_s, rows, dot(n, w_ref[6]))
        put(go_s, rows, dot_nt(up_ref[rows, :], w_ref[7]))
        return carry

    lax.fori_loop(0, span_rows // chunk, project, 0)

    query = lax.broadcasted_iota(jnp.int32, (span, span), 0)
    key = lax.broadcasted_iota(jnp.int32, (span, span), 1)
    distance = key - query
    allowed = (distance >= -(WINDOW // 2)) & (distance < WINDOW // 2)
    if own != span:
        frame = first_ref[0] + key
        allowed = allowed & (frame >= 0) & (frame < total_frames)

    def attend(b, carry):
        rows = pl.ds(b, span, stride=bins)
        q = get(q_s, rows).astype(bf16)
        k = get(k_s, rows).astype(bf16)
        v = get(v_s, rows).astype(bf16)
        grad_out = get(go_s, rows).astype(bf16)
        k_spread = spread(k, scale)
        probs = softmax_heads(dot_nt(q, k_spread), span, allowed)
        o = dot(jnp.concatenate([p.astype(bf16) for p in probs], axis=1), spread(v, 1.0))
        g_q, g_k, g_v = attention_backward(probs, grad_out, q, v, k_spread, scale)
        put(o_s, rows, o)
        put(gq_s, rows, g_q)
        put(gk_s, rows, g_k)
        put(gv_s, rows, g_v)
        return carry

    lax.fori_loop(0, bins, attend, 0)

    dw_ref[...] = jnp.zeros_like(dw_ref)
    dg_ref[...] = jnp.zeros_like(dg_ref)

    def finish(i, carry):
        mine = pl.ds(pl.multiple_of(i * chunk, chunk), chunk)
        rows = pl.ds(pl.multiple_of(own_start + i * chunk, chunk), chunk)
        g_q = get(gq_s, rows).astype(bf16)
        g_k = get(gk_s, rows).astype(bf16)
        g_v = get(gv_s, rows).astype(bf16)
        g_n = dot_nt(g_q, w_ref[4]) + dot_nt(g_k, w_ref[5]) + dot_nt(g_v, w_ref[6])
        inverse, unit = norm_parts(h_ref[rows, :].astype(f32))
        n = (unit * gain).astype(bf16)
        up = up_ref[rows, :]
        grad_hidden = up.astype(f32) + norm_backward(g_n, inverse, unit, gain)
        gh_ref[mine, :] = grad_hidden.astype(bf16)
        dw_ref[0] += dot_tn(n, g_q)
        dw_ref[1] += dot_tn(n, g_k)
        dw_ref[2] += dot_tn(n, g_v)
        dw_ref[3] += dot_tn(get(o_s, rows).astype(bf16), up)
        dg_ref[...] += jnp.sum(g_n * unit, axis=0, keepdims=True)
        return carry

    lax.fori_loop(0, own_rows // chunk, finish, 0)


def time_attention(first, hidden, upstream, weights, gains, bins, own_start, own_rows, total):
    span_rows, width = hidden.shape
    vmem = pl.BlockSpec(memory_space=pltpu.VMEM)
    span = span_rows // bins
    flops = 2 * span_rows * (11 * width * width + 6 * HEADS * span * width)
    return pl.pallas_call(
        functools.partial(time_kernel, bins, own_start, total),
        in_specs=[pl.BlockSpec(memory_space=pltpu.SMEM)] + [vmem] * 4,
        out_specs=[vmem] * 3,
        out_shape=[
            jax.ShapeDtypeStruct((own_rows, width), bf16),
            jax.ShapeDtypeStruct((4, width, width), f32),
            jax.ShapeDtypeStruct((1, width), f32),
        ],
        scratch_shapes=[pltpu.VMEM((width // LANES, span_rows, LANES), f32)] * 8,
        compiler_params=pltpu.CompilerParams(vmem_limit_bytes=VMEM_LIMIT),
        cost_estimate=pl.CostEstimate(
            flops=flops,
            bytes_accessed=4 * 1024 * 1024,
            transcendentals=bins * HEADS * span * span,
        ),
        name="time_attention",
    )(first, hidden, upstream, weights, gains)


def group_size(devices, bins_dev):
    best = 1
    for size in range(1, devices + 1):
        if devices % size == 0 and bins_dev % (8 * size) == 0:
            best = size
    return best


def per_device(features, upstream, weights, gains):
    frames_dev, bins_dev, width = features.shape
    tm, freq = lax.axis_size("tm"), lax.axis_size("freq")
    total_frames = frames_dev * tm
    frames = frames_dev // freq
    group = group_size(tm, bins_dev)
    bins_time = bins_dev // group
    group_frames = group * frames_dev
    whole = group == tm
    sides = 0 if whole else -(-WINDOW // group_frames)
    groups = (
        None
        if whole
        else [list(range(g * group, (g + 1) * group)) for g in range(tm // group)]
    )

    def over_tm(blocks):
        return lax.all_to_all(blocks, "tm", 0, 0, tiled=True, axis_index_groups=groups)

    def over_all(blocks):
        if whole:
            flat = blocks.reshape((tm * freq,) + blocks.shape[2:])
            return lax.all_to_all(flat, ("tm", "freq"), 0, 0, tiled=True).reshape(blocks.shape)
        return over_tm(lax.all_to_all(blocks, "freq", 1, 1, tiled=True))

    def with_sides(rows):
        parts = [rows]
        for away in range(1, sides + 1):
            shift = away * group
            before = lax.ppermute(rows, "tm", [(i, i + shift) for i in range(tm - shift)])
            after = lax.ppermute(rows, "tm", [(i + shift, i) for i in range(tm - shift)])
            parts = [before] + parts + [after]
        return jnp.concatenate(parts, axis=0) if sides else rows

    x = lax.all_to_all(
        features.reshape(freq, frames, bins_dev, width), "freq", 0, 0, tiled=True
    )
    up_blocks = jnp.swapaxes(upstream.reshape(frames_dev, group, bins_time, width), 0, 1)
    up_rows = over_tm(up_blocks).reshape(-1, width)
    q, k, v, o, probs, hidden_blocks = freq_forward(x, weights, gains, group)
    hidden_rows = over_all(hidden_blocks).reshape(-1, width)
    own_rows = hidden_rows.shape[0]
    position = lax.axis_index("tm") // group
    first = ((position - sides) * group_frames).astype(jnp.int32).reshape(1)
    grad_rows, time_dw, time_dg = time_attention(
        first,
        with_sides(hidden_rows),
        with_sides(up_rows),
        weights,
        gains,
        bins_time,
        sides * own_rows,
        own_rows,
        total_frames,
    )
    grad_hidden = over_all(grad_rows.reshape(hidden_blocks.shape))
    grad_x, freq_dw, freq_dg = freq_backward(
        x, q, k, v, o, probs, grad_hidden, weights, gains
    )
    grad_input = lax.all_to_all(grad_x, "freq", 0, 0, tiled=True).reshape(features.shape)

    inv_root = (total_frames * bins_dev * freq) ** (-0.5)
    devices = tm * freq
    partial = jnp.concatenate([freq_dw, time_dw], axis=0)
    pieces = (partial * inv_root).astype(bf16).reshape(devices, -1, width)
    gain_rows = jnp.concatenate([freq_dg, time_dg], axis=0) * inv_root
    high = gain_rows.astype(bf16)
    low = (gain_rows - high.astype(f32)).astype(bf16)
    extra = jnp.broadcast_to(jnp.concatenate([high, low], axis=0)[None], (devices, 4, width))
    sent = jnp.concatenate([pieces, extra], axis=1)
    arrived = lax.all_to_all(sent, ("tm", "freq"), 0, 0, tiled=True)
    summed = jnp.sum(arrived.astype(f32), axis=0)
    count = pieces.shape[1]
    gain_grads = summed[count : count + 2] + summed[count + 2 :]
    own = summed[:count].astype(bf16)
    gathered = lax.all_to_all(
        jnp.broadcast_to(own[None], (devices,) + own.shape), ("tm", "freq"), 0, 0, tiled=True
    )
    weight_grads = gathered.astype(f32).reshape(partial.shape)
    return (grad_input, weight_grads, gain_grads)


def solution(mesh):
    return jax.shard_map(
        per_device,
        mesh=mesh,
        in_specs=(P("tm", "freq", None), P("tm", "freq", None), P(), P()),
        out_specs=(P("tm", "freq", None), P(), P()),
        check_vma=False,
    )
```

time: 946 us -> 170 us (0.18); the launches traced: 933 us -> 169 us
  waiting for transfers between devices: 335 us -> 62 us
  starting transfers between devices: 265 us -> 19.7 us
  matrix products: 160 us -> 0 us
  local copies, waits for them, and re-layouts: 69.3 us -> 5.98 us
  Pallas kernels: 0 us -> 26.1 us
  other arithmetic: 26.9 us -> 2.61 us
  between operations: 16.1 us -> 0.79 us
    ppermute x64 -> x0, starting transfers between devices: 232 us -> none  [passed_along(): return lax.ppermute(block, axis, route)]
    ppermute x64 -> x0, waiting for transfers between devices: 218 us -> none  [passed_along(): return lax.ppermute(block, axis, route)]
    dot_general x37 -> x0, matrix products: 128 us -> none  [the longest x10 22.5 us: project(): product = jnp.dot(flat_rows, matrix, preferred_element_type=jnp.float32)]
    psum x1 -> x0, waiting for transfers between devices: 93 us -> none  [per_device(): lax.psum((jnp.concatenate([freq_stack, time_stack], axis=0), jnp.stack([g...]
    psum x1 -> x0, blocking collectives: 61.1 us -> none  [per_device(): lax.psum((jnp.concatenate([freq_stack, time_stack], axis=0), jnp.stack([g...]
    all_to_all x0 -> x2, blocking collectives: none -> 51.9 us  [the longest x1 33.4 us: per_device(): arrived = lax.all_to_all(sent, ('tm', 'freq'), 0, 0, tiled=True)]
    all_to_all x8 -> x5, waiting for transfers between devices: 24.1 us -> 62 us  [the longest x1 25.6 us: per_device(): lax.all_to_all(jnp.broadcast_to(own[None], (devices,) + own.shape), ('tm'...]
    unnamed x2 -> x0, matrix products: 31.7 us -> none
  transfers between devices with their start and end apart: 73 -> 5, of which waited for: 24 -> 5; matrix products, arithmetic and copies ran while one was open for 16% -> 1% of each run, Pallas kernels for 0% -> 4%
where the time goes in v1:
time: 170 us; the launch traced here: 169 us
  waiting for transfers between devices  62 us (36%)
  blocking collectives  51.9 us (31%)
  Pallas kernels  26.1 us (15%)
  starting transfers between devices  19.7 us (12%)
  local copies, waits for them, and re-layouts  5.98 us (4%)
  other arithmetic  2.61 us (2%)
    all_to_all x1, blocking collectives, per_device(): arrived = lax.all_to_all(sent, ('tm', 'freq'), 0, 0, tiled=True)  33.4 us
    all_to_all x1, waiting for transfers between devices, per_device(): lax.all_to_all(jnp.broadcast_to(own[None], (devices,) + own.shape), ('tm'...  25.6 us
    all_to_all x1, blocking collectives, over_all(): lax.all_to_all(flat, ('tm', 'freq'), 0, 0, tiled=True).reshape(blocks.shape)  18.4 us
    all_to_all x1, waiting for transfers between devices, over_all(): lax.all_to_all(flat, ('tm', 'freq'), 0, 0, tiled=True).reshape(blocks.shape)  15 us
    pallas_call x1, Pallas kernels, time_attention(): pl.pallas_call(functools.partial(time_kernel, bins, own_start, total), in...  11.7 us
    all_to_all x1, waiting for transfers between devices, per_device(): lax.all_to_all(grad_x, 'freq', 0, 0, tiled=True).reshape(features.shape)  8.75 us
    all_to_all x1, waiting for transfers between devices, per_device(): lax.all_to_all(features.reshape(freq, frames, bins_dev, width), 'freq', 0...  7.86 us
    pallas_call x1, Pallas kernels, freq_backward(): pl.pallas_call(freq_backward_kernel, grid=(frames,), in_specs=[xspec, row...  7.85 us
  transfers between devices with their start and end apart: 5, of which 5 were waited for; matrix products, arithmetic and copies ran while one was open for 1% of the time, Pallas kernels for 4%

profile of v1, /device:TPU:0, one launch (start us, length us, event | category | flops | bytes accessed | tf_op | source)
XLA Modules:
  0.0 169.1 jit_solution(10975078377509252442)
XLA Ops:
  0.7 4.4 %all-to-all-start = ((bf16[2,4,128,256]{3,2,1,0:T(8,128)(2,1)}), bf16[2,4,128,256]{3,2,1,0:T(8,128)(2,1)S(1)}, u32[]{:S(2)}, u32[]{:S(2)}) async-start(bf16[2,4,128,256]{3,2,1,0:T(8,128)(2,1)} %bitcast.25), calls=%async_computation | async-start | bytes 1048576 | tf_op jit(solution)/shard_map/all_to_all | solution.py:380
  5.0 0.9 copy_bitcast_fusion
  5.9 7.9 %all-to-all-done.x_ref = bf16[2,4,128,256]{3,2,1,0:T(8,128)(2,1)S(1)} async-done(((bf16[2,4,128,256]{3,2,1,0:T(8,128)(2,1)}), bf16[2,4,128,256]{3,2,1,0:T(8,128)(2,1)S(1)}, u32[]{:S(2)}, u32[]{:S(2)}) %all-to-all-start) | async-done | bytes 524320 | tf_op jit(solution)/shard_map/all_to_all | solution.py:380
  13.8 6.1 %all-to-all-start.2 = ((bf16[16,8,8,256]{3,2,1,0:T(8,128)(2,1)}), bf16[16,8,8,256]{3,2,1,0:T(8,128)(2,1)S(1)}, u32[]{:S(2)}, u32[]{:S(2)}) async-start(bf16[16,8,8,256]{3,2,1,0:T(8,128)(2,1)} %copy_bitcast_fusion), calls=%async_computation.2 | async-start | bytes 1048576 | tf_op jit(solution)/shard_map/all_to_all | solution.py:363
  19.9 6.5 %freq_forward.1 = (bf16[4,256,256]{2,1,0:T(8,128)(2,1)S(1)}, bf16[4,256,256]{2,1,0:T(8,128)(2,1)S(1)}, bf16[4,256,256]{2,1,0:T(8,128)(2,1)S(1)}, bf16[4,256,256]...) custom-call(bf16[2,4,128,256]{3,2,1,0:T(8,128)(2,1)S(1)} %all-to-all-done.x_ref, ...), custom_call_target="tpu_custom_call" | custom-call | flops 1610612736 | bytes 8388608 | tf_op jit(solution)/shard_map/freq_forward/pallas_call | solution.py:130
  26.4 0.8 copy-done.3
  27.2 0.8 copy-done.5
  28.0 0.8 copy-done.7
  28.8 0.8 copy-done.9
  29.6 4.7 %all-to-all-done.2 = bf16[16,8,8,256]{3,2,1,0:T(8,128)(2,1)S(1)} async-done(((bf16[16,8,8,256]{3,2,1,0:T(8,128)(2,1)}), bf16[16,8,8,256]{3,2,1,0:T(8,128)(2,1)S(1)}, u32[]{:S(2)}, u32[]{:S(2)}) %all-to-all-start.2) | async-done | bytes 524320 | tf_op jit(solution)/shard_map/all_to_all | solution.py:363
  34.4 3.1 %all-to-all-start.1 = ((bf16[32,32,256]{2,1,0:T(8,128)(2,1)}), bf16[32,32,256]{2,1,0:T(8,128)(2,1)S(1)}, u32[]{:S(2)}, u32[]{:S(2)}) async-start(bf16[32,32,256]{2,1,0:T(8,128)(2,1)} %bitcast.2), calls=%async_computation.1 | async-start | bytes 1048576 | tf_op jit(solution)/shard_map/all_to_all | solution.py:368
  37.5 15.0 %all-to-all-done.1 = bf16[32,32,256]{2,1,0:T(8,128)(2,1)S(1)} async-done(((bf16[32,32,256]{2,1,0:T(8,128)(2,1)}), bf16[32,32,256]{2,1,0:T(8,128)(2,1)S(1)}, u32[]{:S(2)}, u32[]{:S(2)}) %all-to-all-start.1) | async-done | bytes 524320 | tf_op jit(solution)/shard_map/all_to_all | solution.py:368
  52.5 11.7 %time_attention.1 = (bf16[1024,256]{1,0:T(8,128)(2,1)S(1)}, f32[4,256,256]{2,1,0:T(8,128)S(1)}, f32[1,256]{1,0:T(1,128)S(1)}) custom-call(s32[1]{0:T(128)} %bitcast.1.first_ref, bf16[1024,256]{1,0:T(8,128)(2,1)S(1)} %bitcast.19, bf16[1024,256]{1,0:T(8,128)(2,1)S(1)} %bitcast.18, bf16[8,256,256]{2,1,0:T(8,128)(2,1)S(1)} %copy-done.1, f32[2,256]{1,0:T(2,128)S(1)} %copy-done.2), custom_call_target="tpu_custom_call" | custom-call | flops 3087007744 | bytes 4194304 | tf_op jit(solution)/shard_map/time_attention/pallas_call | solution.py:318
  64.2 18.4 %all_to_all.35 = bf16[32,32,256]{2,1,0:T(8,128)(2,1)S(1)} all-to-all(bf16[32,32,256]{2,1,0:T(8,128)(2,1)S(1)} %bitcast.21), channel_id=1, replica_groups=mesh['tm'=16,'freq'=2] {'tm','freq'}, dimensions={0} | all-to-all | bytes 1048576 | tf_op jit(solution)/shard_map/all_to_all | solution.py:368
  82.7 7.8 %freq_backward.1 = (bf16[2,4,128,256]{3,2,1,0:T(8,128)(2,1)}, f32[4,256,256]{2,1,0:T(8,128)S(1)}, f32[1,256]{1,0:T(1,128)S(1)}) custom-call(bf16[2,4,128,256]{3,2,1,0:T(8,128)(2,1)S(1)} %all-to-all-done.x_ref, bf16[4,256,256]{2,1,0:T(8,128)(2,1)S(1)} %copy-done.4, bf16[4,256,256]{2,1,0:T(8,128)(2,1)S(1)} %copy-done.6, bf16[4,256,256]{2,1,0:T(8,128)(2,1)S(1)} %copy-done.8, ...), custom_call_target="tpu_custom_call" | custom-call | flops 3221225472 | bytes 8388608 | tf_op jit(solution)/shard_map/freq_backward/pallas_call | solution.py:203
  90.9 33.4 %all_to_all.36 = bf16[32,68,256]{2,1,0:T(8,128)(2,1)S(1)} all-to-all(bf16[32,68,256]{2,1,0:T(8,128)(2,1)S(1)} %pad_maximum_fusion), channel_id=1, replica_groups=mesh['tm'=16,'freq'=2] {'tm','freq'}, dimensions={0} | all-to-all | bytes 2228224 | tf_op jit(solution)/shard_map/all_to_all | solution.py:416
  124.4 3.5 %all-to-all-start.4 = ((bf16[2,4,128,256]{3,2,1,0:T(8,128)(2,1)}), bf16[2,4,128,256]{3,2,1,0:T(8,128)(2,1)S(1)}, u32[]{:S(2)}, u32[]{:S(2)}) async-start(bf16[2,4,128,256]{3,2,1,0:T(8,128)(2,1)} %get-tuple-element.22), calls=%async_computation.4 | async-start | bytes 1048576 | tf_op jit(solution)/shard_map/all_to_all | solution.py:405
  128.0 8.7 %all-to-all-done.4 = bf16[2,4,128,256]{3,2,1,0:T(8,128)(2,1)S(1)} async-done(((bf16[2,4,128,256]{3,2,1,0:T(8,128)(2,1)}), bf16[2,4,128,256]{3,2,1,0:T(8,128)(2,1)S(1)}, u32[]{:S(2)}, u32[]{:S(2)}) %all-to-all-start.4) | async-done | bytes 524320 | tf_op jit(solution)/shard_map/all_to_all | solution.py:405
  136.8 1.1 broadcast_in_dim.5
  137.9 2.6 %all-to-all-start.6 = ((bf16[32,64,256]{2,1,0:T(8,128)(2,1)}), bf16[32,64,256]{2,1,0:T(8,128)(2,1)S(1)}, u32[]{:S(2)}, u32[]{:S(2)}) async-start(bf16[32,64,256]{2,1,0:T(8,128)(2,1)} %broadcast_in_dim.5), calls=%async_computation.6 | async-start | bytes 2097152 | tf_op jit(solution)/shard_map/all_to_all | solution.py:421
  140.5 0.6 slice_add_fusion
  141.1 25.6 %all-to-all-done.6 = bf16[32,64,256]{2,1,0:T(8,128)(2,1)S(1)} async-done(((bf16[32,64,256]{2,1,0:T(8,128)(2,1)}), bf16[32,64,256]{2,1,0:T(8,128)(2,1)S(1)}, u32[]{:S(2)}, u32[]{:S(2)}) %all-to-all-start.6) | async-done | bytes 1048608 | tf_op jit(solution)/shard_map/all_to_all | solution.py:421
  166.8 1.5 bitcast_convert_fusion
  168.3 0.8 copy.10
  (25 shorter events, 0.6 us)
Async XLA Ops:
  0.6 4.4 %copy-start = (bf16[8,128,256]{2,1,0:T(8,128)(2,1)S(1)}, bf16[8,128,256]{2,1,0:T(8,128)(2,1)}, u32[]{:S(2)}) copy-start(bf16[8,128,256]{2,1,0:T(8,128)(2,1)} %param.5) | copy-start | bytes 1572868
  0.6 19.3 %copy-start.2 = (f32[2,256]{1,0:T(2,128)S(1)}, f32[2,256]{1,0:T(2,128)}, u32[]{:S(2)}) copy-start(f32[2,256]{1,0:T(2,128)} %gain_ref.5) | copy-start | bytes 6148
  0.7 19.3 %copy-start.1 = (bf16[8,256,256]{2,1,0:T(8,128)(2,1)S(1)}, bf16[8,256,256]{2,1,0:T(8,128)(2,1)}, u32[]{:S(2)}) copy-start(bf16[8,256,256]{2,1,0:T(8,128)(2,1)} %w_ref.5) | copy-start | bytes 3145732
  0.7 13.1 %all-to-all-start = ((bf16[2,4,128,256]{3,2,1,0:T(8,128)(2,1)}), bf16[2,4,128,256]{3,2,1,0:T(8,128)(2,1)S(1)}, u32[]{:S(2)}, u32[]{:S(2)}) async-start(bf16[2,4,128,256]{3,2,1,0:T(8,128)(2,1)} %bitcast.25), calls=%async_computation | async-start | bytes 1048576 | tf_op jit(solution)/shard_map/all_to_all | solution.py:380
  13.8 20.6 %all-to-all-start.2 = ((bf16[16,8,8,256]{3,2,1,0:T(8,128)(2,1)}), bf16[16,8,8,256]{3,2,1,0:T(8,128)(2,1)S(1)}, u32[]{:S(2)}, u32[]{:S(2)}) async-start(bf16[16,8,8,256]{3,2,1,0:T(8,128)(2,1)} %copy_bitcast_fusion), calls=%async_computation.2 | async-start | bytes 1048576 | tf_op jit(solution)/shard_map/all_to_all | solution.py:363
  26.4 0.8 copy-start.3
  27.2 0.8 copy-start.5
  28.0 0.8 copy-start.7
  28.8 0.8 copy-start.9
  34.4 18.1 %all-to-all-start.1 = ((bf16[32,32,256]{2,1,0:T(8,128)(2,1)}), bf16[32,32,256]{2,1,0:T(8,128)(2,1)S(1)}, u32[]{:S(2)}, u32[]{:S(2)}) async-start(bf16[32,32,256]{2,1,0:T(8,128)(2,1)} %bitcast.2), calls=%async_computation.1 | async-start | bytes 1048576 | tf_op jit(solution)/shard_map/all_to_all | solution.py:368
  52.5 30.2 %copy-start.4 = (bf16[4,256,256]{2,1,0:T(8,128)(2,1)S(1)}, bf16[4,256,256]{2,1,0:T(8,128)(2,1)}, u32[]{:S(2)}) copy-start(bf16[4,256,256]{2,1,0:T(8,128)(2,1)} %copy-done.3) | copy-start | bytes 1572868
  52.5 30.2 %copy-start.6 = (bf16[4,256,256]{2,1,0:T(8,128)(2,1)S(1)}, bf16[4,256,256]{2,1,0:T(8,128)(2,1)}, u32[]{:S(2)}) copy-start(bf16[4,256,256]{2,1,0:T(8,128)(2,1)} %copy-done.5) | copy-start | bytes 1572868
  52.5 30.2 %copy-start.8 = (bf16[4,256,256]{2,1,0:T(8,128)(2,1)S(1)}, bf16[4,256,256]{2,1,0:T(8,128)(2,1)}, u32[]{:S(2)}) copy-start(bf16[4,256,256]{2,1,0:T(8,128)(2,1)} %copy-done.7) | copy-start | bytes 1572868
  52.5 30.2 %copy-start.10 = (bf16[4,256,256]{2,1,0:T(8,128)(2,1)S(1)}, bf16[4,256,256]{2,1,0:T(8,128)(2,1)}, u32[]{:S(2)}) copy-start(bf16[4,256,256]{2,1,0:T(8,128)(2,1)} %copy-done.9) | copy-start | bytes 1572868
  124.4 12.4 %all-to-all-start.4 = ((bf16[2,4,128,256]{3,2,1,0:T(8,128)(2,1)}), bf16[2,4,128,256]{3,2,1,0:T(8,128)(2,1)S(1)}, u32[]{:S(2)}, u32[]{:S(2)}) async-start(bf16[2,4,128,256]{3,2,1,0:T(8,128)(2,1)} %get-tuple-element.22), calls=%async_computation.4 | async-start | bytes 1048576 | tf_op jit(solution)/shard_map/all_to_all | solution.py:405
  137.9 28.9 %all-to-all-start.6 = ((bf16[32,64,256]{2,1,0:T(8,128)(2,1)}), bf16[32,64,256]{2,1,0:T(8,128)(2,1)S(1)}, u32[]{:S(2)}, u32[]{:S(2)}) async-start(bf16[32,64,256]{2,1,0:T(8,128)(2,1)} %broadcast_in_dim.5), calls=%async_computation.6 | async-start | bytes 2097152 | tf_op jit(solution)/shard_map/all_to_all | solution.py:421

commit v2 on v1

--- a/solution.py
+++ b/solution.py
@@ -88,13 +88,19 @@
     return g_q, g_k, g_v
 
 
-def freq_forward_kernel(x_ref, w_ref, gain_ref, q_ref, k_ref, v_ref, o_ref, p_ref, h_ref, hold):
+def slot_of(position, back, freq):
+    return lax.rem(position - back + freq, freq)
+
+
+def freq_forward_kernel(
+    place_ref, own_ref, others_ref, w_ref, gain_ref, q_ref, k_ref, v_ref, o_ref, p_ref, h_ref, hold
+):
     step = pl.program_id(0)
-    freq, _, bins_dev, width = x_ref.shape
+    freq, bins_dev, width = others_ref.shape[0] + 1, own_ref.shape[2], own_ref.shape[3]
     bins = freq * bins_dev
     bins_time = hold.shape[2] // pl.num_programs(0)
     scale = (width // HEADS) ** (-0.5)
-    x = x_ref[...].reshape(bins, width).astype(f32)
+    x = joined(own_ref, others_ref)
     _, unit = norm_parts(x)
     n = (unit * gain_ref[0:1, :]).astype(bf16)
     q = dot(n, w_ref[0]).astype(bf16)
@@ -112,54 +118,68 @@
     rows = pl.ds(pl.multiple_of(step * bins_time, bins_time), bins_time)
     for f in range(freq):
         part = hidden[f * bins_dev : (f + 1) * bins_dev].reshape(-1, bins_time, width)
-        hold[:, f, rows, :] = part
+        hold[:, slot_of(place_ref[0], f, freq), rows, :] = part
 
     @pl.when(step == pl.num_programs(0) - 1)
     def _():
         h_ref[...] = hold[...].astype(bf16)
 
 
-def freq_forward(x, weights, gains, group):
-    freq, frames, bins_dev, width = x.shape
+def joined(own_ref, others_ref):
+    width = own_ref.shape[-1]
+    return jnp.concatenate(
+        [own_ref[...].reshape(-1, width), others_ref[...].reshape(-1, width)], axis=0
+    ).astype(f32)
+
+
+def frame_specs(freq, bins_dev, width):
+    own = pl.BlockSpec((1, 1, bins_dev, width), lambda i, place: (place[0], i, 0, 0))
+    others = pl.BlockSpec((freq - 1, 1, bins_dev, width), lambda i, place: (0, i, 0, 0))
+    rows = pl.BlockSpec((1, freq * bins_dev, width), lambda i, place: (i, 0, 0))
+    return own, others, rows
+
+
+def fixed(shape):
+    return pl.BlockSpec(shape, lambda i, place: (0,) * len(shape))
+
+
+def freq_forward(place, features, others, weights, gains, group):
+    freq, frames, bins_dev, width = features.shape
     bins = freq * bins_dev
     rows = frames * (bins_dev // group)
-    rowspec = pl.BlockSpec((1, bins, width), lambda i: (i, 0, 0))
+    own_spec, others_spec, row_spec = frame_specs(freq, bins_dev, width)
     rowshape = jax.ShapeDtypeStruct((frames, bins, width), bf16)
     whole = (group, freq, rows, width)
     flops = frames * 2 * bins * (4 * width * width + 2 * HEADS * bins * width)
     return pl.pallas_call(
         freq_forward_kernel,
-        grid=(frames,),
-        in_specs=[
-            pl.BlockSpec((freq, 1, bins_dev, width), lambda i: (0, i, 0, 0)),
-            pl.BlockSpec(weights.shape, lambda i: (0, 0, 0)),
-            pl.BlockSpec(gains.shape, lambda i: (0, 0)),
-        ],
-        out_specs=[rowspec] * 4
-        + [
-            pl.BlockSpec((1, HEADS, bins, bins), lambda i: (i, 0, 0, 0)),
-            pl.BlockSpec(whole, lambda i: (0, 0, 0, 0)),
-        ],
+        grid_spec=pltpu.PrefetchScalarGridSpec(
+            num_scalar_prefetch=1,
+            grid=(frames,),
+            in_specs=[own_spec, others_spec, fixed(weights.shape), fixed(gains.shape)],
+            out_specs=[row_spec] * 4
+            + [pl.BlockSpec((1, HEADS, bins, bins), lambda i, place: (i, 0, 0, 0)), fixed(whole)],
+            scratch_shapes=[pltpu.VMEM(whole, f32)],
+        ),
         out_shape=[rowshape] * 4
         + [
             jax.ShapeDtypeStruct((frames, HEADS, bins, bins), f32),
             jax.ShapeDtypeStruct(whole, bf16),
         ],
-        scratch_shapes=[pltpu.VMEM(whole, f32)],
         compiler_params=pltpu.CompilerParams(vmem_limit_bytes=VMEM_LIMIT),
         cost_estimate=pl.CostEstimate(
             flops=flops, bytes_accessed=8 * 1024 * 1024, transcendentals=frames * HEADS * bins * bins
         ),
         name="freq_forward",
-    )(x, weights, gains)
+    )(place, features, others, weights, gains)
 
 
 def freq_backward_kernel(
-    x_ref, q_ref, k_ref, v_ref, o_ref, p_ref, gh_ref, w_ref, gain_ref, gx_ref, dw_ref, dg_ref, hold
+    place_ref, own_ref, others_ref, q_ref, k_ref, v_ref, o_ref, p_ref, gh_ref, w_ref, gain_ref,
+    gq_ref, gk_ref, gv_ref, dw_ref, hold, total
 ):
     step = pl.program_id(0)
-    freq, _, bins_dev, width = x_ref.shape
-    bins = freq * bins_dev
+    freq, bins_dev, width = others_ref.shape[0] + 1, own_ref.shape[2], own_ref.shape[3]
     group = hold.shape[0]
     bins_time = bins_dev // group
     scale = (width // HEADS) ** (-0.5)
@@ -167,75 +187,130 @@
     @pl.when(step == 0)
     def _():
         hold[...] = gh_ref[...].astype(f32)
-        dw_ref[...] = jnp.zeros_like(dw_ref)
-        dg_ref[...] = jnp.zeros_like(dg_ref)
-
-    rows = pl.ds(pl.multiple_of(step * bins_time, bins_time), bins_time)
-    grad_hidden = jnp.concatenate(
-        [hold[:, f, rows, :].reshape(bins_dev, width) for f in range(freq)], axis=0
-    )
-    grad_hidden_low = grad_hidden.astype(bf16)
-    grad_out = dot_nt(grad_hidden_low, w_ref[3]).astype(bf16)
+        total[...] = jnp.zeros_like(total)
+
+    grad_hidden = grad_hidden_rows(place_ref, hold, step, freq, bins_time).astype(bf16)
+    grad_out = dot_nt(grad_hidden, w_ref[3]).astype(bf16)
     q, k, v = q_ref[0], k_ref[0], v_ref[0]
     probs = [p_ref[0, h] for h in range(HEADS)]
     g_q, g_k, g_v = attention_backward(probs, grad_out, q, v, spread(k, scale), scale)
     g_q, g_k, g_v = g_q.astype(bf16), g_k.astype(bf16), g_v.astype(bf16)
-    g_n = dot_nt(g_q, w_ref[0]) + dot_nt(g_k, w_ref[1]) + dot_nt(g_v, w_ref[2])
-    x = x_ref[...].reshape(bins, width).astype(f32)
-    inverse, unit = norm_parts(x)
-    gain = gain_ref[0:1, :]
-    n = (unit * gain).astype(bf16)
-    grad_x = grad_hidden + norm_backward(g_n, inverse, unit, gain)
-    gx_ref[...] = grad_x.astype(bf16).reshape(gx_ref.shape)
-    dw_ref[0] += dot_tn(n, g_q)
-    dw_ref[1] += dot_tn(n, g_k)
-    dw_ref[2] += dot_tn(n, g_v)
-    dw_ref[3] += dot_tn(o_ref[0], grad_hidden_low)
-    dg_ref[...] += jnp.sum(g_n * unit, axis=0, keepdims=True)
-
-
-def freq_backward(x, q, k, v, o, probs, grad_hidden, weights, gains):
-    freq, frames, bins_dev, width = x.shape
+    gq_ref[0] = g_q
+    gk_ref[0] = g_k
+    gv_ref[0] = g_v
+    _, unit = norm_parts(joined(own_ref, others_ref))
+    n = (unit * gain_ref[0:1, :]).astype(bf16)
+    total[0] += dot_tn(n, g_q)
+    total[1] += dot_tn(n, g_k)
+    total[2] += dot_tn(n, g_v)
+    total[3] += dot_tn(o_ref[0], grad_hidden)
+
+    @pl.when(step == pl.num_programs(0) - 1)
+    def _():
+        dw_ref[...] = total[...].astype(bf16)
+
+
+def grad_hidden_rows(place_ref, hold, step, freq, bins_time):
+    width = hold.shape[-1]
+    rows = pl.ds(pl.multiple_of(step * bins_time, bins_time), bins_time)
+    return jnp.concatenate(
+        [hold[:, slot_of(place_ref[0], f, freq), rows, :].reshape(-1, width) for f in range(freq)],
+        axis=0,
+    )
+
+
+def freq_backward(place, features, others, q, k, v, o, probs, grad_hidden, weights, gains):
+    freq, frames, bins_dev, width = features.shape
     bins = freq * bins_dev
-    rowspec = pl.BlockSpec((1, bins, width), lambda i: (i, 0, 0))
-    xspec = pl.BlockSpec((freq, 1, bins_dev, width), lambda i: (0, i, 0, 0))
-    flops = frames * 2 * bins * (8 * width * width + 4 * HEADS * bins * width)
+    own_spec, others_spec, row_spec = frame_specs(freq, bins_dev, width)
+    flops = frames * 2 * bins * (5 * width * width + 4 * HEADS * bins * width)
+    rowshape = jax.ShapeDtypeStruct((frames, bins, width), bf16)
     return pl.pallas_call(
         freq_backward_kernel,
-        grid=(frames,),
-        in_specs=[
-            xspec,
-            rowspec,
-            rowspec,
-            rowspec,
-            rowspec,
-            pl.BlockSpec((1, HEADS, bins, bins), lambda i: (i, 0, 0, 0)),
-            pl.BlockSpec(grad_hidden.shape, lambda i: (0, 0, 0, 0)),
-            pl.BlockSpec(weights.shape, lambda i: (0, 0, 0)),
-            pl.BlockSpec(gains.shape, lambda i: (0, 0)),
-        ],
-        out_specs=[
-            xspec,
-            pl.BlockSpec((4, width, width), lambda i: (0, 0, 0)),
-            pl.BlockSpec((1, width), lambda i: (0, 0)),
-        ],
-        out_shape=[
-            jax.ShapeDtypeStruct(x.shape, bf16),
-            jax.ShapeDtypeStruct((4, width, width), f32),
-            jax.ShapeDtypeStruct((1, width), f32),
-        ],
-        scratch_shapes=[pltpu.VMEM(grad_hidden.shape, f32)],
+        grid_spec=pltpu.PrefetchScalarGridSpec(
+            num_scalar_prefetch=1,
+            grid=(frames,),
+            in_specs=[own_spec, others_spec]
+            + [row_spec] * 4
+            + [
+                pl.BlockSpec((1, HEADS, bins, bins), lambda i, place: (i, 0, 0, 0)),
+                fixed(grad_hidden.shape),
+                fixed(weights.shape),
+                fixed(gains.shape),
+            ],
+            out_specs=[row_spec] * 3 + [fixed((4, width, width))],
+            scratch_shapes=[
+                pltpu.VMEM(grad_hidden.shape, f32),
+                pltpu.VMEM((4, width, width), f32),
+            ],
+        ),
+        out_shape=[rowshape] * 3 + [jax.ShapeDtypeStruct((4, width, width), bf16)],
         compiler_params=pltpu.CompilerParams(vmem_limit_bytes=VMEM_LIMIT),
         cost_estimate=pl.CostEstimate(
             flops=flops, bytes_accessed=8 * 1024 * 1024, transcendentals=0
         ),
         name="freq_backward",
-    )(x, q, k, v, o, probs, grad_hidden, weights, gains)
+    )(place, features, others, q, k, v, o, probs, grad_hidden, weights, gains)
+
+
+def input_grad_kernel(
+    place_ref, own_ref, others_ref, gq_ref, gk_ref, gv_ref, gh_ref, w_ref, gain_ref,
+    gown_ref, gothers_ref, dg_ref, hold
+):
+    step = pl.program_id(0)
+    freq, bins_dev, width = others_ref.shape[0] + 1, own_ref.shape[2], own_ref.shape[3]
+    group = hold.shape[0]
+
+    @pl.when(step == 0)
+    def _():
+        hold[...] = gh_ref[...].astype(f32)
+        dg_ref[...] = jnp.zeros_like(dg_ref)
+
+    g_n = dot_nt(gq_ref[0], w_ref[0]) + dot_nt(gk_ref[0], w_ref[1]) + dot_nt(gv_ref[0], w_ref[2])
+    inverse, unit = norm_parts(joined(own_ref, others_ref))
+    grad_hidden = grad_hidden_rows(place_ref, hold, step, freq, bins_dev // group)
+    grad_x = grad_hidden + norm_backward(g_n, inverse, unit, gain_ref[0:1, :])
+    grad_x = grad_x.astype(bf16)
+    gown_ref[0] = grad_x[:bins_dev]
+    gothers_ref[...] = grad_x[bins_dev:].reshape(gothers_ref.shape)
+    dg_ref[...] += jnp.sum(g_n * unit, axis=0, keepdims=True)
+
+
+def input_grad(place, features, others, g_q, g_k, g_v, grad_hidden, weights, gains):
+    freq, frames, bins_dev, width = features.shape
+    own_spec, others_spec, row_spec = frame_specs(freq, bins_dev, width)
+    flops = frames * 2 * freq * bins_dev * 3 * width * width
+    return pl.pallas_call(
+        input_grad_kernel,
+        grid_spec=pltpu.PrefetchScalarGridSpec(
+            num_scalar_prefetch=1,
+            grid=(frames,),
+            in_specs=[own_spec, others_spec]
+            + [row_spec] * 3
+            + [fixed(grad_hidden.shape), fixed(weights.shape), fixed(gains.shape)],
+            out_specs=[
+                pl.BlockSpec((1, bins_dev, width), lambda i, place: (i, 0, 0)),
+                others_spec,
+                fixed((1, width)),
+            ],
+            scratch_shapes=[pltpu.VMEM(grad_hidden.shape, f32)],
+        ),
+        out_shape=[
+            jax.ShapeDtypeStruct((frames, bins_dev, width), bf16),
+            jax.ShapeDtypeStruct(others.shape, bf16),
+            jax.ShapeDtypeStruct((1, width), f32),
+        ],
+        compiler_params=pltpu.CompilerParams(vmem_limit_bytes=VMEM_LIMIT),
+        cost_estimate=pl.CostEstimate(
+            flops=flops, bytes_accessed=4 * 1024 * 1024, transcendentals=0
+        ),
+        name="input_grad",
+    )(place, features, others, g_q, g_k, g_v, grad_hidden, weights, gains)
 
 
 def time_kernel(
-    bins, own_start, total_frames, first_ref, h_ref, up_ref, w_ref, gain_ref, gh_ref, dw_ref,
-    dg_ref, q_s, k_s, v_s, go_s, o_s, gq_s, gk_s, gv_s
+    bins, own_start, total_frames, first_ref, h_ref, up_ref, w_ref, gain_ref, gh_ref, n_ref,
+    o_ref, gq_ref, gk_ref, gv_ref, dg_ref, q_s, k_s, v_s, go_s, o_s, gq_s, gk_s, gv_s
 ):
     span_rows, width = h_ref.shape
     span = span_rows // bins
@@ -285,7 +360,6 @@
 
     lax.fori_loop(0, bins, attend, 0)
 
-    dw_ref[...] = jnp.zeros_like(dw_ref)
     dg_ref[...] = jnp.zeros_like(dg_ref)
 
     def finish(i, carry):
@@ -300,10 +374,11 @@
         up = up_ref[rows, :]
         grad_hidden = up.astype(f32) + norm_backward(g_n, inverse, unit, gain)
         gh_ref[mine, :] = grad_hidden.astype(bf16)
-        dw_ref[0] += dot_tn(n, g_q)
-        dw_ref[1] += dot_tn(n, g_k)
-        dw_ref[2] += dot_tn(n, g_v)
-        dw_ref[3] += dot_tn(get(o_s, rows).astype(bf16), up)
+        n_ref[mine, :] = n
+        o_ref[mine, :] = get(o_s, rows).astype(bf16)
+        gq_ref[mine, :] = g_q
+        gk_ref[mine, :] = g_k
+        gv_ref[mine, :] = g_v
         dg_ref[...] += jnp.sum(g_n * unit, axis=0, keepdims=True)
         return carry
 
@@ -314,16 +389,13 @@
     span_rows, width = hidden.shape
     vmem = pl.BlockSpec(memory_space=pltpu.VMEM)
     span = span_rows // bins
-    flops = 2 * span_rows * (11 * width * width + 6 * HEADS * span * width)
+    flops = 2 * span_rows * (7 * width * width + 6 * HEADS * span * width)
     return pl.pallas_call(
         functools.partial(time_kernel, bins, own_start, total),
         in_specs=[pl.BlockSpec(memory_space=pltpu.SMEM)] + [vmem] * 4,
-        out_specs=[vmem] * 3,
-        out_shape=[
-            jax.ShapeDtypeStruct((own_rows, width), bf16),
-            jax.ShapeDtypeStruct((4, width, width), f32),
-            jax.ShapeDtypeStruct((1, width), f32),
-        ],
+        out_specs=[vmem] * 7,
+        out_shape=[jax.ShapeDtypeStruct((own_rows, width), bf16)] * 6
+        + [jax.ShapeDtypeStruct((1, width), f32)],
         scratch_shapes=[pltpu.VMEM((width // LANES, span_rows, LANES), f32)] * 8,
         compiler_params=pltpu.CompilerParams(vmem_limit_bytes=VMEM_LIMIT),
         cost_estimate=pl.CostEstimate(
@@ -333,6 +405,30 @@
         ),
         name="time_attention",
     )(first, hidden, upstream, weights, gains)
+
+
+def weight_kernel(n_ref, o_ref, gq_ref, gk_ref, gv_ref, up_ref, dw_ref):
+    n = n_ref[...]
+    dw_ref[0] = dot_tn(n, gq_ref[...]).astype(bf16)
+    dw_ref[1] = dot_tn(n, gk_ref[...]).astype(bf16)
+    dw_ref[2] = dot_tn(n, gv_ref[...]).astype(bf16)
+    dw_ref[3] = dot_tn(o_ref[...], up_ref[...]).astype(bf16)
+
+
+def time_weights(n, o, g_q, g_k, g_v, upstream):
+    rows, width = n.shape
+    vmem = pl.BlockSpec(memory_space=pltpu.VMEM)
+    return pl.pallas_call(
+        weight_kernel,
+        in_specs=[vmem] * 6,
+        out_specs=vmem,
+        out_shape=jax.ShapeDtypeStruct((4, width, width), bf16),
+        compiler_params=pltpu.CompilerParams(vmem_limit_bytes=VMEM_LIMIT),
+        cost_estimate=pl.CostEstimate(
+            flops=8 * rows * width * width, bytes_accessed=4 * 1024 * 1024, transcendentals=0
+        ),
+        name="time_weights",
+    )(n, o, g_q, g_k, g_v, upstream)
 
 
 def group_size(devices, bins_dev):
@@ -377,17 +473,28 @@
             parts = [before] + parts + [after]
         return jnp.concatenate(parts, axis=0) if sides else rows
 
-    x = lax.all_to_all(
-        features.reshape(freq, frames, bins_dev, width), "freq", 0, 0, tiled=True
+    place = lax.axis_index("freq").astype(jnp.int32).reshape(1)
+    by_target = features.reshape(freq, frames, bins_dev, width)
+
+    def along_freq(block, steps):
+        return lax.ppermute(block, "freq", [(i, (i + steps) % freq) for i in range(freq)])
+
+    others = jnp.stack(
+        [
+            along_freq(lax.dynamic_index_in_dim(by_target, (place[0] + j) % freq, 0, False), j)
+            for j in range(1, freq)
+        ]
     )
     up_blocks = jnp.swapaxes(upstream.reshape(frames_dev, group, bins_time, width), 0, 1)
     up_rows = over_tm(up_blocks).reshape(-1, width)
-    q, k, v, o, probs, hidden_blocks = freq_forward(x, weights, gains, group)
+    q, k, v, o, probs, hidden_blocks = freq_forward(
+        place, by_target, others, weights, gains, group
+    )
     hidden_rows = over_all(hidden_blocks).reshape(-1, width)
     own_rows = hidden_rows.shape[0]
     position = lax.axis_index("tm") // group
     first = ((position - sides) * group_frames).astype(jnp.int32).reshape(1)
-    grad_rows, time_dw, time_dg = time_attention(
+    grad_rows, n2, o2, g_q2, g_k2, g_v2, time_dg = time_attention(
         first,
         with_sides(hidden_rows),
         with_sides(up_rows),
@@ -399,29 +506,66 @@
         total_frames,
     )
     grad_hidden = over_all(grad_rows.reshape(hidden_blocks.shape))
-    grad_x, freq_dw, freq_dg = freq_backward(
-        x, q, k, v, o, probs, grad_hidden, weights, gains
-    )
-    grad_input = lax.all_to_all(grad_x, "freq", 0, 0, tiled=True).reshape(features.shape)
+    time_dw = time_weights(n2, o2, g_q2, g_k2, g_v2, up_rows)
+
+    core = lax.axis_index("tm") % 2
+    pairs = [(i, i ^ 1) for i in range(tm)]
+    same = [
+        [t * freq + f for t in range(c, tm, 2) for f in range(freq)] for c in range(2)
+    ]
+    peers = len(same[0])
+
+    def over_same(blocks):
+        return lax.all_to_all(
+            blocks, ("tm", "freq"), 0, 0, tiled=True, axis_index_groups=same
+        )
+
+    def pair_sum(partial):
+        halves = partial.reshape(2, -1, width)
+        arrived = lax.ppermute(
+            lax.dynamic_index_in_dim(halves, 1 - core, 0, False), "tm", pairs
+        )
+        kept = lax.dynamic_index_in_dim(halves, core, 0, False)
+        return (kept.astype(f32) + arrived.astype(f32)).astype(bf16).reshape(peers, -1, width)
+
+    time_half = pair_sum(time_dw)
+    g_q1, g_k1, g_v1, freq_dw = freq_backward(
+        place, by_target, others, q, k, v, o, probs, grad_hidden, weights, gains
+    )
+    freq_half = pair_sum(freq_dw)
+    arrived = over_same(jnp.concatenate([freq_half, time_half], axis=1))
+    grad_own, grad_others, freq_dg = input_grad(
+        place, by_target, others, g_q1, g_k1, g_v1, grad_hidden, weights, gains
+    )
+    returned = [grad_own] + [along_freq(grad_others[j - 1], -j) for j in range(1, freq)]
+    grad_input = jnp.roll(jnp.stack(returned), place[0], axis=0).reshape(features.shape)
 
     inv_root = (total_frames * bins_dev * freq) ** (-0.5)
-    devices = tm * freq
-    partial = jnp.concatenate([freq_dw, time_dw], axis=0)
-    pieces = (partial * inv_root).astype(bf16).reshape(devices, -1, width)
+
+    def split(rows):
+        high = rows.astype(bf16)
+        return [high, (rows - high.astype(f32)).astype(bf16)]
+
+    summed = jnp.sum(arrived.astype(f32), axis=0) * inv_root
+    count = summed.shape[0]
     gain_rows = jnp.concatenate([freq_dg, time_dg], axis=0) * inv_root
-    high = gain_rows.astype(bf16)
-    low = (gain_rows - high.astype(f32)).astype(bf16)
-    extra = jnp.broadcast_to(jnp.concatenate([high, low], axis=0)[None], (devices, 4, width))
-    sent = jnp.concatenate([pieces, extra], axis=1)
-    arrived = lax.all_to_all(sent, ("tm", "freq"), 0, 0, tiled=True)
-    summed = jnp.sum(arrived.astype(f32), axis=0)
-    count = pieces.shape[1]
-    gain_grads = summed[count : count + 2] + summed[count + 2 :]
-    own = summed[:count].astype(bf16)
-    gathered = lax.all_to_all(
-        jnp.broadcast_to(own[None], (devices,) + own.shape), ("tm", "freq"), 0, 0, tiled=True
-    )
-    weight_grads = gathered.astype(f32).reshape(partial.shape)
+    sent = jnp.concatenate([summed.astype(bf16)] + split(gain_rows), axis=0)
+    gathered = over_same(jnp.broadcast_to(sent[None], (peers,) + sent.shape))
+    gain_sum = jnp.sum(gathered[:, count:].astype(f32), axis=0)
+    gain_sum = gain_sum[:2] + gain_sum[2:]
+    mine = gathered[:, :count].reshape(-1, width)
+    theirs = lax.ppermute(jnp.concatenate([mine] + split(gain_sum), axis=0), "tm", pairs)
+    gain_high_low = split(gain_sum)
+    other_gain = theirs[-4:].astype(f32)
+    gain_grads = sum(g.astype(f32) for g in gain_high_low) + other_gain[:2] + other_gain[2:]
+    theirs = theirs[:-4]
+    first_core = core == 0
+    halves = jnp.stack(
+        [jnp.where(first_core, mine, theirs), jnp.where(first_core, theirs, mine)]
+    )
+    weight_grads = (
+        halves.reshape(2, peers, 2, -1, width).transpose(2, 0, 1, 3, 4).astype(f32)
+    ).reshape(8, width, width)
     return (grad_input, weight_grads, gain_grads)
 
 

time: 170 us -> 160 us (0.941)
  blocking collectives: 51.9 us -> 21 us
  local copies, waits for them, and re-layouts: 5.98 us -> 28.7 us
  waiting for transfers between devices: 62 us -> 50.4 us
  starting transfers between devices: 19.7 us -> 24.5 us
  other arithmetic: 2.61 us -> 6.06 us
    all_to_all x3 -> x1, waiting for transfers between devices: 42.2 us -> 10.7 us  [over_same(): lax.all_to_all(blocks, ('tm', 'freq'), 0, 0, tiled=True, axis_index_group...]
    all_to_all x2 -> x1, blocking collectives: 51.9 us -> 21 us  [over_same(): lax.all_to_all(blocks, ('tm', 'freq'), 0, 0, tiled=True, axis_index_group...]
    unnamed x23 -> x70, local copies, waits for them, and re-layouts: 4.01 us -> 24.5 us
    ppermute x0 -> x5, waiting for transfers between devices: none -> 15.6 us  [the longest x2 15.1 us: along_freq(): lax.ppermute(block, 'freq', [(i, (i + steps) % freq) for i in range(freq)])]
    all_to_all x1 -> x2, waiting for transfers between devices: 15 us -> 24.1 us  [over_all(): lax.all_to_all(flat, ('tm', 'freq'), 0, 0, tiled=True).reshape(blocks.shape)]
    all_to_all x3 -> x1, starting transfers between devices: 10.5 us -> 4.24 us  [over_same(): lax.all_to_all(blocks, ('tm', 'freq'), 0, 0, tiled=True, axis_index_group...]
    all_to_all x1 -> x2, starting transfers between devices: 3.08 us -> 9.32 us  [over_all(): lax.all_to_all(flat, ('tm', 'freq'), 0, 0, tiled=True).reshape(blocks.shape)]
    all_to_all x1, waiting for transfers between devices: 4.74 us -> 0.01 us  [over_tm(): lax.all_to_all(blocks, 'tm', 0, 0, tiled=True, axis_index_groups=groups)]
  transfers between devices with their start and end apart: 5 -> 9, of which waited for: 5 -> 6; matrix products, arithmetic and copies ran while one was open for 1% -> 2% of each run, Pallas kernels for 4% -> 10%
where the time goes in v2:
time: 160 us; the launch traced here: 159 us
  waiting for transfers between devices  50.4 us (32%)
  local copies, waits for them, and re-layouts  28.7 us (18%)
  Pallas kernels  27.2 us (17%)
  starting transfers between devices  24.5 us (15%)
  blocking collectives  21 us (13%)
  other arithmetic  6.06 us (4%)
    unnamed x70, local copies, waits for them, and re-layouts  24.5 us
    all_to_all x2, waiting for transfers between devices, over_all(): lax.all_to_all(flat, ('tm', 'freq'), 0, 0, tiled=True).reshape(blocks.shape)  24.1 us
    all_to_all x1, blocking collectives, over_same(): lax.all_to_all(blocks, ('tm', 'freq'), 0, 0, tiled=True, axis_index_group...  21 us
    ppermute x2, waiting for transfers between devices, along_freq(): lax.ppermute(block, 'freq', [(i, (i + steps) % freq) for i in range(freq)])  15.1 us
    pallas_call x1, Pallas kernels, time_attention(): pl.pallas_call(functools.partial(time_kernel, bins, own_start, total), in...  11.1 us
    all_to_all x1, waiting for transfers between devices, over_same(): lax.all_to_all(blocks, ('tm', 'freq'), 0, 0, tiled=True, axis_index_group...  10.7 us
    all_to_all x2, starting transfers between devices, over_all(): lax.all_to_all(flat, ('tm', 'freq'), 0, 0, tiled=True).reshape(blocks.shape)  9.32 us
    pallas_call x1, Pallas kernels, freq_backward(): pl.pallas_call(freq_backward_kernel, grid_spec=pltpu.PrefetchScalarGridSp...  7.36 us
  transfers between devices with their start and end apart: 9, of which 6 were waited for; matrix products, arithmetic and copies ran while one was open for 2% of the time, Pallas kernels for 10%

profile of v2, /device:TPU:0, one launch (start us, length us, event | category | flops | bytes accessed | tf_op | source)
XLA Modules:
  0.0 159.0 jit_solution(11699773347875768468)
XLA Ops:
  2.5 7.4 %all-to-all-start.1 = ((bf16[16,8,8,256]{3,2,1,0:T(8,128)(2,1)}), bf16[16,8,8,256]{3,2,1,0:T(8,128)(2,1)S(1)}, u32[]{:S(2)}, u32[]{:S(2)}) async-start(bf16[16,8,8,256]{3,2,1,0:T(8,128)(2,1)} %copy_bitcast_fusion), calls=%async_computation.1 | async-start | bytes 1048576 | tf_op jit(solution)/shard_map/all_to_all | solution.py:459
  10.0 1.6 %collective-permute-start = (bf16[4,128,256]{2,1,0:T(8,128)(2,1)S(1)}, bf16[4,128,256]{2,1,0:T(8,128)(2,1)S(1)}, u32[]{:S(2)}, u32[]{:S(2)}) collective-permute-start(bf16[4,128,256]{2,1,0:T(8,128)(2,1)S(1)} %dynamic-slice_bitcast_fusion.2), channel_id=1, source_target_pairs={{0,1},{1,0},{2,3},{3,2},{4,5},{5,4},{6,7},{7,6},{8,9},{9,8},{10,11... | collective-permute-start | bytes 786440 | tf_op jit(solution)/shard_map/ppermute | solution.py:480
  11.6 7.1 %collective-permute-done = bf16[4,128,256]{2,1,0:T(8,128)(2,1)S(1)} collective-permute-done((bf16[4,128,256]{2,1,0:T(8,128)(2,1)S(1)}, bf16[4,128,256]{2,1,0:T(8,128)(2,1)S(1)}, u32[]{:S(2)}, u32[]{:S(2)}) %collective-permute-start) | collective-permute-done | bytes 262176 | tf_op jit(solution)/shard_map/ppermute | solution.py:480
  18.6 6.3 %freq_forward.1 = (bf16[4,256,256]{2,1,0:T(8,128)(2,1)S(1)}, bf16[4,256,256]{2,1,0:T(8,128)(2,1)S(1)}, bf16[4,256,256]{2,1,0:T(8,128)(2,1)S(1)}, bf16[4,256,256]...) custom-call(s32[1]{0:T(128)} %bitcast.place_ref, ...), custom_call_target="tpu_custom_call" | custom-call | flops 1610612736 | bytes 8388608 | tf_op jit(solution)/shard_map/freq_forward/pallas_call | solution.py:154
  29.0 5.7 %all-to-all-start = ((bf16[32,32,256]{2,1,0:T(8,128)(2,1)}), bf16[32,32,256]{2,1,0:T(8,128)(2,1)S(1)}, u32[]{:S(2)}, u32[]{:S(2)}) async-start(bf16[32,32,256]{2,1,0:T(8,128)(2,1)} %bitcast.53), calls=%async_computation | async-start | bytes 1048576 | tf_op jit(solution)/shard_map/all_to_all | solution.py:464
  34.7 15.0 %all-to-all-done = bf16[32,32,256]{2,1,0:T(8,128)(2,1)S(1)} async-done(((bf16[32,32,256]{2,1,0:T(8,128)(2,1)}), bf16[32,32,256]{2,1,0:T(8,128)(2,1)S(1)}, u32[]{:S(2)}, u32[]{:S(2)}) %all-to-all-start) | async-done | bytes 524320 | tf_op jit(solution)/shard_map/all_to_all | solution.py:464
  51.5 11.1 %time_attention.1 = (bf16[1024,256]{1,0:T(8,128)(2,1)S(1)}, bf16[1024,256]{1,0:T(8,128)(2,1)S(1)}, bf16[1024,256]{1,0:T(8,128)(2,1)S(1)}, bf16[1024,256]{1,0:T(8...) custom-call(s32[1]{0:T(128)} %bitcast.4.first_ref, ...), custom_call_target="tpu_custom_call" | custom-call | flops 2550136832 | bytes 4194304 | tf_op jit(solution)/shard_map/time_attention/pallas_call | solution.py:393
  66.6 3.6 %all-to-all-start.2 = ((bf16[32,32,256]{2,1,0:T(8,128)(2,1)}), bf16[32,32,256]{2,1,0:T(8,128)(2,1)S(1)}, u32[]{:S(2)}, u32[]{:S(2)}) async-start(bf16[32,32,256]{2,1,0:T(8,128)(2,1)} %bitcast.54), calls=%async_computation.2 | async-start | bytes 1048576 | tf_op jit(solution)/shard_map/all_to_all | solution.py:464
  72.4 1.0 copy-done.9
  73.4 1.0 copy-done.11
  76.2 9.1 %all-to-all-done.2 = bf16[32,32,256]{2,1,0:T(8,128)(2,1)S(1)} async-done(((bf16[32,32,256]{2,1,0:T(8,128)(2,1)}), bf16[32,32,256]{2,1,0:T(8,128)(2,1)S(1)}, u32[]{:S(2)}, u32[]{:S(2)}) %all-to-all-start.2) | async-done | bytes 524320 | tf_op jit(solution)/shard_map/all_to_all | solution.py:464
  85.3 1.0 copy-done.28
  86.3 1.0 copy-done.30
  89.4 7.4 %freq_backward.1 = (bf16[4,256,256]{2,1,0:T(8,128)(2,1)S(1)}, bf16[4,256,256]{2,1,0:T(8,128)(2,1)S(1)}, bf16[4,256,256]{2,1,0:T(8,128)(2,1)S(1)}, bf16[4,256,256]{2,1,0:T(8,128)(2,1)S(1)}) custom-call(s32[1]{0:T(128)} %bitcast.place_ref, bf16[2,4,128,256]{3,2,1,0:T(8,128)(2,1)S(1)} %bitcast.50, bf16[1,4,128,256]{3,2,1,0:T(8,128)(2,1)S(1)} %bitcast.59, ...), custom_call_target="tpu_custom_call" | custom-call | flops 2818572288 | bytes 8388608 | tf_op jit(solution)/shard_map/freq_backward/pallas_call | solution.py:228
  100.0 1.1 collective-permute-start.2
  104.4 4.2 %all-to-all-start.3 = ((bf16[16,64,256]{2,1,0:T(8,128)(2,1)}), bf16[16,64,256]{2,1,0:T(8,128)(2,1)}, u32[]{:S(2)}, u32[]{:S(2)}) async-start(bf16[16,64,256]{2,1,0:T(8,128)(2,1)} %pad_maximum_fusion), calls=%async_computation.3 | async-start | bytes 1048576 | tf_op jit(solution)/shard_map/all_to_all | solution.py:519
  108.7 1.2 copy-done.3
  110.9 1.8 %input_grad.1 = (bf16[4,128,256]{2,1,0:T(8,128)(2,1)S(1)}, bf16[1,4,128,256]{3,2,1,0:T(8,128)(2,1)S(1)}, f32[1,256]{1,0:T(1,128)S(1)}) custom-call(s32[1]{0:T(128)} %bitcast.place_ref, bf16[2,4,128,256]{3,2,1,0:T(8,128)(2,1)S(1)} %bitcast.51, bf16[1,4,128,256]{3,2,1,0:T(8,128)(2,1)S(1)} %bitcast.60, bf16[4,256,256]{2,1,0:T(8,128)(2,1)S(1)} %copy-done.17, ...), custom_call_target="tpu_custom_call" | custom-call | flops 402653184 | bytes 4194304 | tf_op jit(solution)/shard_map/input_grad/pallas_call | solution.py:283
  113.4 10.7 %all-to-all-done.3 = bf16[16,64,256]{2,1,0:T(8,128)(2,1)} async-done(((bf16[16,64,256]{2,1,0:T(8,128)(2,1)}), bf16[16,64,256]{2,1,0:T(8,128)(2,1)}, u32[]{:S(2)}, u32[]{:S(2)}) %all-to-all-start.3) | async-done | bytes 524320 | tf_op jit(solution)/shard_map/all_to_all | solution.py:519
  124.1 1.1 convert_reduce_fusion
  125.3 21.0 %all_to_all.25 = bf16[16,68,256]{2,1,0:T(8,128)(2,1)S(1)} all-to-all(bf16[16,68,256]{2,1,0:T(8,128)(2,1)S(1)} %broadcast_in_dim.2), channel_id=1, replica_groups={{0,1,4,5,8,9,12,13,16,17,20,21,24,25,28,29},{2,3,6,7,10,11,14,15,18,19,..., dimensions={0} | all-to-all | bytes 1114112 | tf_op jit(solution)/shard_map/all_to_all | solution.py:519
  147.3 8.1 %collective-permute-done.1 = bf16[4,128,256]{2,1,0:T(8,128)(2,1)S(1)} collective-permute-done((bf16[4,128,256]{2,1,0:T(8,128)(2,1)S(1)}, bf16[4,128,256]{2,1,0:T(8,128)(2,1)S(1)}, u32[]{:S(2)}, u32[]{:S(2)}) %collective-permute-start.1) | collective-permute-done | bytes 262176 | tf_op jit(solution)/shard_map/ppermute | solution.py:480
  155.4 1.2 fusion.2
  157.4 1.6 copy.8
  (92 shorter events, 27.7 us)
Async XLA Ops:
  0.6 1.0 copy-start
  0.6 9.3 %copy-start.1 = (bf16[8,128,256]{2,1,0:T(8,128)(2,1)S(1)}, bf16[8,128,256]{2,1,0:T(8,128)(2,1)}, u32[]{:S(2)}) copy-start(bf16[8,128,256]{2,1,0:T(8,128)(2,1)} %param.4) | copy-start | bytes 1572868
  0.7 18.0 %copy-start.24 = (f32[2,256]{1,0:T(2,128)S(1)}, f32[2,256]{1,0:T(2,128)}, u32[]{:S(2)}) copy-start(f32[2,256]{1,0:T(2,128)} %gain_ref.7) | copy-start | bytes 6148
  1.7 17.0 %copy-start.2 = (bf16[8,256,256]{2,1,0:T(8,128)(2,1)S(1)}, bf16[8,256,256]{2,1,0:T(8,128)(2,1)}, u32[]{:S(2)}) copy-start(bf16[8,256,256]{2,1,0:T(8,128)(2,1)} %w_ref.7) | copy-start | bytes 3145732
  2.5 26.4 %all-to-all-start.1 = ((bf16[16,8,8,256]{3,2,1,0:T(8,128)(2,1)}), bf16[16,8,8,256]{3,2,1,0:T(8,128)(2,1)S(1)}, u32[]{:S(2)}, u32[]{:S(2)}) async-start(bf16[16,8,8,256]{3,2,1,0:T(8,128)(2,1)} %copy_bitcast_fusion), calls=%async_computation.1 | async-start | bytes 1048576 | tf_op jit(solution)/shard_map/all_to_all | solution.py:459
  10.0 8.7 %collective-permute-start = (bf16[4,128,256]{2,1,0:T(8,128)(2,1)S(1)}, bf16[4,128,256]{2,1,0:T(8,128)(2,1)S(1)}, u32[]{:S(2)}, u32[]{:S(2)}) collective-permute-start(bf16[4,128,256]{2,1,0:T(8,128)(2,1)S(1)} %dynamic-slice_bitcast_fusion.2), channel_id=1, source_target_pairs={{0,1},{1,0},{2,3},{3,2},{4,5},{5,4},{6,7},{7,6},{8,9},{9,8},{10,11... | collective-permute-start | bytes 786440 | tf_op jit(solution)/shard_map/ppermute | solution.py:480
  18.6 66.6 %copy-start.22 = (bf16[4,128,256]{2,1,0:T(8,128)(2,1)}, bf16[4,128,256]{2,1,0:T(8,128)(2,1)S(1)}, u32[]{:S(2)}) copy-start(bf16[4,128,256]{2,1,0:T(8,128)(2,1)S(1)} %collective-permute-done) | copy-start | bytes 786436
  29.0 20.7 %all-to-all-start = ((bf16[32,32,256]{2,1,0:T(8,128)(2,1)}), bf16[32,32,256]{2,1,0:T(8,128)(2,1)S(1)}, u32[]{:S(2)}, u32[]{:S(2)}) async-start(bf16[32,32,256]{2,1,0:T(8,128)(2,1)} %bitcast.53), calls=%async_computation | async-start | bytes 1048576 | tf_op jit(solution)/shard_map/all_to_all | solution.py:464
  66.6 18.6 %all-to-all-start.2 = ((bf16[32,32,256]{2,1,0:T(8,128)(2,1)}), bf16[32,32,256]{2,1,0:T(8,128)(2,1)S(1)}, u32[]{:S(2)}, u32[]{:S(2)}) async-start(bf16[32,32,256]{2,1,0:T(8,128)(2,1)} %bitcast.54), calls=%async_computation.2 | async-start | bytes 1048576 | tf_op jit(solution)/shard_map/all_to_all | solution.py:464
  70.3 1.0 copy-start.5
  71.3 1.0 copy-start.7
  72.4 1.0 copy-start.9
  73.4 1.0 copy-start.11
  75.9 25.1 %collective-permute-start.3 = (bf16[512,256]{1,0:T(8,128)(2,1)}, bf16[512,256]{1,0:T(8,128)(2,1)}, u32[]{:S(2)}, u32[]{:S(2)}) collective-permute-start(bf16[512,256]{1,0:T(8,128)(2,1)} %dynamic-slice_bitcast_fusion), channel_id=1, source_target_pairs={{0,2},{2,0},{4,6},{6,4},{8,10},{10,8},{12,14},{14,12},{16,18},{18,... | collective-permute-start | bytes 786440 | tf_op jit(solution)/shard_map/ppermute | solution.py:525
  85.3 1.0 copy-start.28
  99.2 9.4 %copy-start.17 = (bf16[4,256,256]{2,1,0:T(8,128)(2,1)S(1)}, bf16[4,256,256]{2,1,0:T(8,128)(2,1)}, u32[]{:S(2)}) copy-start(bf16[4,256,256]{2,1,0:T(8,128)(2,1)} %copy-done.16) | copy-start | bytes 1572868
  100.0 2.6 %collective-permute-start.2 = (bf16[512,256]{1,0:T(8,128)(2,1)}, bf16[512,256]{1,0:T(8,128)(2,1)}, u32[]{:S(2)}, u32[]{:S(2)}) collective-permute-start(bf16[512,256]{1,0:T(8,128)(2,1)} %dynamic-slice_bitcast_fusion.1), channel_id=1, source_target_pairs={{0,2},{2,0},{4,6},{6,4},{8,10},{10,8},{12,14},{14,12},{16,18},{18,... | collective-permute-start | bytes 786440 | tf_op jit(solution)/shard_map/ppermute | solution.py:525
  102.0 6.6 %copy-start.19 = (bf16[4,256,256]{2,1,0:T(8,128)(2,1)S(1)}, bf16[4,256,256]{2,1,0:T(8,128)(2,1)}, u32[]{:S(2)}) copy-start(bf16[4,256,256]{2,1,0:T(8,128)(2,1)} %copy-done.18) | copy-start | bytes 1572868
  103.5 5.1 %copy-start.21 = (bf16[4,256,256]{2,1,0:T(8,128)(2,1)S(1)}, bf16[4,256,256]{2,1,0:T(8,128)(2,1)}, u32[]{:S(2)}) copy-start(bf16[4,256,256]{2,1,0:T(8,128)(2,1)} %copy-done.20) | copy-start | bytes 1572868
  104.4 19.7 %all-to-all-start.3 = ((bf16[16,64,256]{2,1,0:T(8,128)(2,1)}), bf16[16,64,256]{2,1,0:T(8,128)(2,1)}, u32[]{:S(2)}, u32[]{:S(2)}) async-start(bf16[16,64,256]{2,1,0:T(8,128)(2,1)} %pad_maximum_fusion), calls=%async_computation.3 | async-start | bytes 1048576 | tf_op jit(solution)/shard_map/all_to_all | solution.py:519
  108.7 1.2 copy-start.3
  125.2 21.5 %copy-start.26 = (bf16[1,4,128,256]{3,2,1,0:T(8,128)(2,1)S(1)}, bf16[1,4,128,256]{3,2,1,0:T(8,128)(2,1)}, u32[]{:S(2)}) copy-start(bf16[1,4,128,256]{3,2,1,0:T(8,128)(2,1)} %copy-done.25) | copy-start | bytes 786436
  146.6 10.0 %collective-permute-start.4 = (bf16[1028,256]{1,0:T(8,128)(2,1)S(1)}, bf16[1028,256]{1,0:T(8,128)(2,1)S(1)}, u32[]{:S(2)}, u32[]{:S(2)}) collective-permute-start(bf16[1028,256]{1,0:T(8,128)(2,1)S(1)} %concatenate.22), channel_id=1, source_target_pairs={{0,2},{2,0},{4,6},{6,4},{8,10},{10,8},{12,14},{14,12},{16,18},{18,... | collective-permute-start | bytes 1579016 | tf_op jit(solution)/shard_map/ppermute | solution.py:557
  146.7 8.7 %collective-permute-start.1 = (bf16[4,128,256]{2,1,0:T(8,128)(2,1)S(1)}, bf16[4,128,256]{2,1,0:T(8,128)(2,1)S(1)}, u32[]{:S(2)}, u32[]{:S(2)}) collective-permute-start(bf16[4,128,256]{2,1,0:T(8,128)(2,1)S(1)} %bitcast.61), channel_id=1, source_target_pairs={{0,1},{1,0},{2,3},{3,2},{4,5},{5,4},{6,7},{7,6},{8,9},{9,8},{10,11... | collective-permute-start | bytes 786440 | tf_op jit(solution)/shard_map/ppermute | solution.py:480
  (20 other events, 17.1 us)

commit v3 on v2

v3 whole, which is shorter than its diff:
```python
import functools

import jax
import jax.numpy as jnp
from jax import lax
from jax.experimental import pallas as pl
from jax.experimental.pallas import tpu as pltpu
from jax.sharding import PartitionSpec as P

HEADS = 4
WINDOW = 128

epsilon = 1e-06
masked_score = -1e30

f32 = jnp.float32
bf16 = jnp.bfloat16
LANES = 128
VMEM_LIMIT = 62 * 1024 * 1024

CONTRACT_LAST = (((1,), (1,)), ((), ()))
CONTRACT_FIRST = (((0,), (0,)), ((), ()))


def dot(left, right):
    return jnp.dot(left, right, preferred_element_type=f32)


def dot_nt(left, right):
    return lax.dot_general(left, right, CONTRACT_LAST, preferred_element_type=f32)


def dot_tn(left, right):
    return lax.dot_general(left, right, CONTRACT_FIRST, preferred_element_type=f32)


def put(ref, rows, value):
    for c in range(ref.shape[0]):
        ref[c, rows, :] = value[:, c * LANES : (c + 1) * LANES]


def get(ref, rows):
    return jnp.concatenate([ref[c, rows, :] for c in range(ref.shape[0])], axis=1)


def norm_parts(widened):
    inverse = lax.rsqrt(jnp.mean(widened * widened, axis=-1, keepdims=True) + epsilon)
    return inverse, widened * inverse


def norm_backward(incoming, inverse, unit_rows, gain):
    scaled = incoming * gain
    return inverse * (scaled - unit_rows * jnp.mean(scaled * unit_rows, axis=-1, keepdims=True))


def spread(rows, factor):
    width = rows.shape[-1]
    owner = lax.broadcasted_iota(jnp.int32, (1, width), 1) // (width // HEADS)
    return jnp.concatenate(
        [rows * jnp.where(owner == h, factor, 0.0).astype(rows.dtype) for h in range(HEADS)], axis=0
    )


def own_channels(stacked, rows):
    width = stacked.shape[-1]
    owner = lax.broadcasted_iota(jnp.int32, (1, width), 1) // (width // HEADS)
    result = stacked[:rows]
    for h in range(1, HEADS):
        result = jnp.where(owner == h, stacked[h * rows : (h + 1) * rows], result)
    return result


def head_probs(scores, allowed):
    rows = scores.shape[0] // HEADS
    probs = []
    for h in range(HEADS):
        s = scores[h * rows : (h + 1) * rows]
        if allowed is not None:
            s = jnp.where(allowed, s, masked_score)
        e = jnp.exp(s - jnp.max(s, axis=-1, keepdims=True))
        probs.append(e * (1.0 / jnp.sum(e, axis=-1, keepdims=True)))
    return probs


def head_grads(probs, grad_probs, scale):
    rows = grad_probs.shape[0] // HEADS
    grad_scores = []
    for h in range(HEADS):
        gp = grad_probs[h * rows : (h + 1) * rows]
        row_dot = jnp.sum(gp * probs[h], axis=-1, keepdims=True)
        grad_scores.append((probs[h] * (gp - row_dot) * scale).astype(bf16))
    return jnp.concatenate(grad_scores, axis=0)


def stacked_low(probs):
    return jnp.concatenate([p.astype(bf16) for p in probs], axis=0)


def slot_of(position, back, freq):
    return lax.rem(position - back + freq, freq)


def freq_forward_kernel(
    place_ref, own_ref, others_ref, w_ref, gain_ref, q_ref, k_ref, v_ref, o_ref, p_ref, h_ref, hold
):
    step = pl.program_id(0)
    freq, bins_dev, width = others_ref.shape[0] + 1, own_ref.shape[2], own_ref.shape[3]
    bins = freq * bins_dev
    bins_time = hold.shape[2] // pl.num_programs(0)
    scale = (width // HEADS) ** (-0.5)
    x = joined(own_ref, others_ref)
    _, unit = norm_parts(x)
    n = (unit * gain_ref[0:1, :]).astype(bf16)
    q = dot(n, w_ref[0]).astype(bf16)
    k = dot(n, w_ref[1]).astype(bf16)
    v = dot(n, w_ref[2]).astype(bf16)
    probs = head_probs(dot_nt(spread(q, scale), k), None)
    o = own_channels(dot(stacked_low(probs), v), bins)
    for h in range(HEADS):
        p_ref[0, h] = probs[h]
    o = o.astype(bf16)
    hidden = x + dot(o, w_ref[3])
    q_ref[0] = q
    k_ref[0] = k
    v_ref[0] = v
    o_ref[0] = o
    rows = pl.ds(pl.multiple_of(step * bins_time, bins_time), bins_time)
    for f in range(freq):
        part = hidden[f * bins_dev : (f + 1) * bins_dev].reshape(-1, bins_time, width)
        hold[:, slot_of(place_ref[0], f, freq), rows, :] = part

    @pl.when(step == pl.num_programs(0) - 1)
    def _():
        h_ref[...] = hold[...].astype(bf16)


def joined(own_ref, others_ref):
    width = own_ref.shape[-1]
    return jnp.concatenate(
        [own_ref[...].reshape(-1, width), others_ref[...].reshape(-1, width)], axis=0
    ).astype(f32)


def frame_specs(freq, bins_dev, width):
    own = pl.BlockSpec((1, 1, bins_dev, width), lambda i, place: (place[0], i, 0, 0))
    others = pl.BlockSpec((freq - 1, 1, bins_dev, width), lambda i, place: (0, i, 0, 0))
    rows = pl.BlockSpec((1, freq * bins_dev, width), lambda i, place: (i, 0, 0))
    return own, others, rows


def fixed(shape):
    return pl.BlockSpec(shape, lambda i, place: (0,) * len(shape))


def freq_forward(place, features, others, weights, gains, group):
    freq, frames, bins_dev, width = features.shape
    bins = freq * bins_dev
    rows = frames * (bins_dev // group)
    own_spec, others_spec, row_spec = frame_specs(freq, bins_dev, width)
    rowshape = jax.ShapeDtypeStruct((frames, bins, width), bf16)
    whole = (group, freq, rows, width)
    flops = frames * 2 * bins * (4 * width * width + 2 * HEADS * bins * width)
    return pl.pallas_call(
        freq_forward_kernel,
        grid_spec=pltpu.PrefetchScalarGridSpec(
            num_scalar_prefetch=1,
            grid=(frames,),
            in_specs=[own_spec, others_spec, fixed((4, width, width)), fixed(gains.shape)],
            out_specs=[row_spec] * 4
            + [pl.BlockSpec((1, HEADS, bins, bins), lambda i, place: (i, 0, 0, 0)), fixed(whole)],
            scratch_shapes=[pltpu.VMEM(whole, f32)],
        ),
        out_shape=[rowshape] * 4
        + [
            jax.ShapeDtypeStruct((frames, HEADS, bins, bins), f32),
            jax.ShapeDtypeStruct(whole, bf16),
        ],
        compiler_params=pltpu.CompilerParams(vmem_limit_bytes=VMEM_LIMIT),
        cost_estimate=pl.CostEstimate(
            flops=flops, bytes_accessed=8 * 1024 * 1024, transcendentals=frames * HEADS * bins * bins
        ),
        name="freq_forward",
    )(place, features, others, weights, gains)


def freq_backward_kernel(
    place_ref, own_ref, others_ref, q_ref, k_ref, v_ref, o_ref, p_ref, gh_ref, w_ref, gain_ref,
    gown_ref, gothers_ref, kept_ref, sent_ref, dg_ref, hold, total
):
    step = pl.program_id(0)
    freq, bins_dev, width = others_ref.shape[0] + 1, own_ref.shape[2], own_ref.shape[3]
    group = hold.shape[0]
    bins_time = bins_dev // group
    scale = (width // HEADS) ** (-0.5)

    @pl.when(step == 0)
    def _():
        hold[...] = gh_ref[...].astype(f32)
        total[...] = jnp.zeros_like(total)
        dg_ref[...] = jnp.zeros_like(dg_ref)

    grad_hidden = grad_hidden_rows(place_ref, hold, step, freq, bins_time)
    grad_hidden_low = grad_hidden.astype(bf16)
    grad_out = dot_nt(grad_hidden_low, w_ref[3]).astype(bf16)
    out_spread = spread(grad_out, 1.0)
    grad_probs = dot_nt(out_spread, v_ref[0])
    probs = [p_ref[0, h] for h in range(HEADS)]
    g_v = dot_tn(stacked_low(probs), out_spread).astype(bf16)
    grad_scores = head_grads(probs, grad_probs, scale)
    g_q = own_channels(dot(grad_scores, k_ref[0]), freq * bins_dev).astype(bf16)
    g_k = dot_tn(grad_scores, spread(q_ref[0], 1.0)).astype(bf16)
    inverse, unit = norm_parts(joined(own_ref, others_ref))
    gain = gain_ref[0:1, :]
    n = (unit * gain).astype(bf16)
    total[0] += dot_tn(n, g_q)
    total[1] += dot_tn(n, g_k)
    total[2] += dot_tn(n, g_v)
    total[3] += dot_tn(o_ref[0], grad_hidden_low)
    g_n = dot_nt(g_q, w_ref[0]) + dot_nt(g_k, w_ref[1]) + dot_nt(g_v, w_ref[2])
    grad_x = grad_hidden + norm_backward(g_n, inverse, unit, gain)
    grad_x = grad_x.astype(bf16)
    gown_ref[0] = grad_x[:bins_dev]
    gothers_ref[...] = grad_x[bins_dev:].reshape(gothers_ref.shape)
    dg_ref[...] += jnp.sum(g_n * unit, axis=0, keepdims=True)

    @pl.when(step == pl.num_programs(0) - 1)
    def _():
        put_halves(place_ref[1], total, kept_ref, sent_ref)


def put_halves(core, total, kept_ref, sent_ref):
    half = kept_ref.shape[0]
    kept_ref[...] = total[pl.ds(core * half, half)].astype(bf16)
    sent_ref[...] = total[pl.ds((1 - core) * half, half)].astype(bf16)


def grad_hidden_rows(place_ref, hold, step, freq, bins_time):
    width = hold.shape[-1]
    rows = pl.ds(pl.multiple_of(step * bins_time, bins_time), bins_time)
    return jnp.concatenate(
        [hold[:, slot_of(place_ref[0], f, freq), rows, :].reshape(-1, width) for f in range(freq)],
        axis=0,
    )


def freq_backward(place, features, others, q, k, v, o, probs, grad_hidden, weights, gains):
    freq, frames, bins_dev, width = features.shape
    bins = freq * bins_dev
    own_spec, others_spec, row_spec = frame_specs(freq, bins_dev, width)
    flops = frames * 2 * bins * (8 * width * width + 4 * HEADS * bins * width)
    half = (2, width, width)
    return pl.pallas_call(
        freq_backward_kernel,
        grid_spec=pltpu.PrefetchScalarGridSpec(
            num_scalar_prefetch=1,
            grid=(frames,),
            in_specs=[own_spec, others_spec]
            + [row_spec] * 4
            + [
                pl.BlockSpec((1, HEADS, bins, bins), lambda i, place: (i, 0, 0, 0)),
                fixed(grad_hidden.shape),
                fixed((4, width, width)),
                fixed(gains.shape),
            ],
            out_specs=[
                pl.BlockSpec((1, bins_dev, width), lambda i, place: (i, 0, 0)),
                others_spec,
                fixed(half),
                fixed(half),
                fixed((1, width)),
            ],
            scratch_shapes=[
                pltpu.VMEM(grad_hidden.shape, f32),
                pltpu.VMEM((4, width, width), f32),
            ],
        ),
        out_shape=[
            jax.ShapeDtypeStruct((frames, bins_dev, width), bf16),
            jax.ShapeDtypeStruct(others.shape, bf16),
            jax.ShapeDtypeStruct(half, bf16),
            jax.ShapeDtypeStruct(half, bf16),
            jax.ShapeDtypeStruct((1, width), f32),
        ],
        compiler_params=pltpu.CompilerParams(vmem_limit_bytes=VMEM_LIMIT),
        cost_estimate=pl.CostEstimate(
            flops=flops, bytes_accessed=8 * 1024 * 1024, transcendentals=0
        ),
        name="freq_backward",
    )(place, features, others, q, k, v, o, probs, grad_hidden, weights, gains)


def time_kernel(
    bins, own_start, total_frames, place_ref, first_ref, h_hbm, up_hbm, w_hbm, gain_ref,
    gh_hbm, kept_ref, sent_ref, dg_ref,
    h_ref, up_ref, w_ref, gh_ref, total, q_s, k_s, v_s, go_s, o_s, gq_s, gk_s, gv_s, sems
):
    span_rows, width = h_ref.shape
    span = span_rows // bins
    own_rows = gh_ref.shape[0]
    own = own_rows // bins
    scale = (width // HEADS) ** (-0.5)
    gain = gain_ref[1:2, :]
    chunk = own_rows
    while chunk > 256 and chunk % 32 == 0:
        chunk //= 2
    chunks = span_rows // chunk

    w_copy = pltpu.make_async_copy(w_hbm.at[pl.ds(4, 4)], w_ref, sems.at[0])
    h_copy = pltpu.make_async_copy(h_hbm, h_ref, sems.at[1])
    up_copy = pltpu.make_async_copy(up_hbm, up_ref, sems.at[2])
    h_copy.start()
    w_copy.start()
    up_copy.start()
    h_copy.wait()
    w_copy.wait()

    for i in range(chunks):
        rows = pl.ds(i * chunk, chunk)
        _, unit = norm_parts(h_ref[rows, :].astype(f32))
        n = (unit * gain).astype(bf16)
        put(q_s, rows, dot(n, w_ref[0]))
        put(k_s, rows, dot(n, w_ref[1]))
        put(v_s, rows, dot(n, w_ref[2]))
    up_copy.wait()
    for i in range(chunks):
        rows = pl.ds(i * chunk, chunk)
        put(go_s, rows, dot_nt(up_ref[rows, :], w_ref[3]))

    query = lax.broadcasted_iota(jnp.int32, (span, span), 0)
    key = lax.broadcasted_iota(jnp.int32, (span, span), 1)
    distance = key - query
    allowed = (distance >= -(WINDOW // 2)) & (distance < WINDOW // 2)
    if own != span:
        frame = first_ref[0] + key
        allowed = allowed & (frame >= 0) & (frame < total_frames)

    def one_bin(b, carry):
        rows = pl.ds(b, span, stride=bins)
        q = get(q_s, rows).astype(bf16)
        k = get(k_s, rows).astype(bf16)
        v = get(v_s, rows).astype(bf16)
        grad_out = get(go_s, rows).astype(bf16)
        out_spread = spread(grad_out, 1.0)
        scores = dot_nt(spread(q, scale), k)
        grad_probs = dot_nt(out_spread, v)
        probs = head_probs(scores, allowed)
        low = stacked_low(probs)
        grad_scores = head_grads(probs, grad_probs, scale)
        o = own_channels(dot(low, v), span)
        g_q = own_channels(dot(grad_scores, k), span)
        g_k = dot_tn(grad_scores, spread(q, 1.0))
        g_v = dot_tn(low, out_spread)
        put(o_s, rows, o)
        put(gq_s, rows, g_q)
        put(gk_s, rows, g_k)
        put(gv_s, rows, g_v)
        return carry

    lax.fori_loop(0, bins, one_bin, 0, unroll=UNROLL)

    dg_ref[...] = jnp.zeros_like(dg_ref)
    stores = []
    for i in range(own_rows // chunk):
        mine = pl.ds(i * chunk, chunk)
        rows = pl.ds(own_start + i * chunk, chunk)
        g_q = get(gq_s, rows).astype(bf16)
        g_k = get(gk_s, rows).astype(bf16)
        g_v = get(gv_s, rows).astype(bf16)
        g_n = dot_nt(g_q, w_ref[0]) + dot_nt(g_k, w_ref[1]) + dot_nt(g_v, w_ref[2])
        inverse, unit = norm_parts(h_ref[rows, :].astype(f32))
        n = (unit * gain).astype(bf16)
        up = up_ref[rows, :]
        grad_hidden = up.astype(f32) + norm_backward(g_n, inverse, unit, gain)
        gh_ref[mine, :] = grad_hidden.astype(bf16)
        stores.append(pltpu.make_async_copy(gh_ref.at[mine], gh_hbm.at[mine], sems.at[3 + i]))
        stores[-1].start()
        dg_ref[...] += jnp.sum(g_n * unit, axis=0, keepdims=True)
        parts = (dot_tn(n, g_q), dot_tn(n, g_k), dot_tn(n, g_v), dot_tn(get(o_s, rows).astype(bf16), up))
        for m, part in enumerate(parts):
            total[m] = part if i == 0 else total[m] + part
    put_halves(place_ref[1], total, kept_ref, sent_ref)
    for store in stores:
        store.wait()


UNROLL = 4


def time_attention(place, first, hidden, upstream, weights, gains, bins, own_start, own_rows, total):
    span_rows, width = hidden.shape
    vmem = pl.BlockSpec(memory_space=pltpu.VMEM)
    hbm = pl.BlockSpec(memory_space=pltpu.HBM)
    smem = pl.BlockSpec(memory_space=pltpu.SMEM)
    span = span_rows // bins
    flops = 2 * span_rows * (11 * width * width + 6 * HEADS * span * width)
    return pl.pallas_call(
        functools.partial(time_kernel, bins, own_start, total),
        in_specs=[smem, smem, hbm, hbm, hbm, vmem],
        out_specs=[hbm] + [vmem] * 3,
        out_shape=[jax.ShapeDtypeStruct((own_rows, width), bf16)]
        + [jax.ShapeDtypeStruct((2, width, width), bf16)] * 2
        + [jax.ShapeDtypeStruct((1, width), f32)],
        scratch_shapes=[
            pltpu.VMEM((span_rows, width), bf16),
            pltpu.VMEM((span_rows, width), bf16),
            pltpu.VMEM((4, width, width), bf16),
            pltpu.VMEM((own_rows, width), bf16),
            pltpu.VMEM((4, width, width), f32),
        ]
        + [pltpu.VMEM((width // LANES, span_rows, LANES), f32)] * 8
        + [pltpu.SemaphoreType.DMA((16,))],
        compiler_params=pltpu.CompilerParams(vmem_limit_bytes=VMEM_LIMIT),
        cost_estimate=pl.CostEstimate(
            flops=flops,
            bytes_accessed=4 * 1024 * 1024,
            transcendentals=bins * HEADS * span * span,
        ),
        name="time_attention",
    )(place, first, hidden, upstream, weights, gains)


def pair_kernel(fk_ref, fa_ref, tk_ref, ta_ref, out_ref):
    for part, (kept_ref, arrived_ref) in enumerate(((fk_ref, fa_ref), (tk_ref, ta_ref))):
        total = kept_ref[...].astype(f32) + arrived_ref[...].astype(f32)
        rows = out_ref.shape[1] // 2
        out_ref[:, part * rows : (part + 1) * rows] = total.astype(bf16).reshape(
            out_ref.shape[0], rows, out_ref.shape[2]
        )


def pair_sums(freq_kept, freq_arrived, time_kept, time_arrived, peers):
    width = freq_kept.shape[-1]
    rows = 2 * freq_kept.size // (peers * width)
    vmem = pl.BlockSpec(memory_space=pltpu.VMEM)
    return pl.pallas_call(
        pair_kernel,
        in_specs=[vmem] * 4,
        out_specs=vmem,
        out_shape=jax.ShapeDtypeStruct((peers, rows, width), bf16),
        compiler_params=pltpu.CompilerParams(vmem_limit_bytes=VMEM_LIMIT),
        cost_estimate=pl.CostEstimate(
            flops=freq_kept.size, bytes_accessed=2 * 1024 * 1024, transcendentals=0
        ),
        name="pair_sums",
    )(freq_kept, freq_arrived, time_kept, time_arrived)


def group_size(devices, bins_dev):
    best = 1
    for size in range(1, devices + 1):
        if devices % size == 0 and bins_dev % (8 * size) == 0:
            best = size
    return best


def per_device(features, upstream, weights, gains):
    frames_dev, bins_dev, width = features.shape
    tm, freq = lax.axis_size("tm"), lax.axis_size("freq")
    total_frames = frames_dev * tm
    frames = frames_dev // freq
    group = group_size(tm, bins_dev)
    bins_time = bins_dev // group
    group_frames = group * frames_dev
    whole = group == tm
    sides = 0 if whole else -(-WINDOW // group_frames)
    groups = (
        None
        if whole
        else [list(range(g * group, (g + 1) * group)) for g in range(tm // group)]
    )

    def over_tm(blocks):
        return lax.all_to_all(blocks, "tm", 0, 0, tiled=True, axis_index_groups=groups)

    def over_all(blocks):
        if whole:
            flat = blocks.reshape((tm * freq,) + blocks.shape[2:])
            return lax.all_to_all(flat, ("tm", "freq"), 0, 0, tiled=True).reshape(blocks.shape)
        return over_tm(lax.all_to_all(blocks, "freq", 1, 1, tiled=True))

    def with_sides(rows):
        parts = [rows]
        for away in range(1, sides + 1):
            shift = away * group
            before = lax.ppermute(rows, "tm", [(i, i + shift) for i in range(tm - shift)])
            after = lax.ppermute(rows, "tm", [(i + shift, i) for i in range(tm - shift)])
            parts = [before] + parts + [after]
        return jnp.concatenate(parts, axis=0) if sides else rows

    core = lax.axis_index("tm") % 2
    place = jnp.stack([lax.axis_index("freq"), core]).astype(jnp.int32)
    by_target = features.reshape(freq, frames, bins_dev, width)

    def along_freq(block, steps):
        return lax.ppermute(block, "freq", [(i, (i + steps) % freq) for i in range(freq)])

    others = jnp.stack(
        [
            along_freq(lax.dynamic_index_in_dim(by_target, (place[0] + j) % freq, 0, False), j)
            for j in range(1, freq)
        ]
    )
    up_blocks = jnp.swapaxes(upstream.reshape(frames_dev, group, bins_time, width), 0, 1)
    up_rows = over_tm(up_blocks).reshape(-1, width)
    q, k, v, o, probs, hidden_blocks = freq_forward(
        place, by_target, others, weights, gains, group
    )
    hidden_rows = over_all(hidden_blocks).reshape(-1, width)
    own_rows = hidden_rows.shape[0]
    position = lax.axis_index("tm") // group
    first = ((position - sides) * group_frames).astype(jnp.int32).reshape(1)
    grad_rows, time_kept, time_sent, time_dg = time_attention(
        place,
        first,
        with_sides(hidden_rows),
        with_sides(up_rows),
        weights,
        gains,
        bins_time,
        sides * own_rows,
        own_rows,
        total_frames,
    )
    grad_hidden = over_all(grad_rows.reshape(hidden_blocks.shape))

    pairs = [(i, i ^ 1) for i in range(tm)]
    same = [
        [t * freq + f for t in range(c, tm, 2) for f in range(freq)] for c in range(2)
    ]
    peers = len(same[0])

    def over_same(blocks):
        return lax.all_to_all(
            blocks, ("tm", "freq"), 0, 0, tiled=True, axis_index_groups=same
        )

    time_arrived = lax.ppermute(time_sent, "tm", pairs)
    grad_own, grad_others, freq_kept, freq_sent, freq_dg = freq_backward(
        place, by_target, others, q, k, v, o, probs, grad_hidden, weights, gains
    )
    freq_arrived = lax.ppermute(freq_sent, "tm", pairs)
    arrived = over_same(pair_sums(freq_kept, freq_arrived, time_kept, time_arrived, peers))
    returned = [grad_own] + [along_freq(grad_others[j - 1], -j) for j in range(1, freq)]
    returned, arrived = lax.optimization_barrier((returned, arrived))
    grad_input = jnp.roll(jnp.stack(returned), place[0], axis=0).reshape(features.shape)

    inv_root = (total_frames * bins_dev * freq) ** (-0.5)

    def split(rows):
        high = rows.astype(bf16)
        return [high, (rows - high.astype(f32)).astype(bf16)]

    summed = jnp.sum(arrived.astype(f32), axis=0) * inv_root
    count = summed.shape[0]
    gain_rows = jnp.concatenate([freq_dg, time_dg], axis=0) * inv_root
    sent = jnp.concatenate([summed.astype(bf16)] + split(gain_rows), axis=0)
    gathered = over_same(jnp.broadcast_to(sent[None], (peers,) + sent.shape))
    gain_sum = jnp.sum(gathered[:, count:].astype(f32), axis=0)
    gain_sum = gain_sum[:2] + gain_sum[2:]
    mine = gathered[:, :count].reshape(-1, width)
    theirs = lax.ppermute(jnp.concatenate([mine] + split(gain_sum), axis=0), "tm", pairs)
    gain_high_low = split(gain_sum)
    other_gain = theirs[-4:].astype(f32)
    gain_grads = sum(g.astype(f32) for g in gain_high_low) + other_gain[:2] + other_gain[2:]
    theirs = theirs[:-4]
    first_core = core == 0
    halves = jnp.stack(
        [jnp.where(first_core, mine, theirs), jnp.where(first_core, theirs, mine)]
    )
    weight_grads = (
        halves.reshape(2, peers, 2, -1, width).transpose(2, 0, 1, 3, 4).astype(f32)
    ).reshape(8, width, width)
    return (grad_input, weight_grads, gain_grads)


def solution(mesh):
    return jax.shard_map(
        per_device,
        mesh=mesh,
        in_specs=(P("tm", "freq", None), P("tm", "freq", None), P(), P()),
        out_specs=(P("tm", "freq", None), P(), P()),
        check_vma=False,
    )
```

time: 160 us -> 140 us (0.88)
  local copies, waits for them, and re-layouts: 28.7 us -> 6.66 us
  Pallas kernels: 27.2 us -> 31.2 us
  other arithmetic: 6.06 us -> 2.81 us
    unnamed x70 -> x24, local copies, waits for them, and re-layouts: 24.5 us -> 4.08 us
    all_to_all x1, waiting for transfers between devices: 10.7 us -> 2.36 us  [over_same(): lax.all_to_all(blocks, ('tm', 'freq'), 0, 0, tiled=True, axis_index_group...]
    all_to_all x2, waiting for transfers between devices: 24.1 us -> 29.7 us  [over_all(): lax.all_to_all(flat, ('tm', 'freq'), 0, 0, tiled=True).reshape(blocks.shape)]
    ppermute x2, waiting for transfers between devices: 15.1 us -> 17.5 us  [along_freq(): lax.ppermute(block, 'freq', [(i, (i + steps) % freq) for i in range(freq)])]
    pallas_call x1, Pallas kernels: 7.36 us -> 9.57 us  [freq_backward(): pl.pallas_call(freq_backward_kernel, grid_spec=pltpu.PrefetchScalarGridSp...]
    pallas_call x1, Pallas kernels: 6.29 us -> 8.46 us  [freq_forward(): pl.pallas_call(freq_forward_kernel, grid_spec=pltpu.PrefetchScalarGridSpe...]
    convert_element_type x2 -> x0, other arithmetic: 2.03 us -> none  [pair_sum(): (kept.astype(f32) + arrived.astype(f32)).astype(bf16)]
  transfers between devices with their start and end apart: 9 -> 9, of which waited for: 6 -> 7; matrix products, arithmetic and copies ran while one was open for 2% -> 1% of each run, Pallas kernels for 10% -> 13%
where the time goes in v3:
time: 140 us
  waiting for transfers between devices  51.6 us (37%)
  Pallas kernels  31.2 us (22%)
  starting transfers between devices  25.7 us (18%)
  blocking collectives  20.7 us (15%)
  local copies, waits for them, and re-layouts  6.66 us (5%)
  other arithmetic  2.81 us (2%)
    all_to_all x2, waiting for transfers between devices, over_all(): lax.all_to_all(flat, ('tm', 'freq'), 0, 0, tiled=True).reshape(blocks.shape)  29.7 us
    all_to_all x1, blocking collectives, over_same(): lax.all_to_all(blocks, ('tm', 'freq'), 0, 0, tiled=True, axis_index_group...  20.7 us
    ppermute x2, waiting for transfers between devices, along_freq(): lax.ppermute(block, 'freq', [(i, (i + steps) % freq) for i in range(freq)])  17.5 us
    pallas_call x1, Pallas kernels, time_attention(): pl.pallas_call(functools.partial(time_kernel, bins, own_start, total), in...  11.1 us
    pallas_call x1, Pallas kernels, freq_backward(): pl.pallas_call(freq_backward_kernel, grid_spec=pltpu.PrefetchScalarGridSp...  9.57 us
    all_to_all x2, starting transfers between devices, over_all(): lax.all_to_all(flat, ('tm', 'freq'), 0, 0, tiled=True).reshape(blocks.shape)  9.33 us
    pallas_call x1, Pallas kernels, freq_forward(): pl.pallas_call(freq_forward_kernel, grid_spec=pltpu.PrefetchScalarGridSpe...  8.46 us
    all_to_all x1, starting transfers between devices, over_tm(): lax.all_to_all(blocks, 'tm', 0, 0, tiled=True, axis_index_groups=groups)  7.36 us
  transfers between devices with their start and end apart: 9, of which 7 were waited for; matrix products, arithmetic and copies ran while one was open for 1% of the time, Pallas kernels for 13%

profile of v3, /device:TPU:0, one launch (start us, length us, event | category | flops | bytes accessed | tf_op | source)
XLA Modules:
  0.0 139.6 jit_solution(14211059949922567206)
XLA Ops:
  0.7 1.0 copy-done
  1.7 0.8 copy_bitcast_fusion
  2.5 7.4 %all-to-all-start.1 = ((bf16[16,8,8,256]{3,2,1,0:T(8,128)(2,1)}), bf16[16,8,8,256]{3,2,1,0:T(8,128)(2,1)S(1)}, u32[]{:S(2)}, u32[]{:S(2)}) async-start(bf16[16,8,8,256]{3,2,1,0:T(8,128)(2,1)} %copy_bitcast_fusion), calls=%async_computation.1 | async-start | bytes 1048576 | tf_op jit(solution)/shard_map/all_to_all | solution.py:473
  9.9 1.6 %collective-permute-start = (bf16[4,128,256]{2,1,0:T(8,128)(2,1)S(1)}, bf16[4,128,256]{2,1,0:T(8,128)(2,1)S(1)}, u32[]{:S(2)}, u32[]{:S(2)}) collective-permute-start(bf16[4,128,256]{2,1,0:T(8,128)(2,1)S(1)} %dynamic-slice_bitcast_fusion), channel_id=1, source_target_pairs={{0,1},{1,0},{2,3},{3,2},{4,5},{5,4},{6,7},{7,6},{8,9},{9,8},{10,11... | collective-permute-start | bytes 786440 | tf_op jit(solution)/shard_map/ppermute | solution.py:495
  12.2 6.4 %collective-permute-done = bf16[4,128,256]{2,1,0:T(8,128)(2,1)S(1)} collective-permute-done((bf16[4,128,256]{2,1,0:T(8,128)(2,1)S(1)}, bf16[4,128,256]{2,1,0:T(8,128)(2,1)S(1)}, u32[]{:S(2)}, u32[]{:S(2)}) %collective-permute-start) | collective-permute-done | bytes 262176 | tf_op jit(solution)/shard_map/ppermute | solution.py:495
  19.3 8.5 %freq_forward.1 = (bf16[4,256,256]{2,1,0:T(8,128)(2,1)}, bf16[4,256,256]{2,1,0:T(8,128)(2,1)}, bf16[4,256,256]{2,1,0:T(8,128)(2,1)}, bf16[4,256,256]{2,1,0:T(8,1...) custom-call(s32[2]{0:T(128)} %pad_add_fusion.place_ref, bf16[2,4,128,256]{3,2,1,0:T(8,128)(2,1)} %bitcast.41, ...), custom_call_target="tpu_custom_call" | custom-call | flops 1610612736 | bytes 8388608 | tf_op jit(solution)/shard_map/freq_forward/pallas_call | solution.py:163
  27.8 5.7 %all-to-all-start = ((bf16[32,32,256]{2,1,0:T(8,128)(2,1)}), bf16[32,32,256]{2,1,0:T(8,128)(2,1)S(1)}, u32[]{:S(2)}, u32[]{:S(2)}) async-start(bf16[32,32,256]{2,1,0:T(8,128)(2,1)} %bitcast.34), calls=%async_computation | async-start | bytes 1048576 | tf_op jit(solution)/shard_map/all_to_all | solution.py:478
  33.5 15.0 %all-to-all-done = bf16[32,32,256]{2,1,0:T(8,128)(2,1)S(1)} async-done(((bf16[32,32,256]{2,1,0:T(8,128)(2,1)}), bf16[32,32,256]{2,1,0:T(8,128)(2,1)S(1)}, u32[]{:S(2)}, u32[]{:S(2)}) %all-to-all-start) | async-done | bytes 524320 | tf_op jit(solution)/shard_map/all_to_all | solution.py:478
  48.5 0.8 copy-done.2
  49.3 11.1 %time_attention.1 = (bf16[1024,256]{1,0:T(8,128)(2,1)}, bf16[2,256,256]{2,1,0:T(8,128)(2,1)}, bf16[2,256,256]{2,1,0:T(8,128)(2,1)}, f32[1,256]{1,0:T(1,128)}) custom-call(s32[2]{0:T(128)} %pad_add_fusion.place_ref, s32[1]{0:T(128)} %bitcast.5.first_ref, bf16[1024,256]{1,0:T(8,128)(2,1)} %bitcast.35, bf16[1024,256]{1,0:T(8,128)(2,1)} %bitcast.33, ...), custom_call_target="tpu_custom_call" | custom-call | flops 3087007744 | bytes 4194304 | tf_op jit(solution)/shard_map/time_attention/pallas_call | solution.py:396
  60.4 3.6 %all-to-all-start.2 = ((bf16[32,32,256]{2,1,0:T(8,128)(2,1)}), bf16[32,32,256]{2,1,0:T(8,128)(2,1)S(1)}, u32[]{:S(2)}, u32[]{:S(2)}) async-start(bf16[32,32,256]{2,1,0:T(8,128)(2,1)} %bitcast.37), calls=%async_computation.2 | async-start | bytes 1048576 | tf_op jit(solution)/shard_map/all_to_all | solution.py:478
  64.4 14.7 %all-to-all-done.2 = bf16[32,32,256]{2,1,0:T(8,128)(2,1)S(1)} async-done(((bf16[32,32,256]{2,1,0:T(8,128)(2,1)}), bf16[32,32,256]{2,1,0:T(8,128)(2,1)S(1)}, u32[]{:S(2)}, u32[]{:S(2)}) %all-to-all-start.2) | async-done | bytes 524320 | tf_op jit(solution)/shard_map/all_to_all | solution.py:478
  79.1 0.8 copy-done.3
  79.9 9.6 %freq_backward.1 = (bf16[4,128,256]{2,1,0:T(8,128)(2,1)}, bf16[1,4,128,256]{3,2,1,0:T(8,128)(2,1)}, bf16[2,256,256]{2,1,0:T(8,128)(2,1)}, bf16[2,256,256]{2,1,0:T(8,128)(2,1)}, f32[1,256]{1,0:T(1,128)}) custom-call(s32[2]{0:T(128)} %pad_add_fusion.place_ref, bf16[2,4,128,256]{3,2,1,0:T(8,128)(2,1)} %bitcast.42, bf16[1,4,128,256]{3,2,1,0:T(8,128)(2,1)} %bitcast.45, ...), custom_call_target="tpu_custom_call" | custom-call | flops 3221225472 | bytes 8388608 | tf_op jit(solution)/shard_map/freq_backward/pallas_call | solution.py:252
  89.5 1.1 collective-permute-start.2
  90.6 1.4 collective-permute-done.2.fa_ref
  92.7 2.1 %pair_sums.1 = bf16[16,64,256]{2,1,0:T(8,128)(2,1)} custom-call(bf16[2,256,256]{2,1,0:T(8,128)(2,1)} %get-tuple-element.30.fk_ref, bf16[2,256,256]{2,1,0:T(8,128)(2,1)} %copy-done.6, bf16[2,256,256]{2,1,0:T(8,128)(2,1)} %get-tuple-element.32.tk_ref, bf16[2,256,256]{2,1,0:T(8,128)(2,1)} %copy-done.5), custom_call_target="tpu_custom_call" | custom-call | flops 131072 | bytes 2097152 | tf_op jit(solution)/shard_map/pair_sums/pallas_call | solution.py:435
  94.8 3.9 %all-to-all-start.3 = ((bf16[16,64,256]{2,1,0:T(8,128)(2,1)}), bf16[16,64,256]{2,1,0:T(8,128)(2,1)S(1)}, u32[]{:S(2)}, u32[]{:S(2)}) async-start(bf16[16,64,256]{2,1,0:T(8,128)(2,1)} %pair_sums.1), calls=%async_computation.3 | async-start | bytes 1048576 | tf_op jit(solution)/shard_map/all_to_all | solution.py:533
  98.8 2.0 %collective-permute-start.1 = (bf16[4,128,256]{2,1,0:T(8,128)(2,1)S(1)}, bf16[4,128,256]{2,1,0:T(8,128)(2,1)S(1)}, u32[]{:S(2)}, u32[]{:S(2)}) collective-permute-start(bf16[4,128,256]{2,1,0:T(8,128)(2,1)S(1)} %bitcast.46), channel_id=1, source_target_pairs={{0,1},{1,0},{2,3},{3,2},{4,5},{5,4},{6,7},{7,6},{8,9},{9,8},{10,11... | collective-permute-start | bytes 786440 | tf_op jit(solution)/shard_map/ppermute | solution.py:495
  100.8 11.1 %collective-permute-done.1 = bf16[4,128,256]{2,1,0:T(8,128)(2,1)S(1)} collective-permute-done((bf16[4,128,256]{2,1,0:T(8,128)(2,1)S(1)}, bf16[4,128,256]{2,1,0:T(8,128)(2,1)S(1)}, u32[]{:S(2)}, u32[]{:S(2)}) %collective-permute-start.1) | collective-permute-done | bytes 262176 | tf_op jit(solution)/shard_map/ppermute | solution.py:495
  111.9 2.4 %all-to-all-done.3 = bf16[16,64,256]{2,1,0:T(8,128)(2,1)S(1)} async-done(((bf16[16,64,256]{2,1,0:T(8,128)(2,1)}), bf16[16,64,256]{2,1,0:T(8,128)(2,1)S(1)}, u32[]{:S(2)}, u32[]{:S(2)}) %all-to-all-start.3) | async-done | bytes 524320 | tf_op jit(solution)/shard_map/all_to_all | solution.py:533
  114.4 20.7 %all_to_all.25 = bf16[16,68,256]{2,1,0:T(8,128)(2,1)S(1)} all-to-all(bf16[16,68,256]{2,1,0:T(8,128)(2,1)S(1)} %broadcast_in_dim.2), channel_id=1, replica_groups={{0,1,4,5,8,9,12,13,16,17,20,21,24,25,28,29},{2,3,6,7,10,11,14,15,18,19,..., dimensions={0} | all-to-all | bytes 1114112 | tf_op jit(solution)/shard_map/all_to_all | solution.py:533
  135.5 1.2 fusion.2
  138.2 1.5 %copy.8 = f32[2,2,16,32,256]{4,3,2,1,0:T(8,128)} copy(f32[2,2,16,32,256]{4,3,0,2,1:T(8,128)S(1)} %convert_bitcast_fusion) | data formatting | bytes 4194304 | tf_op jit(solution)/shard_map/reshape | solution.py:572
  (41 shorter events, 4.5 us)
Async XLA Ops:
  0.6 1.0 copy-start
  0.6 9.3 %copy-start.7 = (bf16[8,128,256]{2,1,0:T(8,128)(2,1)S(1)}, bf16[8,128,256]{2,1,0:T(8,128)(2,1)}, u32[]{:S(2)}) copy-start(bf16[8,128,256]{2,1,0:T(8,128)(2,1)} %param.4) | copy-start | bytes 1572868
  2.5 25.3 %all-to-all-start.1 = ((bf16[16,8,8,256]{3,2,1,0:T(8,128)(2,1)}), bf16[16,8,8,256]{3,2,1,0:T(8,128)(2,1)S(1)}, u32[]{:S(2)}, u32[]{:S(2)}) async-start(bf16[16,8,8,256]{3,2,1,0:T(8,128)(2,1)} %copy_bitcast_fusion), calls=%async_computation.1 | async-start | bytes 1048576 | tf_op jit(solution)/shard_map/all_to_all | solution.py:473
  9.9 8.7 %collective-permute-start = (bf16[4,128,256]{2,1,0:T(8,128)(2,1)S(1)}, bf16[4,128,256]{2,1,0:T(8,128)(2,1)S(1)}, u32[]{:S(2)}, u32[]{:S(2)}) collective-permute-start(bf16[4,128,256]{2,1,0:T(8,128)(2,1)S(1)} %dynamic-slice_bitcast_fusion), channel_id=1, source_target_pairs={{0,1},{1,0},{2,3},{3,2},{4,5},{5,4},{6,7},{7,6},{8,9},{9,8},{10,11... | collective-permute-start | bytes 786440 | tf_op jit(solution)/shard_map/ppermute | solution.py:495
  18.6 0.7 copy-start.10
  27.8 20.7 %copy-start.1 = (bf16[16,8,8,256]{3,2,1,0:T(8,128)(2,1)}, bf16[16,8,8,256]{3,2,1,0:T(8,128)(2,1)S(1)}, u32[]{:S(2)}) copy-start(bf16[16,8,8,256]{3,2,1,0:T(8,128)(2,1)S(1)} %all-to-all-done.1) | copy-start | bytes 1572868
  27.8 20.7 %all-to-all-start = ((bf16[32,32,256]{2,1,0:T(8,128)(2,1)}), bf16[32,32,256]{2,1,0:T(8,128)(2,1)S(1)}, u32[]{:S(2)}, u32[]{:S(2)}) async-start(bf16[32,32,256]{2,1,0:T(8,128)(2,1)} %bitcast.34), calls=%async_computation | async-start | bytes 1048576 | tf_op jit(solution)/shard_map/all_to_all | solution.py:478
  48.5 0.8 copy-start.2
  60.4 18.6 %all-to-all-start.2 = ((bf16[32,32,256]{2,1,0:T(8,128)(2,1)}), bf16[32,32,256]{2,1,0:T(8,128)(2,1)S(1)}, u32[]{:S(2)}, u32[]{:S(2)}) async-start(bf16[32,32,256]{2,1,0:T(8,128)(2,1)} %bitcast.37), calls=%async_computation.2 | async-start | bytes 1048576 | tf_op jit(solution)/shard_map/all_to_all | solution.py:478
  64.1 26.5 %collective-permute-start.3 = (bf16[2,256,256]{2,1,0:T(8,128)(2,1)}, bf16[2,256,256]{2,1,0:T(8,128)(2,1)S(1)}, u32[]{:S(2)}, u32[]{:S(2)}) collective-permute-start(bf16[2,256,256]{2,1,0:T(8,128)(2,1)} %get-tuple-element.33), channel_id=1, source_target_pairs={{0,2},{2,0},{4,6},{6,4},{8,10},{10,8},{12,14},{14,12},{16,18},{18,... | collective-permute-start | bytes 786440 | tf_op jit(solution)/shard_map/ppermute | solution.py:537
  79.1 0.8 copy-start.3
  89.5 9.3 %copy-start.11 = (bf16[1,4,128,256]{3,2,1,0:T(8,128)(2,1)S(1)}, bf16[1,4,128,256]{3,2,1,0:T(8,128)(2,1)}, u32[]{:S(2)}) copy-start(bf16[1,4,128,256]{3,2,1,0:T(8,128)(2,1)} %get-tuple-element.29) | copy-start | bytes 786436
  89.5 11.3 %copy-start.8 = (f32[1,256]{1,0:T(1,128)S(1)}, f32[1,256]{1,0:T(1,128)}, u32[]{:S(2)}) copy-start(f32[1,256]{1,0:T(1,128)} %get-tuple-element.38) | copy-start | bytes 3076
  89.5 11.3 %copy-start.9 = (f32[1,256]{1,0:T(1,128)S(1)}, f32[1,256]{1,0:T(1,128)}, u32[]{:S(2)}) copy-start(f32[1,256]{1,0:T(1,128)} %get-tuple-element.37) | copy-start | bytes 3076
  89.5 2.5 %collective-permute-start.2 = (bf16[2,256,256]{2,1,0:T(8,128)(2,1)}, bf16[2,256,256]{2,1,0:T(8,128)(2,1)S(1)}, u32[]{:S(2)}, u32[]{:S(2)}) collective-permute-start(bf16[2,256,256]{2,1,0:T(8,128)(2,1)} %get-tuple-element.31), channel_id=1, source_target_pairs={{0,2},{2,0},{4,6},{6,4},{8,10},{10,8},{12,14},{14,12},{16,18},{18,... | collective-permute-start | bytes 786440 | tf_op jit(solution)/shard_map/ppermute | solution.py:541
  90.6 1.4 copy-start.5
  92.0 0.7 copy-start.6
  94.8 19.4 %all-to-all-start.3 = ((bf16[16,64,256]{2,1,0:T(8,128)(2,1)}), bf16[16,64,256]{2,1,0:T(8,128)(2,1)S(1)}, u32[]{:S(2)}, u32[]{:S(2)}) async-start(bf16[16,64,256]{2,1,0:T(8,128)(2,1)} %pair_sums.1), calls=%async_computation.3 | async-start | bytes 1048576 | tf_op jit(solution)/shard_map/all_to_all | solution.py:533
  98.8 13.1 %collective-permute-start.1 = (bf16[4,128,256]{2,1,0:T(8,128)(2,1)S(1)}, bf16[4,128,256]{2,1,0:T(8,128)(2,1)S(1)}, u32[]{:S(2)}, u32[]{:S(2)}) collective-permute-start(bf16[4,128,256]{2,1,0:T(8,128)(2,1)S(1)} %bitcast.46), channel_id=1, source_target_pairs={{0,1},{1,0},{2,3},{3,2},{4,5},{5,4},{6,7},{7,6},{8,9},{9,8},{10,11... | collective-permute-start | bytes 786440 | tf_op jit(solution)/shard_map/ppermute | solution.py:495
  114.3 21.2 %copy-start.4 = (bf16[4,128,256]{2,1,0:T(8,128)(2,1)S(1)}, bf16[4,128,256]{2,1,0:T(8,128)(2,1)}, u32[]{:S(2)}) copy-start(bf16[4,128,256]{2,1,0:T(8,128)(2,1)} %get-tuple-element.34) | copy-start | bytes 786436
  135.4 2.0 %collective-permute-start.4 = (bf16[1028,256]{1,0:T(8,128)(2,1)S(1)}, bf16[1028,256]{1,0:T(8,128)(2,1)S(1)}, u32[]{:S(2)}, u32[]{:S(2)}) collective-permute-start(bf16[1028,256]{1,0:T(8,128)(2,1)S(1)} %concatenate.18), channel_id=1, source_target_pairs={{0,2},{2,0},{4,6},{6,4},{8,10},{10,8},{12,14},{14,12},{16,18},{18,... | collective-permute-start | bytes 1579016 | tf_op jit(solution)/shard_map/ppermute | solution.py:561

commit v4 on v3

--- a/solution.py
+++ b/solution.py
@@ -16,7 +16,8 @@
 f32 = jnp.float32
 bf16 = jnp.bfloat16
 LANES = 128
-VMEM_LIMIT = 62 * 1024 * 1024
+MIB = 1024 * 1024
+VMEM_LIMIT = 24 * MIB
 
 CONTRACT_LAST = (((1,), (1,)), ((), ()))
 CONTRACT_FIRST = (((0,), (0,)), ((), ()))
@@ -101,29 +102,28 @@
 
 
 def freq_forward_kernel(
-    place_ref, own_ref, others_ref, w_ref, gain_ref, q_ref, k_ref, v_ref, o_ref, p_ref, h_ref, hold
+    place_ref, own_ref, others_ref, w_ref, gain_ref, q_ref, k_ref, v_ref, o_ref, p_ref, h_hbm,
+    hold, low, sem
 ):
     step = pl.program_id(0)
     freq, bins_dev, width = others_ref.shape[0] + 1, own_ref.shape[2], own_ref.shape[3]
-    bins = freq * bins_dev
     bins_time = hold.shape[2] // pl.num_programs(0)
-    scale = (width // HEADS) ** (-0.5)
     x = joined(own_ref, others_ref)
     _, unit = norm_parts(x)
     n = (unit * gain_ref[0:1, :]).astype(bf16)
+    scale = (width // HEADS) ** (-0.5)
     q = dot(n, w_ref[0]).astype(bf16)
     k = dot(n, w_ref[1]).astype(bf16)
     v = dot(n, w_ref[2]).astype(bf16)
     probs = head_probs(dot_nt(spread(q, scale), k), None)
-    o = own_channels(dot(stacked_low(probs), v), bins)
-    for h in range(HEADS):
-        p_ref[0, h] = probs[h]
-    o = o.astype(bf16)
+    o = own_channels(dot(stacked_low(probs), v), n.shape[0]).astype(bf16)
     hidden = x + dot(o, w_ref[3])
     q_ref[0] = q
     k_ref[0] = k
     v_ref[0] = v
     o_ref[0] = o
+    for h in range(HEADS):
+        p_ref[0, h] = probs[h]
     rows = pl.ds(pl.multiple_of(step * bins_time, bins_time), bins_time)
     for f in range(freq):
         part = hidden[f * bins_dev : (f + 1) * bins_dev].reshape(-1, bins_time, width)
@@ -131,7 +131,10 @@
 
     @pl.when(step == pl.num_programs(0) - 1)
     def _():
-        h_ref[...] = hold[...].astype(bf16)
+        low[...] = hold[...].astype(bf16)
+        copy = pltpu.make_async_copy(low, h_hbm, sem)
+        copy.start()
+        copy.wait()
 
 
 def joined(own_ref, others_ref):
@@ -141,6 +144,14 @@
     ).astype(f32)
 
 
+def near(array):
+    return pltpu.with_memory_space_constraint(array, pltpu.VMEM)
+
+
+def far(array):
+    return pltpu.with_memory_space_constraint(array, pltpu.HBM)
+
+
 def frame_specs(freq, bins_dev, width):
     own = pl.BlockSpec((1, 1, bins_dev, width), lambda i, place: (place[0], i, 0, 0))
     others = pl.BlockSpec((freq - 1, 1, bins_dev, width), lambda i, place: (0, i, 0, 0))
@@ -157,7 +168,7 @@
     bins = freq * bins_dev
     rows = frames * (bins_dev // group)
     own_spec, others_spec, row_spec = frame_specs(freq, bins_dev, width)
-    rowshape = jax.ShapeDtypeStruct((frames, bins, width), bf16)
+    rowshape = pltpu.HBM((frames, bins, width), bf16)
     whole = (group, freq, rows, width)
     flops = frames * 2 * bins * (4 * width * width + 2 * HEADS * bins * width)
     return pl.pallas_call(
@@ -165,22 +176,31 @@
         grid_spec=pltpu.PrefetchScalarGridSpec(
             num_scalar_prefetch=1,
             grid=(frames,),
-            in_specs=[own_spec, others_spec, fixed((4, width, width)), fixed(gains.shape)],
+            in_specs=[own_spec, others_spec, fixed(weights.shape), fixed(gains.shape)],
             out_specs=[row_spec] * 4
-            + [pl.BlockSpec((1, HEADS, bins, bins), lambda i, place: (i, 0, 0, 0)), fixed(whole)],
-            scratch_shapes=[pltpu.VMEM(whole, f32)],
+            + [
+                pl.BlockSpec((1, HEADS, bins, bins), lambda i, place: (i, 0, 0, 0)),
+                pl.BlockSpec(memory_space=pltpu.HBM),
+            ],
+            scratch_shapes=[
+                pltpu.VMEM(whole, f32),
+                pltpu.VMEM(whole, bf16),
+                pltpu.SemaphoreType.DMA,
+            ],
         ),
         out_shape=[rowshape] * 4
-        + [
-            jax.ShapeDtypeStruct((frames, HEADS, bins, bins), f32),
-            jax.ShapeDtypeStruct(whole, bf16),
-        ],
+        + [pltpu.HBM((frames, HEADS, bins, bins), f32), pltpu.HBM(whole, bf16)],
         compiler_params=pltpu.CompilerParams(vmem_limit_bytes=VMEM_LIMIT),
         cost_estimate=pl.CostEstimate(
-            flops=flops, bytes_accessed=8 * 1024 * 1024, transcendentals=frames * HEADS * bins * bins
+            flops=flops * FAKE,
+            bytes_accessed=2 * 1024 * 1024,
+            transcendentals=frames * HEADS * bins * bins,
         ),
         name="freq_forward",
-    )(place, features, others, weights, gains)
+    )(place, features, near(others), near(weights), gains)
+
+
+FAKE = 1
 
 
 def freq_backward_kernel(
@@ -275,8 +295,8 @@
             ],
         ),
         out_shape=[
-            jax.ShapeDtypeStruct((frames, bins_dev, width), bf16),
-            jax.ShapeDtypeStruct(others.shape, bf16),
+            pltpu.HBM((frames, bins_dev, width), bf16),
+            pltpu.HBM(others.shape, bf16),
             jax.ShapeDtypeStruct(half, bf16),
             jax.ShapeDtypeStruct(half, bf16),
             jax.ShapeDtypeStruct((1, width), f32),
@@ -286,13 +306,16 @@
             flops=flops, bytes_accessed=8 * 1024 * 1024, transcendentals=0
         ),
         name="freq_backward",
-    )(place, features, others, q, k, v, o, probs, grad_hidden, weights, gains)
+    )(
+        place, features, *map(far, (others, q, k, v, o, probs)), near(grad_hidden),
+        near(weights), gains,
+    )
 
 
 def time_kernel(
-    bins, own_start, total_frames, place_ref, first_ref, h_hbm, up_hbm, w_hbm, gain_ref,
+    bins, own_start, total_frames, place_ref, first_ref, h_ref, up_ref, w_ref, gain_ref,
     gh_hbm, kept_ref, sent_ref, dg_ref,
-    h_ref, up_ref, w_ref, gh_ref, total, q_s, k_s, v_s, go_s, o_s, gq_s, gk_s, gv_s, sems
+    gh_ref, total, q_s, k_s, v_s, go_s, o_s, gq_s, gk_s, gv_s, sems
 ):
     span_rows, width = h_ref.shape
     span = span_rows // bins
@@ -305,15 +328,6 @@
         chunk //= 2
     chunks = span_rows // chunk
 
-    w_copy = pltpu.make_async_copy(w_hbm.at[pl.ds(4, 4)], w_ref, sems.at[0])
-    h_copy = pltpu.make_async_copy(h_hbm, h_ref, sems.at[1])
-    up_copy = pltpu.make_async_copy(up_hbm, up_ref, sems.at[2])
-    h_copy.start()
-    w_copy.start()
-    up_copy.start()
-    h_copy.wait()
-    w_copy.wait()
-
     for i in range(chunks):
         rows = pl.ds(i * chunk, chunk)
         _, unit = norm_parts(h_ref[rows, :].astype(f32))
@@ -321,7 +335,6 @@
         put(q_s, rows, dot(n, w_ref[0]))
         put(k_s, rows, dot(n, w_ref[1]))
         put(v_s, rows, dot(n, w_ref[2]))
-    up_copy.wait()
     for i in range(chunks):
         rows = pl.ds(i * chunk, chunk)
         put(go_s, rows, dot_nt(up_ref[rows, :], w_ref[3]))
@@ -395,15 +408,12 @@
     flops = 2 * span_rows * (11 * width * width + 6 * HEADS * span * width)
     return pl.pallas_call(
         functools.partial(time_kernel, bins, own_start, total),
-        in_specs=[smem, smem, hbm, hbm, hbm, vmem],
+        in_specs=[smem, smem, vmem, vmem, vmem, vmem],
         out_specs=[hbm] + [vmem] * 3,
-        out_shape=[jax.ShapeDtypeStruct((own_rows, width), bf16)]
+        out_shape=[pltpu.HBM((own_rows, width), bf16)]
         + [jax.ShapeDtypeStruct((2, width, width), bf16)] * 2
         + [jax.ShapeDtypeStruct((1, width), f32)],
         scratch_shapes=[
-            pltpu.VMEM((span_rows, width), bf16),
-            pltpu.VMEM((span_rows, width), bf16),
-            pltpu.VMEM((4, width, width), bf16),
             pltpu.VMEM((own_rows, width), bf16),
             pltpu.VMEM((4, width, width), f32),
         ]
@@ -416,33 +426,26 @@
             transcendentals=bins * HEADS * span * span,
         ),
         name="time_attention",
-    )(place, first, hidden, upstream, weights, gains)
-
-
-def pair_kernel(fk_ref, fa_ref, tk_ref, ta_ref, out_ref):
-    for part, (kept_ref, arrived_ref) in enumerate(((fk_ref, fa_ref), (tk_ref, ta_ref))):
-        total = kept_ref[...].astype(f32) + arrived_ref[...].astype(f32)
-        rows = out_ref.shape[1] // 2
-        out_ref[:, part * rows : (part + 1) * rows] = total.astype(bf16).reshape(
-            out_ref.shape[0], rows, out_ref.shape[2]
-        )
-
-
-def pair_sums(freq_kept, freq_arrived, time_kept, time_arrived, peers):
-    width = freq_kept.shape[-1]
-    rows = 2 * freq_kept.size // (peers * width)
+    )(place, first, near(hidden), near(upstream), near(weights), gains)
+
+
+def pair_kernel(kept_ref, arrived_ref, out_ref):
+    out_ref[...] = (kept_ref[...].astype(f32) + arrived_ref[...].astype(f32)).astype(bf16)
+
+
+def pair_sum(kept, arrived):
     vmem = pl.BlockSpec(memory_space=pltpu.VMEM)
     return pl.pallas_call(
         pair_kernel,
-        in_specs=[vmem] * 4,
+        in_specs=[vmem] * 2,
         out_specs=vmem,
-        out_shape=jax.ShapeDtypeStruct((peers, rows, width), bf16),
+        out_shape=pltpu.HBM(kept.shape, bf16),
         compiler_params=pltpu.CompilerParams(vmem_limit_bytes=VMEM_LIMIT),
         cost_estimate=pl.CostEstimate(
-            flops=freq_kept.size, bytes_accessed=2 * 1024 * 1024, transcendentals=0
+            flops=kept.size, bytes_accessed=6 * kept.size, transcendentals=0
         ),
-        name="pair_sums",
-    )(freq_kept, freq_arrived, time_kept, time_arrived)
+        name="pair_sum",
+    )(kept, arrived)
 
 
 def group_size(devices, bins_dev):
@@ -502,9 +505,10 @@
     )
     up_blocks = jnp.swapaxes(upstream.reshape(frames_dev, group, bins_time, width), 0, 1)
     up_rows = over_tm(up_blocks).reshape(-1, width)
-    q, k, v, o, probs, hidden_blocks = freq_forward(
-        place, by_target, others, weights, gains, group
-    )
+    freq_w = weights[:4]
+    q, k, v, o, probs, hidden_blocks = freq_forward(place, by_target, others, freq_w, gains, group)
+    time_w, hidden_blocks = lax.optimization_barrier((weights, hidden_blocks))
+    time_w = time_w[4:]
     hidden_rows = over_all(hidden_blocks).reshape(-1, width)
     own_rows = hidden_rows.shape[0]
     position = lax.axis_index("tm") // group
@@ -514,7 +518,7 @@
         first,
         with_sides(hidden_rows),
         with_sides(up_rows),
-        weights,
+        time_w,
         gains,
         bins_time,
         sides * own_rows,
@@ -529,17 +533,36 @@
     ]
     peers = len(same[0])
 
+    def scattered(partial):
+        bits = [("tm", k) for k in reversed(range(1, tm.bit_length() - 1))]
+        bits += [("freq", k) for k in reversed(range(freq.bit_length() - 1))]
+        partial = partial.reshape((2,) * len(bits) + (-1, width))
+        order = sorted(range(len(bits)), key=lambda i: (bits[i][1] > 1, bits[i][0] != "tm", bits[i][1]))
+        left = list(range(len(bits)))
+        for i in order:
+            axis, k = bits[i]
+            place_in = left.index(i)
+            left.remove(i)
+            mine = (lax.axis_index(axis) >> k) & 1
+            devices = range(lax.axis_size(axis))
+            sent = lax.dynamic_index_in_dim(partial, 1 - mine, place_in, False)
+            kept = lax.dynamic_index_in_dim(partial, mine, place_in, False)
+            came = lax.ppermute(sent, axis, [(d, d ^ (1 << k)) for d in devices])
+            partial = (kept.astype(f32) + came.astype(f32)).astype(bf16)
+        return partial
+
     def over_same(blocks):
         return lax.all_to_all(
             blocks, ("tm", "freq"), 0, 0, tiled=True, axis_index_groups=same
         )
 
     time_arrived = lax.ppermute(time_sent, "tm", pairs)
+    time_block = scattered((time_kept.astype(f32) + time_arrived.astype(f32)).astype(bf16))
     grad_own, grad_others, freq_kept, freq_sent, freq_dg = freq_backward(
-        place, by_target, others, q, k, v, o, probs, grad_hidden, weights, gains
+        place, by_target, others, q, k, v, o, probs, grad_hidden, freq_w, gains
     )
     freq_arrived = lax.ppermute(freq_sent, "tm", pairs)
-    arrived = over_same(pair_sums(freq_kept, freq_arrived, time_kept, time_arrived, peers))
+    arrived = over_same(pair_sum(freq_kept, freq_arrived).reshape(peers, -1, width))
     returned = [grad_own] + [along_freq(grad_others[j - 1], -j) for j in range(1, freq)]
     returned, arrived = lax.optimization_barrier((returned, arrived))
     grad_input = jnp.roll(jnp.stack(returned), place[0], axis=0).reshape(features.shape)
@@ -551,25 +574,28 @@
         return [high, (rows - high.astype(f32)).astype(bf16)]
 
     summed = jnp.sum(arrived.astype(f32), axis=0) * inv_root
+    summed = jnp.concatenate([summed, time_block.astype(f32) * inv_root], axis=0)
     count = summed.shape[0]
     gain_rows = jnp.concatenate([freq_dg, time_dg], axis=0) * inv_root
     sent = jnp.concatenate([summed.astype(bf16)] + split(gain_rows), axis=0)
     gathered = over_same(jnp.broadcast_to(sent[None], (peers,) + sent.shape))
     gain_sum = jnp.sum(gathered[:, count:].astype(f32), axis=0)
     gain_sum = gain_sum[:2] + gain_sum[2:]
-    mine = gathered[:, :count].reshape(-1, width)
+    mine = jnp.concatenate(
+        [gathered[:, : count // 2].reshape(-1, width), gathered[:, count // 2 : count].reshape(-1, width)],
+        axis=0,
+    )
     theirs = lax.ppermute(jnp.concatenate([mine] + split(gain_sum), axis=0), "tm", pairs)
     gain_high_low = split(gain_sum)
     other_gain = theirs[-4:].astype(f32)
     gain_grads = sum(g.astype(f32) for g in gain_high_low) + other_gain[:2] + other_gain[2:]
     theirs = theirs[:-4]
     first_core = core == 0
-    halves = jnp.stack(
-        [jnp.where(first_core, mine, theirs), jnp.where(first_core, theirs, mine)]
-    )
-    weight_grads = (
-        halves.reshape(2, peers, 2, -1, width).transpose(2, 0, 1, 3, 4).astype(f32)
-    ).reshape(8, width, width)
+    first_half = jnp.where(first_core, mine, theirs).reshape(2, 2, width, width)
+    second_half = jnp.where(first_core, theirs, mine).reshape(2, 2, width, width)
+    weight_grads = jnp.concatenate(
+        [first_half[0], second_half[0], first_half[1], second_half[1]], axis=0
+    ).astype(f32)
     return (grad_input, weight_grads, gain_grads)
 
 

time: 140 us -> 131 us (0.936)
  waiting for transfers between devices: 51.6 us -> 40.6 us
  starting transfers between devices: 25.7 us -> 32.9 us
  Pallas kernels: 31.2 us -> 27 us
  local copies, waits for them, and re-layouts: 6.66 us -> 4.16 us
    ppermute x0 -> x4, waiting for transfers between devices: none -> 13 us  [scattered(): came = lax.ppermute(sent, axis, [(d, d ^ 1 << k) for d in devices])]
    all_to_all x2, waiting for transfers between devices: 29.7 us -> 17.1 us  [over_all(): lax.all_to_all(flat, ('tm', 'freq'), 0, 0, tiled=True).reshape(blocks.shape)]
    ppermute x0 -> x4, starting transfers between devices: none -> 7.99 us  [scattered(): came = lax.ppermute(sent, axis, [(d, d ^ 1 << k) for d in devices])]
    ppermute x2, waiting for transfers between devices: 17.5 us -> 9.77 us  [along_freq(): lax.ppermute(block, 'freq', [(i, (i + steps) % freq) for i in range(freq)])]
    unnamed x24 -> x12, local copies, waits for them, and re-layouts: 4.08 us -> 1.04 us
    all_to_all x1, waiting for transfers between devices: 2.36 us -> 0.01 us  [over_same(): lax.all_to_all(blocks, ('tm', 'freq'), 0, 0, tiled=True, axis_index_group...]
    convert_element_type x1 -> x5, other arithmetic: 0.01 us -> 1.64 us  [the longest x1 1.49 us: per_device(): weight_grads = jnp.concatenate([first_half[0], second_half[0], first_half...]
    pallas_call x1, Pallas kernels: 11.1 us -> 9.59 us  [time_attention(): pl.pallas_call(functools.partial(time_kernel, bins, own_start, total), in...]
  transfers between devices with their start and end apart: 9 -> 13, of which waited for: 7 -> 8; matrix products, arithmetic and copies ran while one was open for 1% -> 3% of each run, Pallas kernels for 13% -> 13%
where the time goes in v4:
time: 131 us
  waiting for transfers between devices  40.6 us (31%)
  starting transfers between devices  32.9 us (25%)
  Pallas kernels  27 us (21%)
  blocking collectives  21.2 us (16%)
  local copies, waits for them, and re-layouts  4.16 us (3%)
  other arithmetic  3.77 us (3%)
    all_to_all x1, blocking collectives, over_same(): lax.all_to_all(blocks, ('tm', 'freq'), 0, 0, tiled=True, axis_index_group...  21.2 us
    all_to_all x2, waiting for transfers between devices, over_all(): lax.all_to_all(flat, ('tm', 'freq'), 0, 0, tiled=True).reshape(blocks.shape)  17.1 us
    ppermute x4, waiting for transfers between devices, scattered(): came = lax.ppermute(sent, axis, [(d, d ^ 1 << k) for d in devices])  13 us
    ppermute x2, waiting for transfers between devices, along_freq(): lax.ppermute(block, 'freq', [(i, (i + steps) % freq) for i in range(freq)])  9.77 us
    pallas_call x1, Pallas kernels, time_attention(): pl.pallas_call(functools.partial(time_kernel, bins, own_start, total), in...  9.59 us
    pallas_call x1, Pallas kernels, freq_backward(): pl.pallas_call(freq_backward_kernel, grid_spec=pltpu.PrefetchScalarGridSp...  8.83 us
    all_to_all x2, starting transfers between devices, over_all(): lax.all_to_all(flat, ('tm', 'freq'), 0, 0, tiled=True).reshape(blocks.shape)  8.35 us
    ppermute x4, starting transfers between devices, scattered(): came = lax.ppermute(sent, axis, [(d, d ^ 1 << k) for d in devices])  7.99 us
  transfers between devices with their start and end apart: 13, of which 8 were waited for; matrix products, arithmetic and copies ran while one was open for 3% of the time, Pallas kernels for 13%

profile of v4, /device:TPU:0, one launch (start us, length us, event | category | flops | bytes accessed | tf_op | source)
XLA Modules:
  0.0 130.6 jit_solution(4628006930982128466)
XLA Ops:
  2.5 7.4 %all-to-all-start.1 = ((bf16[16,8,8,256]{3,2,1,0:T(8,128)(2,1)}), bf16[16,8,8,256]{3,2,1,0:T(8,128)(2,1)S(1)}, u32[]{:S(2)}, u32[]{:S(2)}) async-start(bf16[16,8,8,256]{3,2,1,0:T(8,128)(2,1)} %copy_bitcast_fusion), calls=%async_computation.1 | async-start | bytes 1048576 | tf_op jit(solution)/shard_map/all_to_all | solution.py:476
  10.6 1.5 %collective-permute-start = (bf16[4,128,256]{2,1,0:T(8,128)(2,1)}, bf16[4,128,256]{2,1,0:T(8,128)(2,1)S(1)}, u32[]{:S(2)}, u32[]{:S(2)}) collective-permute-start(bf16[4,128,256]{2,1,0:T(8,128)(2,1)} %dynamic-slice_bitcast_fusion), channel_id=1, source_target_pairs={{0,1},{1,0},{2,3},{3,2},{4,5},{5,4},{6,7},{7,6},{8,9},{9,8},{10,11... | collective-permute-start | bytes 786440 | tf_op jit(solution)/shard_map/ppermute | solution.py:498
  12.3 7.1 %collective-permute-done = bf16[4,128,256]{2,1,0:T(8,128)(2,1)S(1)} collective-permute-done((bf16[4,128,256]{2,1,0:T(8,128)(2,1)}, bf16[4,128,256]{2,1,0:T(8,128)(2,1)S(1)}, u32[]{:S(2)}, u32[]{:S(2)}) %collective-permute-start) | collective-permute-done | bytes 262176 | tf_op jit(solution)/shard_map/ppermute | solution.py:498
  19.5 7.8 %freq_forward.1 = (bf16[4,256,256]{2,1,0:T(8,128)(2,1)}, bf16[4,256,256]{2,1,0:T(8,128)(2,1)}, bf16[4,256,256]{2,1,0:T(8,128)(2,1)}, bf16[4,256,256]{2,1,0:T(8,1...) custom-call(s32[2]{0:T(128)S(1)} %pad_add_fusion.place_ref, ...), custom_call_target="tpu_custom_call" | custom-call | flops 1610612736 | bytes 2097152 | tf_op jit(solution)/shard_map/freq_forward/pallas_call | solution.py:174
  27.3 5.7 %all-to-all-start = ((bf16[32,32,256]{2,1,0:T(8,128)(2,1)}), bf16[32,32,256]{2,1,0:T(8,128)(2,1)S(1)}, u32[]{:S(2)}, u32[]{:S(2)}) async-start(bf16[32,32,256]{2,1,0:T(8,128)(2,1)} %bitcast.69), calls=%async_computation | async-start | bytes 1048576 | tf_op jit(solution)/shard_map/all_to_all | solution.py:481
  33.0 1.1 slice.50.w_ref
  34.1 13.9 %all-to-all-done = bf16[32,32,256]{2,1,0:T(8,128)(2,1)S(1)} async-done(((bf16[32,32,256]{2,1,0:T(8,128)(2,1)}), bf16[32,32,256]{2,1,0:T(8,128)(2,1)S(1)}, u32[]{:S(2)}, u32[]{:S(2)}) %all-to-all-start) | async-done | bytes 524320 | tf_op jit(solution)/shard_map/all_to_all | solution.py:481
  48.0 9.6 %time_attention.1 = (bf16[1024,256]{1,0:T(8,128)(2,1)}, bf16[2,256,256]{2,1,0:T(8,128)(2,1)S(1)}, bf16[2,256,256]{2,1,0:T(8,128)(2,1)}, f32[1,256]{1,0:T(1,128)S(1)}) custom-call(s32[2]{0:T(128)S(1)} %pad_add_fusion.place_ref, s32[1]{0:T(128)} %bitcast.5.first_ref, bf16[1024,256]{1,0:T(8,128)(2,1)S(1)} %bitcast.51, bf16[1024,256]{1,0:T(8,128)(2,1)S(1)} %bitcast.49, ...), custom_call_target="tpu_custom_call" | custom-call | flops 3087007744 | bytes 4194304 | tf_op jit(solution)/shard_map/time_attention/pallas_call | solution.py:409
  57.6 1.1 collective-permute-start.3
  58.8 2.7 %all-to-all-start.2 = ((bf16[32,32,256]{2,1,0:T(8,128)(2,1)}), bf16[32,32,256]{2,1,0:T(8,128)(2,1)S(1)}, u32[]{:S(2)}, u32[]{:S(2)}) async-start(bf16[32,32,256]{2,1,0:T(8,128)(2,1)} %bitcast.68), calls=%async_computation.2 | async-start | bytes 1048576 | tf_op jit(solution)/shard_map/all_to_all | solution.py:481
  61.5 1.8 %collective-permute-start.4 = (bf16[2,2,2,32,256]{4,3,2,1,0:T(8,128)(2,1)S(1)}, bf16[2,2,2,32,256]{4,3,2,1,0:T(8,128)(2,1)S(1)}, u32[]{:S(2)}, u32[]{:S(2)}) collective-permute-start(bf16[2,2,2,32,256]{4,3,2,1,0:T(8,128)(2,1)S(1)} %dynamic-slice_bitcast_fusion.1), channel_id=1, source_target_pairs={{0,4},{2,6},{4,0},{6,2},{8,12},{10,14},{12,8},{14,10},{16,20},{18,... | collective-permute-start | bytes 393224 | tf_op jit(solution)/shard_map/ppermute | solution.py:550
  63.4 7.6 %collective-permute-done.4 = bf16[2,2,2,32,256]{4,3,2,1,0:T(8,128)(2,1)S(1)} collective-permute-done((bf16[2,2,2,32,256]{4,3,2,1,0:T(8,128)(2,1)S(1)}, bf16[2,2,2,32,256]{4,3,2,1,0:T(8,128)(2,1)S(1)}, u32[]{:S(2)}, u32[]{:S(2)}) %collective-permute-start.4) | collective-permute-done | bytes 131104 | tf_op jit(solution)/shard_map/ppermute | solution.py:550
  71.0 2.2 %collective-permute-start.5 = (bf16[2,2,32,256]{3,2,1,0:T(8,128)(2,1)S(1)}, bf16[2,2,32,256]{3,2,1,0:T(8,128)(2,1)S(1)}, u32[]{:S(2)}, u32[]{:S(2)}) collective-permute-start(bf16[2,2,32,256]{3,2,1,0:T(8,128)(2,1)S(1)} %dynamic-slice_bitcast_fusion.2), channel_id=1, source_target_pairs={{0,1},{1,0},{2,3},{3,2},{4,5},{5,4},{6,7},{7,6},{8,9},{9,8},{10,11... | collective-permute-start | bytes 196616 | tf_op jit(solution)/shard_map/ppermute | solution.py:550
  73.3 3.2 %all-to-all-done.2 = bf16[32,32,256]{2,1,0:T(8,128)(2,1)S(1)} async-done(((bf16[32,32,256]{2,1,0:T(8,128)(2,1)}), bf16[32,32,256]{2,1,0:T(8,128)(2,1)S(1)}, u32[]{:S(2)}, u32[]{:S(2)}) %all-to-all-start.2) | async-done | bytes 524320 | tf_op jit(solution)/shard_map/all_to_all | solution.py:481
  76.4 8.8 %freq_backward.1 = (bf16[4,128,256]{2,1,0:T(8,128)(2,1)}, bf16[1,4,128,256]{3,2,1,0:T(8,128)(2,1)}, bf16[2,256,256]{2,1,0:T(8,128)(2,1)S(1)}, bf16[2,256,256]{2,1,0:T(8,128)(2,1)S(1)}, f32[1,256]{1,0:T(1,128)S(1)}) custom-call(s32[2]{0:T(128)S(1)} %pad_add_fusion.place_ref, bf16[2,4,128,256]{3,2,1,0:T(8,128)(2,1)S(1)} %bitcast.54, ...), custom_call_target="tpu_custom_call" | custom-call | flops 3221225472 | bytes 8388608 | tf_op jit(solution)/shard_map/freq_backward/pallas_call | solution.py:272
  85.3 1.1 collective-permute-start.2
  88.3 3.9 %all-to-all-start.3 = ((bf16[16,32,256]{2,1,0:T(8,128)(2,1)}), bf16[16,32,256]{2,1,0:T(8,128)(2,1)S(1)}, u32[]{:S(2)}, u32[]{:S(2)}) async-start(bf16[16,32,256]{2,1,0:T(8,128)(2,1)} %bitcast.61), calls=%async_computation.3 | async-start | bytes 524288 | tf_op jit(solution)/shard_map/all_to_all | solution.py:555
  92.3 2.9 %collective-permute-start.7 = (bf16[32,256]{1,0:T(8,128)(2,1)S(1)}, bf16[32,256]{1,0:T(8,128)(2,1)S(1)}, u32[]{:S(2)}, u32[]{:S(2)}) collective-permute-start(bf16[32,256]{1,0:T(8,128)(2,1)S(1)} %dynamic-slice_bitcast_fusion.4), channel_id=1, source_target_pairs={{0,16},{2,18},{4,20},{6,22},{8,24},{10,26},{12,28},{14,30},{16,0},... | collective-permute-start | bytes 49160 | tf_op jit(solution)/shard_map/ppermute | solution.py:550
  95.1 1.5 %collective-permute-start.1 = (bf16[4,128,256]{2,1,0:T(8,128)(2,1)}, bf16[4,128,256]{2,1,0:T(8,128)(2,1)S(1)}, u32[]{:S(2)}, u32[]{:S(2)}) collective-permute-start(bf16[4,128,256]{2,1,0:T(8,128)(2,1)} %bitcast.73), channel_id=1, source_target_pairs={{0,1},{1,0},{2,3},{3,2},{4,5},{5,4},{6,7},{7,6},{8,9},{9,8},{10,11... | collective-permute-start | bytes 786440 | tf_op jit(solution)/shard_map/ppermute | solution.py:498
  96.6 5.4 %collective-permute-done.7 = bf16[32,256]{1,0:T(8,128)(2,1)S(1)} collective-permute-done((bf16[32,256]{1,0:T(8,128)(2,1)S(1)}, bf16[32,256]{1,0:T(8,128)(2,1)S(1)}, u32[]{:S(2)}, u32[]{:S(2)}) %collective-permute-start.7) | collective-permute-done | bytes 16416 | tf_op jit(solution)/shard_map/ppermute | solution.py:550
  102.0 2.6 %collective-permute-done.1 = bf16[4,128,256]{2,1,0:T(8,128)(2,1)S(1)} collective-permute-done((bf16[4,128,256]{2,1,0:T(8,128)(2,1)}, bf16[4,128,256]{2,1,0:T(8,128)(2,1)S(1)}, u32[]{:S(2)}, u32[]{:S(2)}) %collective-permute-start.1) | collective-permute-done | bytes 262176 | tf_op jit(solution)/shard_map/ppermute | solution.py:498
  104.8 21.2 %all_to_all.25 = bf16[16,68,256]{2,1,0:T(8,128)(2,1)S(1)} all-to-all(bf16[16,68,256]{2,1,0:T(8,128)(2,1)S(1)} %broadcast_in_dim.2), channel_id=1, replica_groups={{0,1,4,5,8,9,12,13,16,17,20,21,24,25,28,29},{2,3,6,7,10,11,14,15,18,19,..., dimensions={0} | all-to-all | bytes 1114112 | tf_op jit(solution)/shard_map/all_to_all | solution.py:555
  126.4 1.2 fusion.2
  129.1 1.5 %maximum_convert_fusion = f32[8,256,256]{2,1,0:T(8,128)} fusion(bf16[2,256,256]{2,1,0:T(8,128)(2,1)S(1)} %bitcast.66, bf16[2,256,256]{2,1,0:T(8,128)(2,1)S(1)} %bitcast.65, bf16[2,256,256]{2,1,0:T(8,128)(2,1)S(1)} %bitcast.67, bf16[2,256,256]{2,1,0:T(8,128)(2,1)S(1)} %bitcast.64), kind=kLoop, calls=%fused_computation.4 | loop fusion | flops 2097152 | bytes 3145728 | tf_op jit(solution)/shard_map/convert_element_type | solution.py:598
  (48 shorter events, 6.9 us)
Async XLA Ops:
  0.6 1.0 copy-start
  0.6 9.3 %copy-start.1 = (bf16[8,128,256]{2,1,0:T(8,128)(2,1)S(1)}, bf16[8,128,256]{2,1,0:T(8,128)(2,1)}, u32[]{:S(2)}) copy-start(bf16[8,128,256]{2,1,0:T(8,128)(2,1)} %param.4) | copy-start | bytes 1572868
  0.7 11.5 %copy-start.4 = (bf16[8,256,256]{2,1,0:T(8,128)(2,1)S(1)}, bf16[8,256,256]{2,1,0:T(8,128)(2,1)}, u32[]{:S(2)}) copy-start(bf16[8,256,256]{2,1,0:T(8,128)(2,1)} %param.6) | copy-start | bytes 3145732
  1.7 17.8 %copy-start.3 = (f32[2,256]{1,0:T(2,128)S(1)}, f32[2,256]{1,0:T(2,128)}, u32[]{:S(2)}) copy-start(f32[2,256]{1,0:T(2,128)} %gain_ref.5) | copy-start | bytes 6148
  2.5 24.8 %all-to-all-start.1 = ((bf16[16,8,8,256]{3,2,1,0:T(8,128)(2,1)}), bf16[16,8,8,256]{3,2,1,0:T(8,128)(2,1)S(1)}, u32[]{:S(2)}, u32[]{:S(2)}) async-start(bf16[16,8,8,256]{3,2,1,0:T(8,128)(2,1)} %copy_bitcast_fusion), calls=%async_computation.1 | async-start | bytes 1048576 | tf_op jit(solution)/shard_map/all_to_all | solution.py:476
  10.6 8.8 %collective-permute-start = (bf16[4,128,256]{2,1,0:T(8,128)(2,1)}, bf16[4,128,256]{2,1,0:T(8,128)(2,1)S(1)}, u32[]{:S(2)}, u32[]{:S(2)}) collective-permute-start(bf16[4,128,256]{2,1,0:T(8,128)(2,1)} %dynamic-slice_bitcast_fusion), channel_id=1, source_target_pairs={{0,1},{1,0},{2,3},{3,2},{4,5},{5,4},{6,7},{7,6},{8,9},{9,8},{10,11... | collective-permute-start | bytes 786440 | tf_op jit(solution)/shard_map/ppermute | solution.py:498
  19.5 7.9 %copy-start.2 = (bf16[4,128,256]{2,1,0:T(8,128)(2,1)}, bf16[4,128,256]{2,1,0:T(8,128)(2,1)S(1)}, u32[]{:S(2)}) copy-start(bf16[4,128,256]{2,1,0:T(8,128)(2,1)S(1)} %collective-permute-done) | copy-start | bytes 786436
  27.3 20.7 %all-to-all-start = ((bf16[32,32,256]{2,1,0:T(8,128)(2,1)}), bf16[32,32,256]{2,1,0:T(8,128)(2,1)S(1)}, u32[]{:S(2)}, u32[]{:S(2)}) async-start(bf16[32,32,256]{2,1,0:T(8,128)(2,1)} %bitcast.69), calls=%async_computation | async-start | bytes 1048576 | tf_op jit(solution)/shard_map/all_to_all | solution.py:481
  57.6 3.8 %collective-permute-start.3 = (bf16[2,256,256]{2,1,0:T(8,128)(2,1)}, bf16[2,256,256]{2,1,0:T(8,128)(2,1)S(1)}, u32[]{:S(2)}, u32[]{:S(2)}) collective-permute-start(bf16[2,256,256]{2,1,0:T(8,128)(2,1)} %get-tuple-element.40), channel_id=1, source_target_pairs={{0,2},{2,0},{4,6},{6,4},{8,10},{10,8},{12,14},{14,12},{16,18},{18,... | collective-permute-start | bytes 786440 | tf_op jit(solution)/shard_map/ppermute | solution.py:559
  58.8 17.7 %all-to-all-start.2 = ((bf16[32,32,256]{2,1,0:T(8,128)(2,1)}), bf16[32,32,256]{2,1,0:T(8,128)(2,1)S(1)}, u32[]{:S(2)}, u32[]{:S(2)}) async-start(bf16[32,32,256]{2,1,0:T(8,128)(2,1)} %bitcast.68), calls=%async_computation.2 | async-start | bytes 1048576 | tf_op jit(solution)/shard_map/all_to_all | solution.py:481
  61.5 9.4 %collective-permute-start.4 = (bf16[2,2,2,32,256]{4,3,2,1,0:T(8,128)(2,1)S(1)}, bf16[2,2,2,32,256]{4,3,2,1,0:T(8,128)(2,1)S(1)}, u32[]{:S(2)}, u32[]{:S(2)}) collective-permute-start(bf16[2,2,2,32,256]{4,3,2,1,0:T(8,128)(2,1)S(1)} %dynamic-slice_bitcast_fusion.1), channel_id=1, source_target_pairs={{0,4},{2,6},{4,0},{6,2},{8,12},{10,14},{12,8},{14,10},{16,20},{18,... | collective-permute-start | bytes 393224 | tf_op jit(solution)/shard_map/ppermute | solution.py:550
  71.0 15.3 %collective-permute-start.5 = (bf16[2,2,32,256]{3,2,1,0:T(8,128)(2,1)S(1)}, bf16[2,2,32,256]{3,2,1,0:T(8,128)(2,1)S(1)}, u32[]{:S(2)}, u32[]{:S(2)}) collective-permute-start(bf16[2,2,32,256]{3,2,1,0:T(8,128)(2,1)S(1)} %dynamic-slice_bitcast_fusion.2), channel_id=1, source_target_pairs={{0,1},{1,0},{2,3},{3,2},{4,5},{5,4},{6,7},{7,6},{8,9},{9,8},{10,11... | collective-permute-start | bytes 196616 | tf_op jit(solution)/shard_map/ppermute | solution.py:550
  85.3 2.2 %collective-permute-start.2 = (bf16[2,256,256]{2,1,0:T(8,128)(2,1)S(1)}, bf16[2,256,256]{2,1,0:T(8,128)(2,1)S(1)}, u32[]{:S(2)}, u32[]{:S(2)}) collective-permute-start(bf16[2,256,256]{2,1,0:T(8,128)(2,1)S(1)} %get-tuple-element.35), channel_id=1, source_target_pairs={{0,2},{2,0},{4,6},{6,4},{8,10},{10,8},{12,14},{14,12},{16,18},{18,... | collective-permute-start | bytes 786440 | tf_op jit(solution)/shard_map/ppermute | solution.py:564
  86.4 5.8 %collective-permute-start.6 = (bf16[2,32,256]{2,1,0:T(8,128)(2,1)S(1)}, bf16[2,32,256]{2,1,0:T(8,128)(2,1)S(1)}, u32[]{:S(2)}, u32[]{:S(2)}) collective-permute-start(bf16[2,32,256]{2,1,0:T(8,128)(2,1)S(1)} %dynamic-slice_bitcast_fusion.3), channel_id=1, source_target_pairs={{0,8},{2,10},{4,12},{6,14},{8,0},{10,2},{12,4},{14,6},{16,24},{18,... | collective-permute-start | bytes 98312 | tf_op jit(solution)/shard_map/ppermute | solution.py:550
  88.3 16.4 %all-to-all-start.3 = ((bf16[16,32,256]{2,1,0:T(8,128)(2,1)}), bf16[16,32,256]{2,1,0:T(8,128)(2,1)S(1)}, u32[]{:S(2)}, u32[]{:S(2)}) async-start(bf16[16,32,256]{2,1,0:T(8,128)(2,1)} %bitcast.61), calls=%async_computation.3 | async-start | bytes 524288 | tf_op jit(solution)/shard_map/all_to_all | solution.py:555
  92.3 9.8 %collective-permute-start.7 = (bf16[32,256]{1,0:T(8,128)(2,1)S(1)}, bf16[32,256]{1,0:T(8,128)(2,1)S(1)}, u32[]{:S(2)}, u32[]{:S(2)}) collective-permute-start(bf16[32,256]{1,0:T(8,128)(2,1)S(1)} %dynamic-slice_bitcast_fusion.4), channel_id=1, source_target_pairs={{0,16},{2,18},{4,20},{6,22},{8,24},{10,26},{12,28},{14,30},{16,0},... | collective-permute-start | bytes 49160 | tf_op jit(solution)/shard_map/ppermute | solution.py:550
  95.1 9.5 %collective-permute-start.1 = (bf16[4,128,256]{2,1,0:T(8,128)(2,1)}, bf16[4,128,256]{2,1,0:T(8,128)(2,1)S(1)}, u32[]{:S(2)}, u32[]{:S(2)}) collective-permute-start(bf16[4,128,256]{2,1,0:T(8,128)(2,1)} %bitcast.73), channel_id=1, source_target_pairs={{0,1},{1,0},{2,3},{3,2},{4,5},{5,4},{6,7},{7,6},{8,9},{9,8},{10,11... | collective-permute-start | bytes 786440 | tf_op jit(solution)/shard_map/ppermute | solution.py:498
  104.7 21.7 %copy-start.5 = (bf16[4,128,256]{2,1,0:T(8,128)(2,1)S(1)}, bf16[4,128,256]{2,1,0:T(8,128)(2,1)}, u32[]{:S(2)}) copy-start(bf16[4,128,256]{2,1,0:T(8,128)(2,1)} %get-tuple-element.36) | copy-start | bytes 786436
  126.3 2.0 %collective-permute-start.8 = (bf16[1028,256]{1,0:T(8,128)(2,1)S(1)}, bf16[1028,256]{1,0:T(8,128)(2,1)S(1)}, u32[]{:S(2)}, u32[]{:S(2)}) collective-permute-start(bf16[1028,256]{1,0:T(8,128)(2,1)S(1)} %concatenate.28), channel_id=1, source_target_pairs={{0,2},{2,0},{4,6},{6,4},{8,10},{10,8},{12,14},{14,12},{16,18},{18,... | collective-permute-start | bytes 1579016 | tf_op jit(solution)/shard_map/ppermute | solution.py:588

commit v5 on v4

--- a/solution.py
+++ b/solution.py
@@ -18,6 +18,7 @@
 LANES = 128
 MIB = 1024 * 1024
 VMEM_LIMIT = 24 * MIB
+FORWARD_WEIGHT = 40
 
 CONTRACT_LAST = (((1,), (1,)), ((), ()))
 CONTRACT_FIRST = (((0,), (0,)), ((), ()))
@@ -192,15 +193,12 @@
         + [pltpu.HBM((frames, HEADS, bins, bins), f32), pltpu.HBM(whole, bf16)],
         compiler_params=pltpu.CompilerParams(vmem_limit_bytes=VMEM_LIMIT),
         cost_estimate=pl.CostEstimate(
-            flops=flops * FAKE,
+            flops=flops * FORWARD_WEIGHT,
             bytes_accessed=2 * 1024 * 1024,
             transcendentals=frames * HEADS * bins * bins,
         ),
         name="freq_forward",
     )(place, features, near(others), near(weights), gains)
-
-
-FAKE = 1
 
 
 def freq_backward_kernel(
@@ -295,10 +293,10 @@
             ],
         ),
         out_shape=[
-            pltpu.HBM((frames, bins_dev, width), bf16),
-            pltpu.HBM(others.shape, bf16),
-            jax.ShapeDtypeStruct(half, bf16),
-            jax.ShapeDtypeStruct(half, bf16),
+            pltpu.VMEM((frames, bins_dev, width), bf16),
+            pltpu.VMEM(others.shape, bf16),
+            pltpu.VMEM(half, bf16),
+            pltpu.VMEM(half, bf16),
             jax.ShapeDtypeStruct((1, width), f32),
         ],
         compiler_params=pltpu.CompilerParams(vmem_limit_bytes=VMEM_LIMIT),
@@ -411,7 +409,7 @@
         in_specs=[smem, smem, vmem, vmem, vmem, vmem],
         out_specs=[hbm] + [vmem] * 3,
         out_shape=[pltpu.HBM((own_rows, width), bf16)]
-        + [jax.ShapeDtypeStruct((2, width, width), bf16)] * 2
+        + [pltpu.VMEM((2, width, width), bf16)] * 2
         + [jax.ShapeDtypeStruct((1, width), f32)],
         scratch_shapes=[
             pltpu.VMEM((own_rows, width), bf16),
@@ -429,23 +427,51 @@
     )(place, first, near(hidden), near(upstream), near(weights), gains)
 
 
-def pair_kernel(kept_ref, arrived_ref, out_ref):
-    out_ref[...] = (kept_ref[...].astype(f32) + arrived_ref[...].astype(f32)).astype(bf16)
-
-
-def pair_sum(kept, arrived):
+def sums_kernel(kept_ref, arrived_ref, time_ref, freq_gain_ref, time_gain_ref, out_ref, gain_rows):
+    peers, _, width = out_ref.shape
+    total = kept_ref[...].astype(f32) + arrived_ref[...].astype(f32)
+    gain_rows[...] = jnp.zeros_like(gain_rows)
+    for m, ref in enumerate((freq_gain_ref, time_gain_ref)):
+        high = ref[...].astype(bf16).astype(f32)
+        gain_rows[m : m + 1] = high
+        gain_rows[m + 2 : m + 3] = ref[...] - high
+    parts = [
+        total.reshape(peers, -1, width),
+        time_ref[...].astype(f32).reshape(peers, -1, width),
+        jnp.broadcast_to(gain_rows[...][None], (peers,) + gain_rows.shape),
+    ]
+    out_ref[...] = jnp.concatenate(parts, axis=1).astype(bf16)
+
+
+def sums_by_peer(kept, arrived, time_rows, freq_gain, time_gain, peers):
+    width = kept.shape[-1]
+    freq_count = kept.size // (peers * width)
+    time_count = time_rows.size // (peers * width)
+    if freq_count % 8 or time_count % 8:
+        total = (kept.astype(f32) + arrived.astype(f32)).astype(bf16)
+        gains = jnp.concatenate([freq_gain, time_gain], axis=0)
+        high = gains.astype(bf16)
+        gains = jnp.concatenate([high, (gains - high.astype(f32)).astype(bf16)], axis=0)
+        parts = [
+            total.reshape(peers, -1, width),
+            time_rows.reshape(peers, -1, width),
+            jnp.broadcast_to(gains[None], (peers,) + gains.shape),
+        ]
+        return jnp.concatenate(parts, axis=1), freq_count, time_count
     vmem = pl.BlockSpec(memory_space=pltpu.VMEM)
-    return pl.pallas_call(
-        pair_kernel,
-        in_specs=[vmem] * 2,
+    sums = pl.pallas_call(
+        sums_kernel,
+        in_specs=[vmem] * 5,
         out_specs=vmem,
-        out_shape=pltpu.HBM(kept.shape, bf16),
+        out_shape=pltpu.HBM((peers, freq_count + time_count + 8, width), bf16),
+        scratch_shapes=[pltpu.VMEM((8, width), f32)],
         compiler_params=pltpu.CompilerParams(vmem_limit_bytes=VMEM_LIMIT),
         cost_estimate=pl.CostEstimate(
             flops=kept.size, bytes_accessed=6 * kept.size, transcendentals=0
         ),
-        name="pair_sum",
-    )(kept, arrived)
+        name="sums_by_peer",
+    )(kept, arrived, time_rows, freq_gain, time_gain)
+    return sums, freq_count, time_count
 
 
 def group_size(devices, bins_dev):
@@ -533,20 +559,20 @@
     ]
     peers = len(same[0])
 
+    rows = 2 * width
+    sets = 2 * freq
+    halved = tm % 4 == 0 and freq & (freq - 1) == 0 and rows % (8 * sets * peers) == 0
+    steps = [("tm", 1)] + [("freq", k) for k in reversed(range(freq.bit_length() - 1))]
+    if not halved:
+        sets, steps = 1, []
+
     def scattered(partial):
-        bits = [("tm", k) for k in reversed(range(1, tm.bit_length() - 1))]
-        bits += [("freq", k) for k in reversed(range(freq.bit_length() - 1))]
-        partial = partial.reshape((2,) * len(bits) + (-1, width))
-        order = sorted(range(len(bits)), key=lambda i: (bits[i][1] > 1, bits[i][0] != "tm", bits[i][1]))
-        left = list(range(len(bits)))
-        for i in order:
-            axis, k = bits[i]
-            place_in = left.index(i)
-            left.remove(i)
+        partial = partial.reshape((2,) * len(steps) + (-1, width))
+        for axis, k in steps:
             mine = (lax.axis_index(axis) >> k) & 1
+            sent = lax.dynamic_index_in_dim(partial, 1 - mine, 0, False)
+            kept = lax.dynamic_index_in_dim(partial, mine, 0, False)
             devices = range(lax.axis_size(axis))
-            sent = lax.dynamic_index_in_dim(partial, 1 - mine, place_in, False)
-            kept = lax.dynamic_index_in_dim(partial, mine, place_in, False)
             came = lax.ppermute(sent, axis, [(d, d ^ (1 << k)) for d in devices])
             partial = (kept.astype(f32) + came.astype(f32)).astype(bf16)
         return partial
@@ -557,45 +583,39 @@
         )
 
     time_arrived = lax.ppermute(time_sent, "tm", pairs)
-    time_block = scattered((time_kept.astype(f32) + time_arrived.astype(f32)).astype(bf16))
+    time_rows = scattered((time_kept.astype(f32) + time_arrived.astype(f32)).astype(bf16))
     grad_own, grad_others, freq_kept, freq_sent, freq_dg = freq_backward(
         place, by_target, others, q, k, v, o, probs, grad_hidden, freq_w, gains
     )
     freq_arrived = lax.ppermute(freq_sent, "tm", pairs)
-    arrived = over_same(pair_sum(freq_kept, freq_arrived).reshape(peers, -1, width))
+    sums, freq_count, time_count = sums_by_peer(
+        freq_kept, freq_arrived, time_rows, freq_dg, time_dg, peers
+    )
+    arrived = over_same(sums)
     returned = [grad_own] + [along_freq(grad_others[j - 1], -j) for j in range(1, freq)]
     returned, arrived = lax.optimization_barrier((returned, arrived))
     grad_input = jnp.roll(jnp.stack(returned), place[0], axis=0).reshape(features.shape)
 
     inv_root = (total_frames * bins_dev * freq) ** (-0.5)
-
-    def split(rows):
-        high = rows.astype(bf16)
-        return [high, (rows - high.astype(f32)).astype(bf16)]
-
     summed = jnp.sum(arrived.astype(f32), axis=0) * inv_root
-    summed = jnp.concatenate([summed, time_block.astype(f32) * inv_root], axis=0)
-    count = summed.shape[0]
-    gain_rows = jnp.concatenate([freq_dg, time_dg], axis=0) * inv_root
-    sent = jnp.concatenate([summed.astype(bf16)] + split(gain_rows), axis=0)
-    gathered = over_same(jnp.broadcast_to(sent[None], (peers,) + sent.shape))
-    gain_sum = jnp.sum(gathered[:, count:].astype(f32), axis=0)
-    gain_sum = gain_sum[:2] + gain_sum[2:]
-    mine = jnp.concatenate(
-        [gathered[:, : count // 2].reshape(-1, width), gathered[:, count // 2 : count].reshape(-1, width)],
-        axis=0,
-    )
-    theirs = lax.ppermute(jnp.concatenate([mine] + split(gain_sum), axis=0), "tm", pairs)
-    gain_high_low = split(gain_sum)
-    other_gain = theirs[-4:].astype(f32)
-    gain_grads = sum(g.astype(f32) for g in gain_high_low) + other_gain[:2] + other_gain[2:]
-    theirs = theirs[:-4]
+    gain_sum = summed[freq_count + time_count :]
+    gain_sum = gain_sum[:2] + gain_sum[2:4]
+    time_arrived = arrived[:, freq_count : freq_count + time_count].astype(f32)
+    time_sum = jnp.sum(time_arrived.reshape(-1, sets, time_count, width), axis=0) * inv_root
+    block = jnp.concatenate([summed[:freq_count], time_sum.reshape(-1, width)], axis=0)
+    block, gain_sum = lax.optimization_barrier((block.astype(bf16), gain_sum))
+    gathered = over_same(jnp.broadcast_to(block[None], (peers,) + block.shape))
+    gathered, gain_sum = lax.optimization_barrier((gathered, gain_sum))
+    gain_grads = gain_sum + lax.ppermute(gain_sum, "tm", pairs)
+    theirs = lax.ppermute(gathered, "tm", pairs)
     first_core = core == 0
-    first_half = jnp.where(first_core, mine, theirs).reshape(2, 2, width, width)
-    second_half = jnp.where(first_core, theirs, mine).reshape(2, 2, width, width)
-    weight_grads = jnp.concatenate(
-        [first_half[0], second_half[0], first_half[1], second_half[1]], axis=0
-    ).astype(f32)
+    halves = jnp.stack(
+        [jnp.where(first_core, gathered, theirs), jnp.where(first_core, theirs, gathered)]
+    )
+    freq_grads = halves[:, :, :freq_count].reshape(4, width, width)
+    time_grads = halves[:, :, freq_count:].reshape(2, peers, sets, time_count, width)
+    time_grads = jnp.swapaxes(time_grads, 1, 2).reshape(4, width, width)
+    weight_grads = jnp.concatenate([freq_grads, time_grads], axis=0).astype(f32)
     return (grad_input, weight_grads, gain_grads)
 
 

time: 131 us -> 126 us (0.962)
  starting transfers between devices: 32.9 us -> 27.4 us
  waiting for transfers between devices: 40.6 us -> 43.5 us
    all_to_all x1, waiting for transfers between devices: 0.01 us -> 6.47 us  [over_tm(): lax.all_to_all(blocks, 'tm', 0, 0, tiled=True, axis_index_groups=groups)]
    ppermute x4 -> x2, waiting for transfers between devices: 13 us -> 7.58 us  [scattered(): came = lax.ppermute(sent, axis, [(d, d ^ 1 << k) for d in devices])]
    ppermute x4 -> x2, starting transfers between devices: 7.99 us -> 4.07 us  [scattered(): came = lax.ppermute(sent, axis, [(d, d ^ 1 << k) for d in devices])]
    all_to_all x2, starting transfers between devices: 8.35 us -> 5.76 us  [over_all(): lax.all_to_all(flat, ('tm', 'freq'), 0, 0, tiled=True).reshape(blocks.shape)]
    ppermute x2, starting transfers between devices: 3.01 us -> 4.89 us  [along_freq(): lax.ppermute(block, 'freq', [(i, (i + steps) % freq) for i in range(freq)])]
    all_to_all x1, starting transfers between devices: 7.36 us -> 5.91 us  [over_tm(): lax.all_to_all(blocks, 'tm', 0, 0, tiled=True, axis_index_groups=groups)]
  transfers between devices with their start and end apart: 13 -> 12, of which waited for: 8 -> 8; matrix products, arithmetic and copies ran while one was open for 3% -> 3% of each run, Pallas kernels for 13% -> 13%
where the time goes in v5:
time: 126 us
  waiting for transfers between devices  43.5 us (35%)
  starting transfers between devices  27.4 us (22%)
  Pallas kernels  26.4 us (21%)
  blocking collectives  19.9 us (16%)
  local copies, waits for them, and re-layouts  3.91 us (3%)
  other arithmetic  3.7 us (3%)
    all_to_all x1, blocking collectives, over_same(): lax.all_to_all(blocks, ('tm', 'freq'), 0, 0, tiled=True, axis_index_group...  19.9 us
    all_to_all x2, waiting for transfers between devices, over_all(): lax.all_to_all(flat, ('tm', 'freq'), 0, 0, tiled=True).reshape(blocks.shape)  17.1 us
    ppermute x2, waiting for transfers between devices, along_freq(): lax.ppermute(block, 'freq', [(i, (i + steps) % freq) for i in range(freq)])  9.98 us
    pallas_call x1, Pallas kernels, time_attention(): pl.pallas_call(functools.partial(time_kernel, bins, own_start, total), in...  9.56 us
    pallas_call x1, Pallas kernels, freq_backward(): pl.pallas_call(freq_backward_kernel, grid_spec=pltpu.PrefetchScalarGridSp...  8.13 us
    pallas_call x1, Pallas kernels, freq_forward(): pl.pallas_call(freq_forward_kernel, grid_spec=pltpu.PrefetchScalarGridSpe...  7.82 us
    ppermute x2, waiting for transfers between devices, scattered(): came = lax.ppermute(sent, axis, [(d, d ^ 1 << k) for d in devices])  7.58 us
    all_to_all x1, waiting for transfers between devices, over_tm(): lax.all_to_all(blocks, 'tm', 0, 0, tiled=True, axis_index_groups=groups)  6.47 us
  transfers between devices with their start and end apart: 12, of which 8 were waited for; matrix products, arithmetic and copies ran while one was open for 3% of the time, Pallas kernels for 13%

profile of v5, /device:TPU:0, one launch (start us, length us, event | category | flops | bytes accessed | tf_op | source)
XLA Modules:
  0.0 125.7 jit_solution(6731969567112706519)
XLA Ops:
  0.7 1.8 %dynamic-slice_bitcast_fusion = bf16[4,128,256]{2,1,0:T(8,128)(2,1)} fusion(bf16[2,4,128,256]{3,2,1,0:T(8,128)(2,1)} %bitcast.50, s32[]{:T(128)S(6)} %select_n.59), kind=kLoop, calls=%fused_computation.20 | loop fusion | bytes 524292 | tf_op jit(solution)/shard_map/jit(dynamic_index_in_dim)/squeeze | solution.py:528
  2.5 3.0 %collective-permute-start = (bf16[4,128,256]{2,1,0:T(8,128)(2,1)}, bf16[4,128,256]{2,1,0:T(8,128)(2,1)S(1)}, u32[]{:S(2)}, u32[]{:S(2)}) collective-permute-start(bf16[4,128,256]{2,1,0:T(8,128)(2,1)} %dynamic-slice_bitcast_fusion), channel_id=1, source_target_pairs={{0,1},{1,0},{2,3},{3,2},{4,5},{5,4},{6,7},{7,6},{8,9},{9,8},{10,11... | collective-permute-start | bytes 786440 | tf_op jit(solution)/shard_map/ppermute | solution.py:524
  6.3 5.9 %all-to-all-start.1 = ((bf16[16,8,8,256]{3,2,1,0:T(8,128)(2,1)}), bf16[16,8,8,256]{3,2,1,0:T(8,128)(2,1)S(1)}, u32[]{:S(2)}, u32[]{:S(2)}) async-start(bf16[16,8,8,256]{3,2,1,0:T(8,128)(2,1)} %copy_bitcast_fusion), calls=%async_computation.1 | async-start | bytes 1048576 | tf_op jit(solution)/shard_map/all_to_all | solution.py:502
  12.4 7.8 %freq_forward.1 = (bf16[4,256,256]{2,1,0:T(8,128)(2,1)}, bf16[4,256,256]{2,1,0:T(8,128)(2,1)}, bf16[4,256,256]{2,1,0:T(8,128)(2,1)}, bf16[4,256,256]{2,1,0:T(8,1...) custom-call(s32[2]{0:T(128)S(1)} %pad_add_fusion.place_ref, ...), custom_call_target="tpu_custom_call" | custom-call | flops 64424509440 | bytes 2097152 | tf_op jit(solution)/shard_map/freq_forward/pallas_call | solution.py:175
  20.2 6.5 %all-to-all-done.1 = bf16[16,8,8,256]{3,2,1,0:T(8,128)(2,1)S(1)} async-done(((bf16[16,8,8,256]{3,2,1,0:T(8,128)(2,1)}), bf16[16,8,8,256]{3,2,1,0:T(8,128)(2,1)S(1)}, u32[]{:S(2)}, u32[]{:S(2)}) %all-to-all-start.1) | async-done | bytes 524320 | tf_op jit(solution)/shard_map/all_to_all | solution.py:502
  26.7 3.1 %all-to-all-start = ((bf16[32,32,256]{2,1,0:T(8,128)(2,1)}), bf16[32,32,256]{2,1,0:T(8,128)(2,1)S(1)}, u32[]{:S(2)}, u32[]{:S(2)}) async-start(bf16[32,32,256]{2,1,0:T(8,128)(2,1)} %bitcast.61), calls=%async_computation | async-start | bytes 1048576 | tf_op jit(solution)/shard_map/all_to_all | solution.py:507
  29.8 1.1 slice.29.w_ref
  30.9 13.9 %all-to-all-done = bf16[32,32,256]{2,1,0:T(8,128)(2,1)S(1)} async-done(((bf16[32,32,256]{2,1,0:T(8,128)(2,1)}), bf16[32,32,256]{2,1,0:T(8,128)(2,1)S(1)}, u32[]{:S(2)}, u32[]{:S(2)}) %all-to-all-start) | async-done | bytes 524320 | tf_op jit(solution)/shard_map/all_to_all | solution.py:507
  44.8 9.6 %time_attention.1 = (bf16[1024,256]{1,0:T(8,128)(2,1)}, bf16[2,256,256]{2,1,0:T(8,128)(2,1)S(1)}, bf16[2,256,256]{2,1,0:T(8,128)(2,1)}, f32[1,256]{1,0:T(1,128)S(1)}) custom-call(s32[2]{0:T(128)S(1)} %pad_add_fusion.place_ref, s32[1]{0:T(128)} %bitcast.5.first_ref, bf16[1024,256]{1,0:T(8,128)(2,1)S(1)} %bitcast.48, bf16[1024,256]{1,0:T(8,128)(2,1)S(1)} %bitcast.46, ...), custom_call_target="tpu_custom_call" | custom-call | flops 3087007744 | bytes 4194304 | tf_op jit(solution)/shard_map/time_attention/pallas_call | solution.py:407
  54.4 1.1 collective-permute-start.3
  55.5 2.7 %all-to-all-start.2 = ((bf16[32,32,256]{2,1,0:T(8,128)(2,1)}), bf16[32,32,256]{2,1,0:T(8,128)(2,1)S(1)}, u32[]{:S(2)}, u32[]{:S(2)}) async-start(bf16[32,32,256]{2,1,0:T(8,128)(2,1)} %bitcast.60), calls=%async_computation.2 | async-start | bytes 1048576 | tf_op jit(solution)/shard_map/all_to_all | solution.py:507
  58.3 1.8 %collective-permute-start.4 = (bf16[2,128,256]{2,1,0:T(8,128)(2,1)S(1)}, bf16[2,128,256]{2,1,0:T(8,128)(2,1)S(1)}, u32[]{:S(2)}, u32[]{:S(2)}) collective-permute-start(bf16[2,128,256]{2,1,0:T(8,128)(2,1)S(1)} %dynamic-slice_bitcast_fusion.1), channel_id=1, source_target_pairs={{0,4},{2,6},{4,0},{6,2},{8,12},{10,14},{12,8},{14,10},{16,20},{18,... | collective-permute-start | bytes 393224 | tf_op jit(solution)/shard_map/ppermute | solution.py:576
  60.1 7.6 %collective-permute-done.4 = bf16[2,128,256]{2,1,0:T(8,128)(2,1)S(1)} collective-permute-done((bf16[2,128,256]{2,1,0:T(8,128)(2,1)S(1)}, bf16[2,128,256]{2,1,0:T(8,128)(2,1)S(1)}, u32[]{:S(2)}, u32[]{:S(2)}) %collective-permute-start.4) | collective-permute-done | bytes 131104 | tf_op jit(solution)/shard_map/ppermute | solution.py:576
  67.8 2.2 %collective-permute-start.5 = (bf16[128,256]{1,0:T(8,128)(2,1)S(1)}, bf16[128,256]{1,0:T(8,128)(2,1)S(1)}, u32[]{:S(2)}, u32[]{:S(2)}) collective-permute-start(bf16[128,256]{1,0:T(8,128)(2,1)S(1)} %dynamic-slice_bitcast_fusion.2), channel_id=1, source_target_pairs={{0,1},{1,0},{2,3},{3,2},{4,5},{5,4},{6,7},{7,6},{8,9},{9,8},{10,11... | collective-permute-start | bytes 196616 | tf_op jit(solution)/shard_map/ppermute | solution.py:576
  70.0 3.2 %all-to-all-done.2 = bf16[32,32,256]{2,1,0:T(8,128)(2,1)S(1)} async-done(((bf16[32,32,256]{2,1,0:T(8,128)(2,1)}), bf16[32,32,256]{2,1,0:T(8,128)(2,1)S(1)}, u32[]{:S(2)}, u32[]{:S(2)}) %all-to-all-start.2) | async-done | bytes 524320 | tf_op jit(solution)/shard_map/all_to_all | solution.py:507
  73.2 8.1 %freq_backward.1 = (bf16[4,128,256]{2,1,0:T(8,128)(2,1)S(1)}, bf16[1,4,128,256]{3,2,1,0:T(8,128)(2,1)S(1)}, bf16[2,256,256]{2,1,0:T(8,128)(2,1)S(1)}, bf16[2,256,256]{2,1,0:T(8,128)(2,1)S(1)}, f32[1,256]{1,0:T(1,128)S(1)}) custom-call(s32[2]{0:T(128)S(1)} %pad_add_fusion.place_ref, bf16[2,4,128,256]{3,2,1,0:T(8,128)(2,1)S(1)} %bitcast.52, ...), custom_call_target="tpu_custom_call" | custom-call | flops 3221225472 | bytes 8388608 | tf_op jit(solution)/shard_map/freq_backward/pallas_call | solution.py:270
  81.3 1.1 collective-permute-start.2
  82.5 1.1 collective-permute-done.2.arrived_ref
  84.5 3.9 %all-to-all-start.3 = ((bf16[16,48,256]{2,1,0:T(8,128)(2,1)}), bf16[16,48,256]{2,1,0:T(8,128)(2,1)S(1)}, u32[]{:S(2)}, u32[]{:S(2)}) async-start(bf16[16,48,256]{2,1,0:T(8,128)(2,1)} %sums_by_peer.1), calls=%async_computation.3 | async-start | bytes 786432 | tf_op jit(solution)/shard_map/all_to_all | solution.py:581
  88.4 1.9 %collective-permute-start.1 = (bf16[4,128,256]{2,1,0:T(8,128)(2,1)S(1)}, bf16[4,128,256]{2,1,0:T(8,128)(2,1)S(1)}, u32[]{:S(2)}, u32[]{:S(2)}) collective-permute-start(bf16[4,128,256]{2,1,0:T(8,128)(2,1)S(1)} %bitcast.55), channel_id=1, source_target_pairs={{0,1},{1,0},{2,3},{3,2},{4,5},{5,4},{6,7},{7,6},{8,9},{9,8},{10,11... | collective-permute-start | bytes 786440 | tf_op jit(solution)/shard_map/ppermute | solution.py:524
  90.4 10.0 %collective-permute-done.1 = bf16[4,128,256]{2,1,0:T(8,128)(2,1)S(1)} collective-permute-done((bf16[4,128,256]{2,1,0:T(8,128)(2,1)S(1)}, bf16[4,128,256]{2,1,0:T(8,128)(2,1)S(1)}, u32[]{:S(2)}, u32[]{:S(2)}) %collective-permute-start.1) | collective-permute-done | bytes 262176 | tf_op jit(solution)/shard_map/ppermute | solution.py:524
  101.6 19.9 %all_to_all.25 = bf16[16,64,256]{2,1,0:T(8,128)(2,1)S(1)} all-to-all(bf16[16,64,256]{2,1,0:T(8,128)(2,1)S(1)} %broadcast_in_dim.2), channel_id=1, replica_groups={{0,1,4,5,8,9,12,13,16,17,20,21,24,25,28,29},{2,3,6,7,10,11,14,15,18,19,..., dimensions={0} | all-to-all | bytes 1048576 | tf_op jit(solution)/shard_map/all_to_all | solution.py:581
  122.0 1.2 fusion.3
  124.3 1.5 %maximum_convert_fusion = f32[8,256,256]{2,1,0:T(8,128)} fusion(bf16[4,256,256]{2,1,0:T(8,128)(2,1)S(1)} %bitcast.56, bf16[4,256,256]{2,1,0:T(8,128)(2,1)S(1)} %bitcast.57), kind=kLoop, calls=%fused_computation.6 | loop fusion | flops 1048576 | bytes 3145728 | tf_op jit(solution)/shard_map/convert_element_type | solution.py:618
  (40 shorter events, 4.8 us)
Async XLA Ops:
  0.6 4.8 %copy-start = (bf16[8,128,256]{2,1,0:T(8,128)(2,1)S(1)}, bf16[8,128,256]{2,1,0:T(8,128)(2,1)}, u32[]{:S(2)}) copy-start(bf16[8,128,256]{2,1,0:T(8,128)(2,1)} %param.5) | copy-start | bytes 1572868
  0.6 11.7 %copy-start.1 = (bf16[8,128,256]{2,1,0:T(8,128)(2,1)S(1)}, bf16[8,128,256]{2,1,0:T(8,128)(2,1)}, u32[]{:S(2)}) copy-start(bf16[8,128,256]{2,1,0:T(8,128)(2,1)} %param.4) | copy-start | bytes 1572868
  0.7 11.6 %copy-start.4 = (bf16[8,256,256]{2,1,0:T(8,128)(2,1)S(1)}, bf16[8,256,256]{2,1,0:T(8,128)(2,1)}, u32[]{:S(2)}) copy-start(bf16[8,256,256]{2,1,0:T(8,128)(2,1)} %param.6) | copy-start | bytes 3145732
  0.7 11.7 %copy-start.3 = (f32[2,256]{1,0:T(2,128)S(1)}, f32[2,256]{1,0:T(2,128)}, u32[]{:S(2)}) copy-start(f32[2,256]{1,0:T(2,128)} %gain_ref.5) | copy-start | bytes 6148
  2.5 9.9 %collective-permute-start = (bf16[4,128,256]{2,1,0:T(8,128)(2,1)}, bf16[4,128,256]{2,1,0:T(8,128)(2,1)S(1)}, u32[]{:S(2)}, u32[]{:S(2)}) collective-permute-start(bf16[4,128,256]{2,1,0:T(8,128)(2,1)} %dynamic-slice_bitcast_fusion), channel_id=1, source_target_pairs={{0,1},{1,0},{2,3},{3,2},{4,5},{5,4},{6,7},{7,6},{8,9},{9,8},{10,11... | collective-permute-start | bytes 786440 | tf_op jit(solution)/shard_map/ppermute | solution.py:524
  6.3 20.4 %all-to-all-start.1 = ((bf16[16,8,8,256]{3,2,1,0:T(8,128)(2,1)}), bf16[16,8,8,256]{3,2,1,0:T(8,128)(2,1)S(1)}, u32[]{:S(2)}, u32[]{:S(2)}) async-start(bf16[16,8,8,256]{3,2,1,0:T(8,128)(2,1)} %copy_bitcast_fusion), calls=%async_computation.1 | async-start | bytes 1048576 | tf_op jit(solution)/shard_map/all_to_all | solution.py:502
  12.4 7.8 %copy-start.2 = (bf16[4,128,256]{2,1,0:T(8,128)(2,1)}, bf16[4,128,256]{2,1,0:T(8,128)(2,1)S(1)}, u32[]{:S(2)}) copy-start(bf16[4,128,256]{2,1,0:T(8,128)(2,1)S(1)} %collective-permute-done) | copy-start | bytes 786436
  26.7 18.1 %all-to-all-start = ((bf16[32,32,256]{2,1,0:T(8,128)(2,1)}), bf16[32,32,256]{2,1,0:T(8,128)(2,1)S(1)}, u32[]{:S(2)}, u32[]{:S(2)}) async-start(bf16[32,32,256]{2,1,0:T(8,128)(2,1)} %bitcast.61), calls=%async_computation | async-start | bytes 1048576 | tf_op jit(solution)/shard_map/all_to_all | solution.py:507
  54.4 3.8 %collective-permute-start.3 = (bf16[2,256,256]{2,1,0:T(8,128)(2,1)}, bf16[2,256,256]{2,1,0:T(8,128)(2,1)S(1)}, u32[]{:S(2)}, u32[]{:S(2)}) collective-permute-start(bf16[2,256,256]{2,1,0:T(8,128)(2,1)} %get-tuple-element.41), channel_id=1, source_target_pairs={{0,2},{2,0},{4,6},{6,4},{8,10},{10,8},{12,14},{14,12},{16,18},{18,... | collective-permute-start | bytes 786440 | tf_op jit(solution)/shard_map/ppermute | solution.py:585
  55.5 17.7 %all-to-all-start.2 = ((bf16[32,32,256]{2,1,0:T(8,128)(2,1)}), bf16[32,32,256]{2,1,0:T(8,128)(2,1)S(1)}, u32[]{:S(2)}, u32[]{:S(2)}) async-start(bf16[32,32,256]{2,1,0:T(8,128)(2,1)} %bitcast.60), calls=%async_computation.2 | async-start | bytes 1048576 | tf_op jit(solution)/shard_map/all_to_all | solution.py:507
  58.3 9.4 %collective-permute-start.4 = (bf16[2,128,256]{2,1,0:T(8,128)(2,1)S(1)}, bf16[2,128,256]{2,1,0:T(8,128)(2,1)S(1)}, u32[]{:S(2)}, u32[]{:S(2)}) collective-permute-start(bf16[2,128,256]{2,1,0:T(8,128)(2,1)S(1)} %dynamic-slice_bitcast_fusion.1), channel_id=1, source_target_pairs={{0,4},{2,6},{4,0},{6,2},{8,12},{10,14},{12,8},{14,10},{16,20},{18,... | collective-permute-start | bytes 393224 | tf_op jit(solution)/shard_map/ppermute | solution.py:576
  67.8 14.7 %collective-permute-start.5 = (bf16[128,256]{1,0:T(8,128)(2,1)S(1)}, bf16[128,256]{1,0:T(8,128)(2,1)S(1)}, u32[]{:S(2)}, u32[]{:S(2)}) collective-permute-start(bf16[128,256]{1,0:T(8,128)(2,1)S(1)} %dynamic-slice_bitcast_fusion.2), channel_id=1, source_target_pairs={{0,1},{1,0},{2,3},{3,2},{4,5},{5,4},{6,7},{7,6},{8,9},{9,8},{10,11... | collective-permute-start | bytes 196616 | tf_op jit(solution)/shard_map/ppermute | solution.py:576
  81.3 2.3 %collective-permute-start.2 = (bf16[2,256,256]{2,1,0:T(8,128)(2,1)S(1)}, bf16[2,256,256]{2,1,0:T(8,128)(2,1)S(1)}, u32[]{:S(2)}, u32[]{:S(2)}) collective-permute-start(bf16[2,256,256]{2,1,0:T(8,128)(2,1)S(1)} %get-tuple-element.39), channel_id=1, source_target_pairs={{0,2},{2,0},{4,6},{6,4},{8,10},{10,8},{12,14},{14,12},{16,18},{18,... | collective-permute-start | bytes 786440 | tf_op jit(solution)/shard_map/ppermute | solution.py:590
  84.5 16.9 %all-to-all-start.3 = ((bf16[16,48,256]{2,1,0:T(8,128)(2,1)}), bf16[16,48,256]{2,1,0:T(8,128)(2,1)S(1)}, u32[]{:S(2)}, u32[]{:S(2)}) async-start(bf16[16,48,256]{2,1,0:T(8,128)(2,1)} %sums_by_peer.1), calls=%async_computation.3 | async-start | bytes 786432 | tf_op jit(solution)/shard_map/all_to_all | solution.py:581
  88.4 11.9 %collective-permute-start.1 = (bf16[4,128,256]{2,1,0:T(8,128)(2,1)S(1)}, bf16[4,128,256]{2,1,0:T(8,128)(2,1)S(1)}, u32[]{:S(2)}, u32[]{:S(2)}) collective-permute-start(bf16[4,128,256]{2,1,0:T(8,128)(2,1)S(1)} %bitcast.55), channel_id=1, source_target_pairs={{0,1},{1,0},{2,3},{3,2},{4,5},{5,4},{6,7},{7,6},{8,9},{9,8},{10,11... | collective-permute-start | bytes 786440 | tf_op jit(solution)/shard_map/ppermute | solution.py:524
  121.5 2.5 %collective-permute-start.6 = (bf16[16,64,256]{2,1,0:T(8,128)(2,1)S(1)}, bf16[16,64,256]{2,1,0:T(8,128)(2,1)S(1)}, u32[]{:S(2)}, u32[]{:S(2)}) collective-permute-start(bf16[16,64,256]{2,1,0:T(8,128)(2,1)S(1)} %all_to_all.25), channel_id=1, source_target_pairs={{0,2},{2,0},{4,6},{6,4},{8,10},{10,8},{12,14},{14,12},{16,18},{18,... | collective-permute-start | bytes 1572872 | tf_op jit(solution)/shard_map/ppermute | solution.py:610
  121.5 1.9 %collective-permute-start.7 = (f32[2,256]{1,0:T(2,128)S(1)}, f32[2,256]{1,0:T(2,128)S(1)}, u32[]{:S(2)}, u32[]{:S(2)}) collective-permute-start(f32[2,256]{1,0:T(2,128)S(1)} %slice_add_fusion), channel_id=1, source_target_pairs={{0,2},{2,0},{4,6},{6,4},{8,10},{10,8},{12,14},{14,12},{16,18},{18,... | collective-permute-start | bytes 6152 | tf_op jit(solution)/shard_map/ppermute | solution.py:609

commit v6 on v5

--- a/solution.py
+++ b/solution.py
@@ -109,7 +109,7 @@
     step = pl.program_id(0)
     freq, bins_dev, width = others_ref.shape[0] + 1, own_ref.shape[2], own_ref.shape[3]
     bins_time = hold.shape[2] // pl.num_programs(0)
-    x = joined(own_ref, others_ref)
+    x = joined(own_ref.at[0, 0], others_ref.at[:, 0])
     _, unit = norm_parts(x)
     n = (unit * gain_ref[0:1, :]).astype(bf16)
     scale = (width // HEADS) ** (-0.5)
@@ -124,7 +124,7 @@
     v_ref[0] = v
     o_ref[0] = o
     for h in range(HEADS):
-        p_ref[0, h] = probs[h]
+        p_ref[0, h] = probs[h].astype(bf16)
     rows = pl.ds(pl.multiple_of(step * bins_time, bins_time), bins_time)
     for f in range(freq):
         part = hidden[f * bins_dev : (f + 1) * bins_dev].reshape(-1, bins_time, width)
@@ -153,10 +153,10 @@
     return pltpu.with_memory_space_constraint(array, pltpu.HBM)
 
 
-def frame_specs(freq, bins_dev, width):
-    own = pl.BlockSpec((1, 1, bins_dev, width), lambda i, place: (place[0], i, 0, 0))
-    others = pl.BlockSpec((freq - 1, 1, bins_dev, width), lambda i, place: (0, i, 0, 0))
-    rows = pl.BlockSpec((1, freq * bins_dev, width), lambda i, place: (i, 0, 0))
+def frame_specs(freq, bins_dev, width, count=1):
+    own = pl.BlockSpec((1, count, bins_dev, width), lambda i, place: (place[0], i, 0, 0))
+    others = pl.BlockSpec((freq - 1, count, bins_dev, width), lambda i, place: (0, i, 0, 0))
+    rows = pl.BlockSpec((count, freq * bins_dev, width), lambda i, place: (i, 0, 0))
     return own, others, rows
 
 
@@ -190,7 +190,7 @@
             ],
         ),
         out_shape=[rowshape] * 4
-        + [pltpu.HBM((frames, HEADS, bins, bins), f32), pltpu.HBM(whole, bf16)],
+        + [pltpu.HBM((frames, HEADS, bins, bins), bf16), pltpu.HBM(whole, bf16)],
         compiler_params=pltpu.CompilerParams(vmem_limit_bytes=VMEM_LIMIT),
         cost_estimate=pl.CostEstimate(
             flops=flops * FORWARD_WEIGHT,
@@ -202,48 +202,62 @@
 
 
 def freq_backward_kernel(
-    place_ref, own_ref, others_ref, q_ref, k_ref, v_ref, o_ref, p_ref, gh_ref, w_ref, gain_ref,
-    gown_ref, gothers_ref, kept_ref, sent_ref, dg_ref, hold, total
+    place_ref, x_hbm, others_hbm, q_hbm, k_hbm, v_hbm, o_hbm, p_hbm, gh_ref, w_ref, gain_ref,
+    gown_ref, gothers_ref, kept_ref, sent_ref, dg_ref,
+    own_ref, others_ref, q_ref, k_ref, v_ref, o_ref, p_ref, hold, total, sems
 ):
-    step = pl.program_id(0)
-    freq, bins_dev, width = others_ref.shape[0] + 1, own_ref.shape[2], own_ref.shape[3]
-    group = hold.shape[0]
-    bins_time = bins_dev // group
+    frames, bins_dev, width = own_ref.shape
+    freq = others_ref.shape[0] + 1
+    bins_time = bins_dev // hold.shape[0]
     scale = (width // HEADS) ** (-0.5)
-
-    @pl.when(step == 0)
-    def _():
-        hold[...] = gh_ref[...].astype(f32)
-        total[...] = jnp.zeros_like(total)
-        dg_ref[...] = jnp.zeros_like(dg_ref)
-
-    grad_hidden = grad_hidden_rows(place_ref, hold, step, freq, bins_time)
-    grad_hidden_low = grad_hidden.astype(bf16)
-    grad_out = dot_nt(grad_hidden_low, w_ref[3]).astype(bf16)
-    out_spread = spread(grad_out, 1.0)
-    grad_probs = dot_nt(out_spread, v_ref[0])
-    probs = [p_ref[0, h] for h in range(HEADS)]
-    g_v = dot_tn(stacked_low(probs), out_spread).astype(bf16)
-    grad_scores = head_grads(probs, grad_probs, scale)
-    g_q = own_channels(dot(grad_scores, k_ref[0]), freq * bins_dev).astype(bf16)
-    g_k = dot_tn(grad_scores, spread(q_ref[0], 1.0)).astype(bf16)
-    inverse, unit = norm_parts(joined(own_ref, others_ref))
     gain = gain_ref[0:1, :]
-    n = (unit * gain).astype(bf16)
-    total[0] += dot_tn(n, g_q)
-    total[1] += dot_tn(n, g_k)
-    total[2] += dot_tn(n, g_v)
-    total[3] += dot_tn(o_ref[0], grad_hidden_low)
-    g_n = dot_nt(g_q, w_ref[0]) + dot_nt(g_k, w_ref[1]) + dot_nt(g_v, w_ref[2])
-    grad_x = grad_hidden + norm_backward(g_n, inverse, unit, gain)
-    grad_x = grad_x.astype(bf16)
-    gown_ref[0] = grad_x[:bins_dev]
-    gothers_ref[...] = grad_x[bins_dev:].reshape(gothers_ref.shape)
-    dg_ref[...] += jnp.sum(g_n * unit, axis=0, keepdims=True)
-
-    @pl.when(step == pl.num_programs(0) - 1)
-    def _():
-        put_halves(place_ref[1], total, kept_ref, sent_ref)
+    loads = {}
+    for name, source, target in (
+        ("v", v_hbm, v_ref),
+        ("p", p_hbm, p_ref),
+        ("k", k_hbm, k_ref),
+        ("q", q_hbm, q_ref),
+        ("own", x_hbm.at[place_ref[0]], own_ref),
+        ("others", others_hbm, others_ref),
+        ("o", o_hbm, o_ref),
+    ):
+        loads[name] = pltpu.make_async_copy(source, target, sems.at[len(loads)])
+        loads[name].start()
+    hold[...] = gh_ref[...].astype(f32)
+    first = []
+    for f in range(frames):
+        grad_hidden = grad_hidden_rows(place_ref, hold, f, freq, bins_time)
+        low = grad_hidden.astype(bf16)
+        out_spread = spread(dot_nt(low, w_ref[3]).astype(bf16), 1.0)
+        first.append((grad_hidden, low, out_spread))
+    loads["v"].wait()
+    first = [parts + (dot_nt(parts[2], v_ref[f]),) for f, parts in enumerate(first)]
+    loads["p"].wait()
+    second = []
+    for f, (_, _, out_spread, grad_probs) in enumerate(first):
+        probs = [p_ref[f, h].astype(f32) for h in range(HEADS)]
+        g_v = dot_tn(p_ref[f].reshape(-1, p_ref.shape[3]), out_spread).astype(bf16)
+        second.append((g_v, head_grads(probs, grad_probs, scale)))
+    for name in ("k", "q", "own", "others", "o"):
+        loads[name].wait()
+    third = []
+    for f, (g_v, grad_scores) in enumerate(second):
+        g_q = own_channels(dot(grad_scores, k_ref[f]), freq * bins_dev).astype(bf16)
+        g_k = dot_tn(grad_scores, spread(q_ref[f], 1.0)).astype(bf16)
+        third.append((g_q, g_k, g_v))
+    dg_ref[...] = jnp.zeros_like(dg_ref)
+    for f, ((grad_hidden, low, _, _), (g_q, g_k, g_v)) in enumerate(zip(first, third)):
+        inverse, unit = norm_parts(joined(own_ref.at[f], others_ref.at[:, f]))
+        n = (unit * gain).astype(bf16)
+        parts = (dot_tn(n, g_q), dot_tn(n, g_k), dot_tn(n, g_v), dot_tn(o_ref[f], low))
+        for m, part in enumerate(parts):
+            total[m] = part if f == 0 else total[m] + part
+        g_n = dot_nt(g_q, w_ref[0]) + dot_nt(g_k, w_ref[1]) + dot_nt(g_v, w_ref[2])
+        grad_x = (grad_hidden + norm_backward(g_n, inverse, unit, gain)).astype(bf16)
+        gown_ref[f] = grad_x[:bins_dev]
+        gothers_ref[:, f] = grad_x[bins_dev:].reshape(freq - 1, bins_dev, width)
+        dg_ref[...] += jnp.sum(g_n * unit, axis=0, keepdims=True)
+    put_halves(place_ref[1], total, kept_ref, sent_ref)
 
 
 def put_halves(core, total, kept_ref, sent_ref):
@@ -252,9 +266,9 @@
     sent_ref[...] = total[pl.ds((1 - core) * half, half)].astype(bf16)
 
 
-def grad_hidden_rows(place_ref, hold, step, freq, bins_time):
+def grad_hidden_rows(place_ref, hold, frame, freq, bins_time):
     width = hold.shape[-1]
-    rows = pl.ds(pl.multiple_of(step * bins_time, bins_time), bins_time)
+    rows = pl.ds(frame * bins_time, bins_time)
     return jnp.concatenate(
         [hold[:, slot_of(place_ref[0], f, freq), rows, :].reshape(-1, width) for f in range(freq)],
         axis=0,
@@ -264,34 +278,15 @@
 def freq_backward(place, features, others, q, k, v, o, probs, grad_hidden, weights, gains):
     freq, frames, bins_dev, width = features.shape
     bins = freq * bins_dev
-    own_spec, others_spec, row_spec = frame_specs(freq, bins_dev, width)
     flops = frames * 2 * bins * (8 * width * width + 4 * HEADS * bins * width)
     half = (2, width, width)
+    vmem = pl.BlockSpec(memory_space=pltpu.VMEM)
+    hbm = pl.BlockSpec(memory_space=pltpu.HBM)
+    rows = pltpu.VMEM((frames, bins, width), bf16)
     return pl.pallas_call(
         freq_backward_kernel,
-        grid_spec=pltpu.PrefetchScalarGridSpec(
-            num_scalar_prefetch=1,
-            grid=(frames,),
-            in_specs=[own_spec, others_spec]
-            + [row_spec] * 4
-            + [
-                pl.BlockSpec((1, HEADS, bins, bins), lambda i, place: (i, 0, 0, 0)),
-                fixed(grad_hidden.shape),
-                fixed((4, width, width)),
-                fixed(gains.shape),
-            ],
-            out_specs=[
-                pl.BlockSpec((1, bins_dev, width), lambda i, place: (i, 0, 0)),
-                others_spec,
-                fixed(half),
-                fixed(half),
-                fixed((1, width)),
-            ],
-            scratch_shapes=[
-                pltpu.VMEM(grad_hidden.shape, f32),
-                pltpu.VMEM((4, width, width), f32),
-            ],
-        ),
+        in_specs=[pl.BlockSpec(memory_space=pltpu.SMEM)] + [hbm] * 7 + [vmem] * 3,
+        out_specs=[vmem] * 5,
         out_shape=[
             pltpu.VMEM((frames, bins_dev, width), bf16),
             pltpu.VMEM(others.shape, bf16),
@@ -299,13 +294,25 @@
             pltpu.VMEM(half, bf16),
             jax.ShapeDtypeStruct((1, width), f32),
         ],
+        scratch_shapes=[
+            pltpu.VMEM((frames, bins_dev, width), bf16),
+            pltpu.VMEM(others.shape, bf16),
+            rows,
+            rows,
+            rows,
+            rows,
+            pltpu.VMEM(probs.shape, bf16),
+            pltpu.VMEM(grad_hidden.shape, f32),
+            pltpu.VMEM((4, width, width), f32),
+            pltpu.SemaphoreType.DMA((7,)),
+        ],
         compiler_params=pltpu.CompilerParams(vmem_limit_bytes=VMEM_LIMIT),
         cost_estimate=pl.CostEstimate(
             flops=flops, bytes_accessed=8 * 1024 * 1024, transcendentals=0
         ),
         name="freq_backward",
     )(
-        place, features, *map(far, (others, q, k, v, o, probs)), near(grad_hidden),
+        place, *map(far, (features, others, q, k, v, o, probs)), near(grad_hidden),
         near(weights), gains,
     )
 
@@ -345,29 +352,27 @@
         frame = first_ref[0] + key
         allowed = allowed & (frame >= 0) & (frame < total_frames)
 
-    def one_bin(b, carry):
-        rows = pl.ds(b, span, stride=bins)
-        q = get(q_s, rows).astype(bf16)
-        k = get(k_s, rows).astype(bf16)
-        v = get(v_s, rows).astype(bf16)
-        grad_out = get(go_s, rows).astype(bf16)
-        out_spread = spread(grad_out, 1.0)
-        scores = dot_nt(spread(q, scale), k)
-        grad_probs = dot_nt(out_spread, v)
-        probs = head_probs(scores, allowed)
-        low = stacked_low(probs)
-        grad_scores = head_grads(probs, grad_probs, scale)
-        o = own_channels(dot(low, v), span)
-        g_q = own_channels(dot(grad_scores, k), span)
-        g_k = dot_tn(grad_scores, spread(q, 1.0))
-        g_v = dot_tn(low, out_spread)
-        put(o_s, rows, o)
-        put(gq_s, rows, g_q)
-        put(gk_s, rows, g_k)
-        put(gv_s, rows, g_v)
-        return carry
-
-    lax.fori_loop(0, bins, one_bin, 0, unroll=UNROLL)
+    together = max(n for n in (1, 2, 4) if bins % n == 0 and (n == 1 or n * span <= 512))
+
+    def some_bins(start):
+        places = [pl.ds(start + b, span, stride=bins) for b in range(together)]
+        first = []
+        for rows in places:
+            q, k, v, grad_out = (get(ref, rows).astype(bf16) for ref in (q_s, k_s, v_s, go_s))
+            out_spread = spread(grad_out, 1.0)
+            first.append((q, k, v, out_spread, dot_nt(spread(q, scale), k), dot_nt(out_spread, v)))
+        second = []
+        for q, k, v, out_spread, scores, grad_probs in first:
+            probs = head_probs(scores, allowed)
+            second.append((stacked_low(probs), head_grads(probs, grad_probs, scale)))
+        for rows, (q, k, v, out_spread, _, _), (low, grad_scores) in zip(places, first, second):
+            put(o_s, rows, own_channels(dot(low, v), span))
+            put(gq_s, rows, own_channels(dot(grad_scores, k), span))
+            put(gk_s, rows, dot_tn(grad_scores, spread(q, 1.0)))
+            put(gv_s, rows, dot_tn(low, out_spread))
+
+    for start in range(0, bins, together):
+        some_bins(start)
 
     dg_ref[...] = jnp.zeros_like(dg_ref)
     stores = []
@@ -392,9 +397,6 @@
     put_halves(place_ref[1], total, kept_ref, sent_ref)
     for store in stores:
         store.wait()
-
-
-UNROLL = 4
 
 
 def time_attention(place, first, hidden, upstream, weights, gains, bins, own_start, own_rows, total):

time: 126 us -> 123 us (0.976)
  Pallas kernels: 26.4 us -> 22.5 us
    pallas_call x1, Pallas kernels: 8.13 us -> 6.22 us  [freq_backward(): pl.pallas_call(freq_backward_kernel, in_specs=[pl.BlockSpec(memory_space=...]
    pallas_call x1, Pallas kernels: 9.56 us -> 7.81 us  [time_attention(): pl.pallas_call(functools.partial(time_kernel, bins, own_start, total), in...]
  transfers between devices with their start and end apart: 12 -> 12, of which waited for: 8 -> 8; matrix products, arithmetic and copies ran while one was open for 3% -> 3% of each run, Pallas kernels for 13% -> 11%
where the time goes in v6:
time: 123 us; the launch traced here: 122 us
  waiting for transfers between devices  43.7 us (36%)
  starting transfers between devices  27.3 us (22%)
  Pallas kernels  22.5 us (18%)
  blocking collectives  19.9 us (16%)
  local copies, waits for them, and re-layouts  3.92 us (3%)
  other arithmetic  3.7 us (3%)
    all_to_all x1, blocking collectives, over_same(): lax.all_to_all(blocks, ('tm', 'freq'), 0, 0, tiled=True, axis_index_group...  19.9 us
    all_to_all x2, waiting for transfers between devices, over_all(): lax.all_to_all(flat, ('tm', 'freq'), 0, 0, tiled=True).reshape(blocks.shape)  17.1 us
    ppermute x2, waiting for transfers between devices, along_freq(): lax.ppermute(block, 'freq', [(i, (i + steps) % freq) for i in range(freq)])  9.98 us
    pallas_call x1, Pallas kernels, time_attention(): pl.pallas_call(functools.partial(time_kernel, bins, own_start, total), in...  7.81 us
    pallas_call x1, Pallas kernels, freq_forward(): pl.pallas_call(freq_forward_kernel, grid_spec=pltpu.PrefetchScalarGridSpe...  7.63 us
    ppermute x2, waiting for transfers between devices, scattered(): came = lax.ppermute(sent, axis, [(d, d ^ 1 << k) for d in devices])  7.58 us
    all_to_all x1, waiting for transfers between devices, over_tm(): lax.all_to_all(blocks, 'tm', 0, 0, tiled=True, axis_index_groups=groups)  6.66 us
    pallas_call x1, Pallas kernels, freq_backward(): pl.pallas_call(freq_backward_kernel, in_specs=[pl.BlockSpec(memory_space=...  6.22 us
  transfers between devices with their start and end apart: 12, of which 8 were waited for; matrix products, arithmetic and copies ran while one was open for 3% of the time, Pallas kernels for 11%

profile of v6, /device:TPU:0, one launch (start us, length us, event | category | flops | bytes accessed | tf_op | source)
XLA Modules:
  0.0 122.1 jit_solution(12477735798811976719)
XLA Ops:
  0.7 1.8 %dynamic-slice_bitcast_fusion = bf16[4,128,256]{2,1,0:T(8,128)(2,1)} fusion(bf16[2,4,128,256]{3,2,1,0:T(8,128)(2,1)} %bitcast.50, s32[]{:T(128)S(6)} %select_n.59), kind=kLoop, calls=%fused_computation.20 | loop fusion | bytes 524292 | tf_op jit(solution)/shard_map/jit(dynamic_index_in_dim)/squeeze | solution.py:530
  2.5 3.0 %collective-permute-start = (bf16[4,128,256]{2,1,0:T(8,128)(2,1)}, bf16[4,128,256]{2,1,0:T(8,128)(2,1)S(1)}, u32[]{:S(2)}, u32[]{:S(2)}) collective-permute-start(bf16[4,128,256]{2,1,0:T(8,128)(2,1)} %dynamic-slice_bitcast_fusion), channel_id=1, source_target_pairs={{0,1},{1,0},{2,3},{3,2},{4,5},{5,4},{6,7},{7,6},{8,9},{9,8},{10,11... | collective-permute-start | bytes 786440 | tf_op jit(solution)/shard_map/ppermute | solution.py:526
  6.3 5.9 %all-to-all-start.1 = ((bf16[16,8,8,256]{3,2,1,0:T(8,128)(2,1)}), bf16[16,8,8,256]{3,2,1,0:T(8,128)(2,1)S(1)}, u32[]{:S(2)}, u32[]{:S(2)}) async-start(bf16[16,8,8,256]{3,2,1,0:T(8,128)(2,1)} %copy_bitcast_fusion), calls=%async_computation.1 | async-start | bytes 1048576 | tf_op jit(solution)/shard_map/all_to_all | solution.py:504
  12.4 7.6 %freq_forward.1 = (bf16[4,256,256]{2,1,0:T(8,128)(2,1)}, bf16[4,256,256]{2,1,0:T(8,128)(2,1)}, bf16[4,256,256]{2,1,0:T(8,128)(2,1)}, bf16[4,256,256]{2,1,0:T(8,1...) custom-call(s32[2]{0:T(128)S(1)} %pad_add_fusion.place_ref, ...), custom_call_target="tpu_custom_call" | custom-call | flops 64424509440 | bytes 2097152 | tf_op jit(solution)/shard_map/freq_forward/pallas_call | solution.py:175
  20.0 6.7 %all-to-all-done.1 = bf16[16,8,8,256]{3,2,1,0:T(8,128)(2,1)S(1)} async-done(((bf16[16,8,8,256]{3,2,1,0:T(8,128)(2,1)}), bf16[16,8,8,256]{3,2,1,0:T(8,128)(2,1)S(1)}, u32[]{:S(2)}, u32[]{:S(2)}) %all-to-all-start.1) | async-done | bytes 524320 | tf_op jit(solution)/shard_map/all_to_all | solution.py:504
  26.7 3.1 %all-to-all-start = ((bf16[32,32,256]{2,1,0:T(8,128)(2,1)}), bf16[32,32,256]{2,1,0:T(8,128)(2,1)S(1)}, u32[]{:S(2)}, u32[]{:S(2)}) async-start(bf16[32,32,256]{2,1,0:T(8,128)(2,1)} %bitcast.61), calls=%async_computation | async-start | bytes 1048576 | tf_op jit(solution)/shard_map/all_to_all | solution.py:509
  29.8 1.1 slice.29.w_ref
  30.9 13.9 %all-to-all-done = bf16[32,32,256]{2,1,0:T(8,128)(2,1)S(1)} async-done(((bf16[32,32,256]{2,1,0:T(8,128)(2,1)}), bf16[32,32,256]{2,1,0:T(8,128)(2,1)S(1)}, u32[]{:S(2)}, u32[]{:S(2)}) %all-to-all-start) | async-done | bytes 524320 | tf_op jit(solution)/shard_map/all_to_all | solution.py:509
  44.8 7.8 %time_attention.1 = (bf16[1024,256]{1,0:T(8,128)(2,1)}, bf16[2,256,256]{2,1,0:T(8,128)(2,1)S(1)}, bf16[2,256,256]{2,1,0:T(8,128)(2,1)S(1)}, f32[1,256]{1,0:T(1,128)S(1)}) custom-call(s32[2]{0:T(128)S(1)} %pad_add_fusion.place_ref, s32[1]{0:T(128)} %bitcast.5.first_ref, bf16[1024,256]{1,0:T(8,128)(2,1)S(1)} %bitcast.48, bf16[1024,256]{1,0:T(8,128)(2,1)S(1)} %bitcast.46, ...), custom_call_target="tpu_custom_call" | custom-call | flops 3087007744 | bytes 4194304 | tf_op jit(solution)/shard_map/time_attention/pallas_call | solution.py:409
  52.6 1.1 collective-permute-start.3
  53.8 2.8 %all-to-all-start.2 = ((bf16[32,32,256]{2,1,0:T(8,128)(2,1)}), bf16[32,32,256]{2,1,0:T(8,128)(2,1)S(1)}, u32[]{:S(2)}, u32[]{:S(2)}) async-start(bf16[32,32,256]{2,1,0:T(8,128)(2,1)} %bitcast.60), calls=%async_computation.2 | async-start | bytes 1048576 | tf_op jit(solution)/shard_map/all_to_all | solution.py:509
  56.7 1.7 %collective-permute-start.4 = (bf16[2,128,256]{2,1,0:T(8,128)(2,1)S(1)}, bf16[2,128,256]{2,1,0:T(8,128)(2,1)S(1)}, u32[]{:S(2)}, u32[]{:S(2)}) collective-permute-start(bf16[2,128,256]{2,1,0:T(8,128)(2,1)S(1)} %dynamic-slice_bitcast_fusion.1), channel_id=1, source_target_pairs={{0,4},{2,6},{4,0},{6,2},{8,12},{10,14},{12,8},{14,10},{16,20},{18,... | collective-permute-start | bytes 393224 | tf_op jit(solution)/shard_map/ppermute | solution.py:578
  58.4 7.6 %collective-permute-done.4 = bf16[2,128,256]{2,1,0:T(8,128)(2,1)S(1)} collective-permute-done((bf16[2,128,256]{2,1,0:T(8,128)(2,1)S(1)}, bf16[2,128,256]{2,1,0:T(8,128)(2,1)S(1)}, u32[]{:S(2)}, u32[]{:S(2)}) %collective-permute-start.4) | collective-permute-done | bytes 131104 | tf_op jit(solution)/shard_map/ppermute | solution.py:578
  66.0 2.2 %collective-permute-start.5 = (bf16[128,256]{1,0:T(8,128)(2,1)S(1)}, bf16[128,256]{1,0:T(8,128)(2,1)S(1)}, u32[]{:S(2)}, u32[]{:S(2)}) collective-permute-start(bf16[128,256]{1,0:T(8,128)(2,1)S(1)} %dynamic-slice_bitcast_fusion.2), channel_id=1, source_target_pairs={{0,1},{1,0},{2,3},{3,2},{4,5},{5,4},{6,7},{7,6},{8,9},{9,8},{10,11... | collective-permute-start | bytes 196616 | tf_op jit(solution)/shard_map/ppermute | solution.py:578
  68.3 3.2 %all-to-all-done.2 = bf16[32,32,256]{2,1,0:T(8,128)(2,1)S(1)} async-done(((bf16[32,32,256]{2,1,0:T(8,128)(2,1)}), bf16[32,32,256]{2,1,0:T(8,128)(2,1)S(1)}, u32[]{:S(2)}, u32[]{:S(2)}) %all-to-all-start.2) | async-done | bytes 524320 | tf_op jit(solution)/shard_map/all_to_all | solution.py:509
  71.4 6.2 %freq_backward.1 = (bf16[4,128,256]{2,1,0:T(8,128)(2,1)S(1)}, bf16[1,4,128,256]{3,2,1,0:T(8,128)(2,1)S(1)}, bf16[2,256,256]{2,1,0:T(8,128)(2,1)S(1)}, bf16[2,256,256]{2,1,0:T(8,128)(2,1)S(1)}, f32[1,256]{1,0:T(1,128)S(1)}) custom-call(s32[2]{0:T(128)S(1)} %pad_add_fusion.place_ref, bf16[2,4,128,256]{3,2,1,0:T(8,128)(2,1)} %bitcast.51, ...), custom_call_target="tpu_custom_call" | custom-call | flops 3221225472 | bytes 8388608 | tf_op jit(solution)/shard_map/freq_backward/pallas_call | solution.py:286
  77.7 1.1 collective-permute-start.2
  78.8 1.1 collective-permute-done.2.arrived_ref
  80.8 3.9 %all-to-all-start.3 = ((bf16[16,48,256]{2,1,0:T(8,128)(2,1)}), bf16[16,48,256]{2,1,0:T(8,128)(2,1)S(1)}, u32[]{:S(2)}, u32[]{:S(2)}) async-start(bf16[16,48,256]{2,1,0:T(8,128)(2,1)} %sums_by_peer.1), calls=%async_computation.3 | async-start | bytes 786432 | tf_op jit(solution)/shard_map/all_to_all | solution.py:583
  84.8 1.9 %collective-permute-start.1 = (bf16[4,128,256]{2,1,0:T(8,128)(2,1)S(1)}, bf16[4,128,256]{2,1,0:T(8,128)(2,1)S(1)}, u32[]{:S(2)}, u32[]{:S(2)}) collective-permute-start(bf16[4,128,256]{2,1,0:T(8,128)(2,1)S(1)} %bitcast.55), channel_id=1, source_target_pairs={{0,1},{1,0},{2,3},{3,2},{4,5},{5,4},{6,7},{7,6},{8,9},{9,8},{10,11... | collective-permute-start | bytes 786440 | tf_op jit(solution)/shard_map/ppermute | solution.py:526
  86.7 10.0 %collective-permute-done.1 = bf16[4,128,256]{2,1,0:T(8,128)(2,1)S(1)} collective-permute-done((bf16[4,128,256]{2,1,0:T(8,128)(2,1)S(1)}, bf16[4,128,256]{2,1,0:T(8,128)(2,1)S(1)}, u32[]{:S(2)}, u32[]{:S(2)}) %collective-permute-start.1) | collective-permute-done | bytes 262176 | tf_op jit(solution)/shard_map/ppermute | solution.py:526
  97.9 19.9 %all_to_all.25 = bf16[16,64,256]{2,1,0:T(8,128)(2,1)S(1)} all-to-all(bf16[16,64,256]{2,1,0:T(8,128)(2,1)S(1)} %broadcast_in_dim.2), channel_id=1, replica_groups={{0,1,4,5,8,9,12,13,16,17,20,21,24,25,28,29},{2,3,6,7,10,11,14,15,18,19,..., dimensions={0} | all-to-all | bytes 1048576 | tf_op jit(solution)/shard_map/all_to_all | solution.py:583
  118.4 1.2 fusion.3
  120.6 1.5 %maximum_convert_fusion = f32[8,256,256]{2,1,0:T(8,128)} fusion(bf16[4,256,256]{2,1,0:T(8,128)(2,1)S(1)} %bitcast.56, bf16[4,256,256]{2,1,0:T(8,128)(2,1)S(1)} %bitcast.57), kind=kLoop, calls=%fused_computation.6 | loop fusion | flops 1048576 | bytes 3145728 | tf_op jit(solution)/shard_map/convert_element_type | solution.py:620
  (40 shorter events, 4.8 us)
Async XLA Ops:
  0.6 4.8 %copy-start = (bf16[8,128,256]{2,1,0:T(8,128)(2,1)S(1)}, bf16[8,128,256]{2,1,0:T(8,128)(2,1)}, u32[]{:S(2)}) copy-start(bf16[8,128,256]{2,1,0:T(8,128)(2,1)} %param.5) | copy-start | bytes 1572868
  0.6 11.7 %copy-start.1 = (bf16[8,128,256]{2,1,0:T(8,128)(2,1)S(1)}, bf16[8,128,256]{2,1,0:T(8,128)(2,1)}, u32[]{:S(2)}) copy-start(bf16[8,128,256]{2,1,0:T(8,128)(2,1)} %param.4) | copy-start | bytes 1572868
  0.7 11.6 %copy-start.4 = (bf16[8,256,256]{2,1,0:T(8,128)(2,1)S(1)}, bf16[8,256,256]{2,1,0:T(8,128)(2,1)}, u32[]{:S(2)}) copy-start(bf16[8,256,256]{2,1,0:T(8,128)(2,1)} %param.6) | copy-start | bytes 3145732
  0.7 11.7 %copy-start.3 = (f32[2,256]{1,0:T(2,128)S(1)}, f32[2,256]{1,0:T(2,128)}, u32[]{:S(2)}) copy-start(f32[2,256]{1,0:T(2,128)} %gain_ref.5) | copy-start | bytes 6148
  2.5 9.9 %collective-permute-start = (bf16[4,128,256]{2,1,0:T(8,128)(2,1)}, bf16[4,128,256]{2,1,0:T(8,128)(2,1)S(1)}, u32[]{:S(2)}, u32[]{:S(2)}) collective-permute-start(bf16[4,128,256]{2,1,0:T(8,128)(2,1)} %dynamic-slice_bitcast_fusion), channel_id=1, source_target_pairs={{0,1},{1,0},{2,3},{3,2},{4,5},{5,4},{6,7},{7,6},{8,9},{9,8},{10,11... | collective-permute-start | bytes 786440 | tf_op jit(solution)/shard_map/ppermute | solution.py:526
  6.3 20.4 %all-to-all-start.1 = ((bf16[16,8,8,256]{3,2,1,0:T(8,128)(2,1)}), bf16[16,8,8,256]{3,2,1,0:T(8,128)(2,1)S(1)}, u32[]{:S(2)}, u32[]{:S(2)}) async-start(bf16[16,8,8,256]{3,2,1,0:T(8,128)(2,1)} %copy_bitcast_fusion), calls=%async_computation.1 | async-start | bytes 1048576 | tf_op jit(solution)/shard_map/all_to_all | solution.py:504
  12.4 7.6 %copy-start.2 = (bf16[4,128,256]{2,1,0:T(8,128)(2,1)}, bf16[4,128,256]{2,1,0:T(8,128)(2,1)S(1)}, u32[]{:S(2)}) copy-start(bf16[4,128,256]{2,1,0:T(8,128)(2,1)S(1)} %collective-permute-done) | copy-start | bytes 786436
  26.7 18.1 %all-to-all-start = ((bf16[32,32,256]{2,1,0:T(8,128)(2,1)}), bf16[32,32,256]{2,1,0:T(8,128)(2,1)S(1)}, u32[]{:S(2)}, u32[]{:S(2)}) async-start(bf16[32,32,256]{2,1,0:T(8,128)(2,1)} %bitcast.61), calls=%async_computation | async-start | bytes 1048576 | tf_op jit(solution)/shard_map/all_to_all | solution.py:509
  52.6 4.0 %collective-permute-start.3 = (bf16[2,256,256]{2,1,0:T(8,128)(2,1)S(1)}, bf16[2,256,256]{2,1,0:T(8,128)(2,1)S(1)}, u32[]{:S(2)}, u32[]{:S(2)}) collective-permute-start(bf16[2,256,256]{2,1,0:T(8,128)(2,1)S(1)} %get-tuple-element.41), channel_id=1, source_target_pairs={{0,2},{2,0},{4,6},{6,4},{8,10},{10,8},{12,14},{14,12},{16,18},{18,... | collective-permute-start | bytes 786440 | tf_op jit(solution)/shard_map/ppermute | solution.py:587
  53.8 17.7 %all-to-all-start.2 = ((bf16[32,32,256]{2,1,0:T(8,128)(2,1)}), bf16[32,32,256]{2,1,0:T(8,128)(2,1)S(1)}, u32[]{:S(2)}, u32[]{:S(2)}) async-start(bf16[32,32,256]{2,1,0:T(8,128)(2,1)} %bitcast.60), calls=%async_computation.2 | async-start | bytes 1048576 | tf_op jit(solution)/shard_map/all_to_all | solution.py:509
  56.7 9.2 %collective-permute-start.4 = (bf16[2,128,256]{2,1,0:T(8,128)(2,1)S(1)}, bf16[2,128,256]{2,1,0:T(8,128)(2,1)S(1)}, u32[]{:S(2)}, u32[]{:S(2)}) collective-permute-start(bf16[2,128,256]{2,1,0:T(8,128)(2,1)S(1)} %dynamic-slice_bitcast_fusion.1), channel_id=1, source_target_pairs={{0,4},{2,6},{4,0},{6,2},{8,12},{10,14},{12,8},{14,10},{16,20},{18,... | collective-permute-start | bytes 393224 | tf_op jit(solution)/shard_map/ppermute | solution.py:578
  66.0 12.8 %collective-permute-start.5 = (bf16[128,256]{1,0:T(8,128)(2,1)S(1)}, bf16[128,256]{1,0:T(8,128)(2,1)S(1)}, u32[]{:S(2)}, u32[]{:S(2)}) collective-permute-start(bf16[128,256]{1,0:T(8,128)(2,1)S(1)} %dynamic-slice_bitcast_fusion.2), channel_id=1, source_target_pairs={{0,1},{1,0},{2,3},{3,2},{4,5},{5,4},{6,7},{7,6},{8,9},{9,8},{10,11... | collective-permute-start | bytes 196616 | tf_op jit(solution)/shard_map/ppermute | solution.py:578
  77.7 2.3 %collective-permute-start.2 = (bf16[2,256,256]{2,1,0:T(8,128)(2,1)S(1)}, bf16[2,256,256]{2,1,0:T(8,128)(2,1)S(1)}, u32[]{:S(2)}, u32[]{:S(2)}) collective-permute-start(bf16[2,256,256]{2,1,0:T(8,128)(2,1)S(1)} %get-tuple-element.39), channel_id=1, source_target_pairs={{0,2},{2,0},{4,6},{6,4},{8,10},{10,8},{12,14},{14,12},{16,18},{18,... | collective-permute-start | bytes 786440 | tf_op jit(solution)/shard_map/ppermute | solution.py:592
  80.8 16.9 %all-to-all-start.3 = ((bf16[16,48,256]{2,1,0:T(8,128)(2,1)}), bf16[16,48,256]{2,1,0:T(8,128)(2,1)S(1)}, u32[]{:S(2)}, u32[]{:S(2)}) async-start(bf16[16,48,256]{2,1,0:T(8,128)(2,1)} %sums_by_peer.1), calls=%async_computation.3 | async-start | bytes 786432 | tf_op jit(solution)/shard_map/all_to_all | solution.py:583
  84.8 11.9 %collective-permute-start.1 = (bf16[4,128,256]{2,1,0:T(8,128)(2,1)S(1)}, bf16[4,128,256]{2,1,0:T(8,128)(2,1)S(1)}, u32[]{:S(2)}, u32[]{:S(2)}) collective-permute-start(bf16[4,128,256]{2,1,0:T(8,128)(2,1)S(1)} %bitcast.55), channel_id=1, source_target_pairs={{0,1},{1,0},{2,3},{3,2},{4,5},{5,4},{6,7},{7,6},{8,9},{9,8},{10,11... | collective-permute-start | bytes 786440 | tf_op jit(solution)/shard_map/ppermute | solution.py:526
  117.8 2.5 %collective-permute-start.6 = (bf16[16,64,256]{2,1,0:T(8,128)(2,1)S(1)}, bf16[16,64,256]{2,1,0:T(8,128)(2,1)S(1)}, u32[]{:S(2)}, u32[]{:S(2)}) collective-permute-start(bf16[16,64,256]{2,1,0:T(8,128)(2,1)S(1)} %all_to_all.25), channel_id=1, source_target_pairs={{0,2},{2,0},{4,6},{6,4},{8,10},{10,8},{12,14},{14,12},{16,18},{18,... | collective-permute-start | bytes 1572872 | tf_op jit(solution)/shard_map/ppermute | solution.py:612
  117.9 1.9 %collective-permute-start.7 = (f32[2,256]{1,0:T(2,128)S(1)}, f32[2,256]{1,0:T(2,128)S(1)}, u32[]{:S(2)}, u32[]{:S(2)}) collective-permute-start(f32[2,256]{1,0:T(2,128)S(1)} %slice_add_fusion), channel_id=1, source_target_pairs={{0,2},{2,0},{4,6},{6,4},{8,10},{10,8},{12,14},{14,12},{16,18},{18,... | collective-permute-start | bytes 6152 | tf_op jit(solution)/shard_map/ppermute | solution.py:611

commit v7 on v6

--- a/solution.py
+++ b/solution.py
@@ -16,6 +16,7 @@
 f32 = jnp.float32
 bf16 = jnp.bfloat16
 LANES = 128
+GAIN_ROWS = 16
 MIB = 1024 * 1024
 VMEM_LIMIT = 24 * MIB
 FORWARD_WEIGHT = 40
@@ -100,6 +101,31 @@
 
 def slot_of(position, back, freq):
     return lax.rem(position - back + freq, freq)
+
+
+def pick_kernel(x_hbm, out_ref, sems):
+    freq = x_hbm.shape[0]
+    place = lax.axis_index("freq")
+    copies = [
+        pltpu.make_async_copy(x_hbm.at[lax.rem(place + j, freq)], out_ref.at[j - 1], sems.at[j - 1])
+        for j in range(1, freq)
+    ]
+    for copy in copies:
+        copy.start()
+    for copy in copies:
+        copy.wait()
+
+
+def pick_others(features):
+    freq = features.shape[0]
+    return pl.pallas_call(
+        pick_kernel,
+        in_specs=[pl.BlockSpec(memory_space=pltpu.HBM)],
+        out_specs=pl.BlockSpec(memory_space=pltpu.VMEM),
+        out_shape=pltpu.VMEM((freq - 1,) + features.shape[1:], bf16),
+        scratch_shapes=[pltpu.SemaphoreType.DMA((freq - 1,))],
+        name="pick_others",
+    )(far(features))
 
 
 def freq_forward_kernel(
@@ -203,7 +229,7 @@
 
 def freq_backward_kernel(
     place_ref, x_hbm, others_hbm, q_hbm, k_hbm, v_hbm, o_hbm, p_hbm, gh_ref, w_ref, gain_ref,
-    gown_ref, gothers_ref, kept_ref, sent_ref, dg_ref,
+    time_dg_ref, gown_ref, gothers_ref, kept_ref, sent_ref, gains_ref,
     own_ref, others_ref, q_ref, k_ref, v_ref, o_ref, p_ref, hold, total, sems
 ):
     frames, bins_dev, width = own_ref.shape
@@ -245,7 +271,7 @@
         g_q = own_channels(dot(grad_scores, k_ref[f]), freq * bins_dev).astype(bf16)
         g_k = dot_tn(grad_scores, spread(q_ref[f], 1.0)).astype(bf16)
         third.append((g_q, g_k, g_v))
-    dg_ref[...] = jnp.zeros_like(dg_ref)
+    gains_ref[...] = jnp.zeros_like(gains_ref)
     for f, ((grad_hidden, low, _, _), (g_q, g_k, g_v)) in enumerate(zip(first, third)):
         inverse, unit = norm_parts(joined(own_ref.at[f], others_ref.at[:, f]))
         n = (unit * gain).astype(bf16)
@@ -256,8 +282,16 @@
         grad_x = (grad_hidden + norm_backward(g_n, inverse, unit, gain)).astype(bf16)
         gown_ref[f] = grad_x[:bins_dev]
         gothers_ref[:, f] = grad_x[bins_dev:].reshape(freq - 1, bins_dev, width)
-        dg_ref[...] += jnp.sum(g_n * unit, axis=0, keepdims=True)
-    put_halves(place_ref[1], total, kept_ref, sent_ref)
+        gains_ref[0:1] += jnp.sum(g_n * unit, axis=0, keepdims=True)
+    gains_ref[1:2] = time_dg_ref[...]
+    gains = gains_ref[0:2]
+    high = gains.astype(bf16).astype(f32)
+    gains_ref[0:2] = high
+    gains_ref[2:4] = gains - high
+    matrices = kept_ref.shape[0]
+    kept_ref[...] = total[pl.ds(place_ref[1] * matrices, matrices)].astype(bf16)
+    sent = total[pl.ds((1 - place_ref[1]) * matrices, matrices)].reshape(-1, width)
+    sent_ref[...] = jnp.concatenate([sent, gains_ref[...]], axis=0).astype(bf16)
 
 
 def put_halves(core, total, kept_ref, sent_ref):
@@ -275,7 +309,9 @@
     )
 
 
-def freq_backward(place, features, others, q, k, v, o, probs, grad_hidden, weights, gains):
+def freq_backward(
+    place, features, others, q, k, v, o, probs, grad_hidden, weights, gains, time_dg
+):
     freq, frames, bins_dev, width = features.shape
     bins = freq * bins_dev
     flops = frames * 2 * bins * (8 * width * width + 4 * HEADS * bins * width)
@@ -285,14 +321,14 @@
     rows = pltpu.VMEM((frames, bins, width), bf16)
     return pl.pallas_call(
         freq_backward_kernel,
-        in_specs=[pl.BlockSpec(memory_space=pltpu.SMEM)] + [hbm] * 7 + [vmem] * 3,
+        in_specs=[pl.BlockSpec(memory_space=pltpu.SMEM)] + [hbm] * 7 + [vmem] * 4,
         out_specs=[vmem] * 5,
         out_shape=[
             pltpu.VMEM((frames, bins_dev, width), bf16),
             pltpu.VMEM(others.shape, bf16),
             pltpu.VMEM(half, bf16),
-            pltpu.VMEM(half, bf16),
-            jax.ShapeDtypeStruct((1, width), f32),
+            pltpu.VMEM((2 * width + GAIN_ROWS, width), bf16),
+            pltpu.VMEM((GAIN_ROWS, width), f32),
         ],
         scratch_shapes=[
             pltpu.VMEM((frames, bins_dev, width), bf16),
@@ -313,7 +349,7 @@
         name="freq_backward",
     )(
         place, *map(far, (features, others, q, k, v, o, probs)), near(grad_hidden),
-        near(weights), gains,
+        near(weights), gains, time_dg,
     )
 
 
@@ -429,33 +465,30 @@
     )(place, first, near(hidden), near(upstream), near(weights), gains)
 
 
-def sums_kernel(kept_ref, arrived_ref, time_ref, freq_gain_ref, time_gain_ref, out_ref, gain_rows):
+def sums_kernel(kept_ref, arrived_ref, time_ref, gains_ref, out_ref):
     peers, _, width = out_ref.shape
-    total = kept_ref[...].astype(f32) + arrived_ref[...].astype(f32)
-    gain_rows[...] = jnp.zeros_like(gain_rows)
-    for m, ref in enumerate((freq_gain_ref, time_gain_ref)):
-        high = ref[...].astype(bf16).astype(f32)
-        gain_rows[m : m + 1] = high
-        gain_rows[m + 2 : m + 3] = ref[...] - high
+    arrived = arrived_ref[...].astype(f32)
+    rows = arrived.shape[0] - gains_ref.shape[0]
+    total = kept_ref[...].astype(f32).reshape(rows, width) + arrived[:rows]
+    gains = jnp.concatenate([gains_ref[0:4], arrived[rows : rows + 4]], axis=0)
     parts = [
         total.reshape(peers, -1, width),
         time_ref[...].astype(f32).reshape(peers, -1, width),
-        jnp.broadcast_to(gain_rows[...][None], (peers,) + gain_rows.shape),
+        jnp.broadcast_to(gains[None], (peers,) + gains.shape),
     ]
     out_ref[...] = jnp.concatenate(parts, axis=1).astype(bf16)
 
 
-def sums_by_peer(kept, arrived, time_rows, freq_gain, time_gain, peers):
+def sums_by_peer(kept, arrived, time_rows, gains, peers):
     width = kept.shape[-1]
     freq_count = kept.size // (peers * width)
     time_count = time_rows.size // (peers * width)
     if freq_count % 8 or time_count % 8:
-        total = (kept.astype(f32) + arrived.astype(f32)).astype(bf16)
-        gains = jnp.concatenate([freq_gain, time_gain], axis=0)
-        high = gains.astype(bf16)
-        gains = jnp.concatenate([high, (gains - high.astype(f32)).astype(bf16)], axis=0)
+        rows = 2 * width
+        total = kept.astype(f32).reshape(rows, width) + arrived[:rows].astype(f32)
+        gains = jnp.concatenate([gains[:4].astype(bf16), arrived[rows : rows + 4]], axis=0)
         parts = [
-            total.reshape(peers, -1, width),
+            total.astype(bf16).reshape(peers, -1, width),
             time_rows.reshape(peers, -1, width),
             jnp.broadcast_to(gains[None], (peers,) + gains.shape),
         ]
@@ -463,16 +496,15 @@
     vmem = pl.BlockSpec(memory_space=pltpu.VMEM)
     sums = pl.pallas_call(
         sums_kernel,
-        in_specs=[vmem] * 5,
+        in_specs=[vmem] * 4,
         out_specs=vmem,
         out_shape=pltpu.HBM((peers, freq_count + time_count + 8, width), bf16),
-        scratch_shapes=[pltpu.VMEM((8, width), f32)],
         compiler_params=pltpu.CompilerParams(vmem_limit_bytes=VMEM_LIMIT),
         cost_estimate=pl.CostEstimate(
             flops=kept.size, bytes_accessed=6 * kept.size, transcendentals=0
         ),
         name="sums_by_peer",
-    )(kept, arrived, time_rows, freq_gain, time_gain)
+    )(kept, arrived, time_rows, gains)
     return sums, freq_count, time_count
 
 
@@ -525,10 +557,10 @@
     def along_freq(block, steps):
         return lax.ppermute(block, "freq", [(i, (i + steps) % freq) for i in range(freq)])
 
+    picked = pick_others(by_target)
     others = jnp.stack(
         [
-            along_freq(lax.dynamic_index_in_dim(by_target, (place[0] + j) % freq, 0, False), j)
-            for j in range(1, freq)
+            along_freq(picked[j - 1], j) for j in range(1, freq)
         ]
     )
     up_blocks = jnp.swapaxes(upstream.reshape(frames_dev, group, bins_time, width), 0, 1)
@@ -586,12 +618,12 @@
 
     time_arrived = lax.ppermute(time_sent, "tm", pairs)
     time_rows = scattered((time_kept.astype(f32) + time_arrived.astype(f32)).astype(bf16))
-    grad_own, grad_others, freq_kept, freq_sent, freq_dg = freq_backward(
-        place, by_target, others, q, k, v, o, probs, grad_hidden, freq_w, gains
+    grad_own, grad_others, freq_kept, freq_sent, own_gains = freq_backward(
+        place, by_target, others, q, k, v, o, probs, grad_hidden, freq_w, gains, time_dg
     )
     freq_arrived = lax.ppermute(freq_sent, "tm", pairs)
     sums, freq_count, time_count = sums_by_peer(
-        freq_kept, freq_arrived, time_rows, freq_dg, time_dg, peers
+        freq_kept, freq_arrived, time_rows, own_gains, peers
     )
     arrived = over_same(sums)
     returned = [grad_own] + [along_freq(grad_others[j - 1], -j) for j in range(1, freq)]
@@ -601,14 +633,13 @@
     inv_root = (total_frames * bins_dev * freq) ** (-0.5)
     summed = jnp.sum(arrived.astype(f32), axis=0) * inv_root
     gain_sum = summed[freq_count + time_count :]
-    gain_sum = gain_sum[:2] + gain_sum[2:4]
     time_arrived = arrived[:, freq_count : freq_count + time_count].astype(f32)
     time_sum = jnp.sum(time_arrived.reshape(-1, sets, time_count, width), axis=0) * inv_root
     block = jnp.concatenate([summed[:freq_count], time_sum.reshape(-1, width)], axis=0)
     block, gain_sum = lax.optimization_barrier((block.astype(bf16), gain_sum))
     gathered = over_same(jnp.broadcast_to(block[None], (peers,) + block.shape))
     gathered, gain_sum = lax.optimization_barrier((gathered, gain_sum))
-    gain_grads = gain_sum + lax.ppermute(gain_sum, "tm", pairs)
+    gain_grads = jnp.sum(gain_sum.reshape(4, 2, width), axis=0)
     theirs = lax.ppermute(gathered, "tm", pairs)
     first_core = core == 0
     halves = jnp.stack(

time: 123 us -> 121 us (0.984)
    squeeze x1 -> x0, local copies, waits for them, and re-layouts: 1.81 us -> none  [per_device(): lax.dynamic_index_in_dim(by_target, (place[0] + j) % freq, 0, False)]
  transfers between devices with their start and end apart: 12 -> 11, of which waited for: 8 -> 8; matrix products, arithmetic and copies ran while one was open for 3% -> 4% of each run, Pallas kernels for 11% -> 11%
where the time goes in v7:
time: 121 us
  waiting for transfers between devices  42.6 us (35%)
  starting transfers between devices  26.9 us (22%)
  Pallas kernels  23.5 us (19%)
  blocking collectives  19.9 us (16%)
  other arithmetic  3.71 us (3%)
  local copies, waits for them, and re-layouts  3.17 us (3%)
    all_to_all x1, blocking collectives, over_same(): lax.all_to_all(blocks, ('tm', 'freq'), 0, 0, tiled=True, axis_index_group...  19.9 us
    all_to_all x2, waiting for transfers between devices, over_all(): lax.all_to_all(flat, ('tm', 'freq'), 0, 0, tiled=True).reshape(blocks.shape)  17.1 us
    ppermute x2, waiting for transfers between devices, along_freq(): lax.ppermute(block, 'freq', [(i, (i + steps) % freq) for i in range(freq)])  9.98 us
    pallas_call x1, Pallas kernels, time_attention(): pl.pallas_call(functools.partial(time_kernel, bins, own_start, total), in...  7.78 us
    pallas_call x1, Pallas kernels, freq_forward(): pl.pallas_call(freq_forward_kernel, grid_spec=pltpu.PrefetchScalarGridSpe...  7.63 us
    ppermute x2, waiting for transfers between devices, scattered(): came = lax.ppermute(sent, axis, [(d, d ^ 1 << k) for d in devices])  7.58 us
    pallas_call x1, Pallas kernels, freq_backward(): pl.pallas_call(freq_backward_kernel, in_specs=[pl.BlockSpec(memory_space=...  6.22 us
    all_to_all x2, starting transfers between devices, over_all(): lax.all_to_all(flat, ('tm', 'freq'), 0, 0, tiled=True).reshape(blocks.shape)  5.93 us
  transfers between devices with their start and end apart: 11, of which 8 were waited for; matrix products, arithmetic and copies ran while one was open for 4% of the time, Pallas kernels for 11%

profile of v7, /device:TPU:0, one launch (start us, length us, event | category | flops | bytes accessed | tf_op | source)
XLA Modules:
  0.0 120.7 jit_solution(1559231947456820760)
XLA Ops:
  1.7 3.0 %collective-permute-start = (bf16[4,128,256]{2,1,0:T(8,128)(2,1)S(1)}, bf16[4,128,256]{2,1,0:T(8,128)(2,1)S(1)}, u32[]{:S(2)}, u32[]{:S(2)}) collective-permute-start(bf16[4,128,256]{2,1,0:T(8,128)(2,1)S(1)} %bitcast.51), channel_id=1, source_target_pairs={{0,1},{1,0},{2,3},{3,2},{4,5},{5,4},{6,7},{7,6},{8,9},{9,8},{10,11... | collective-permute-start | bytes 786440 | tf_op jit(solution)/shard_map/ppermute | solution.py:558
  5.6 5.9 %all-to-all-start.1 = ((bf16[16,8,8,256]{3,2,1,0:T(8,128)(2,1)}), bf16[16,8,8,256]{3,2,1,0:T(8,128)(2,1)S(1)}, u32[]{:S(2)}, u32[]{:S(2)}) async-start(bf16[16,8,8,256]{3,2,1,0:T(8,128)(2,1)} %copy_bitcast_fusion), calls=%async_computation.1 | async-start | bytes 1048576 | tf_op jit(solution)/shard_map/all_to_all | solution.py:536
  11.5 1.1 slice.22.w_ref
  12.7 7.6 %freq_forward.1 = (bf16[4,256,256]{2,1,0:T(8,128)(2,1)}, bf16[4,256,256]{2,1,0:T(8,128)(2,1)}, bf16[4,256,256]{2,1,0:T(8,128)(2,1)}, bf16[4,256,256]{2,1,0:T(8,1...) custom-call(s32[2]{0:T(128)S(1)} %pad_add_fusion.place_ref, ...), custom_call_target="tpu_custom_call" | custom-call | flops 64424509440 | bytes 2097152 | tf_op jit(solution)/shard_map/freq_forward/pallas_call | solution.py:201
  20.4 5.6 %all-to-all-done.1 = bf16[16,8,8,256]{3,2,1,0:T(8,128)(2,1)S(1)} async-done(((bf16[16,8,8,256]{3,2,1,0:T(8,128)(2,1)}), bf16[16,8,8,256]{3,2,1,0:T(8,128)(2,1)S(1)}, u32[]{:S(2)}, u32[]{:S(2)}) %all-to-all-start.1) | async-done | bytes 524320 | tf_op jit(solution)/shard_map/all_to_all | solution.py:536
  26.0 3.1 %all-to-all-start = ((bf16[32,32,256]{2,1,0:T(8,128)(2,1)}), bf16[32,32,256]{2,1,0:T(8,128)(2,1)S(1)}, u32[]{:S(2)}, u32[]{:S(2)}) async-start(bf16[32,32,256]{2,1,0:T(8,128)(2,1)} %bitcast.61), calls=%async_computation | async-start | bytes 1048576 | tf_op jit(solution)/shard_map/all_to_all | solution.py:541
  29.1 1.1 slice.23.w_ref
  30.2 13.9 %all-to-all-done = bf16[32,32,256]{2,1,0:T(8,128)(2,1)S(1)} async-done(((bf16[32,32,256]{2,1,0:T(8,128)(2,1)}), bf16[32,32,256]{2,1,0:T(8,128)(2,1)S(1)}, u32[]{:S(2)}, u32[]{:S(2)}) %all-to-all-start) | async-done | bytes 524320 | tf_op jit(solution)/shard_map/all_to_all | solution.py:541
  44.1 7.8 %time_attention.1 = (bf16[1024,256]{1,0:T(8,128)(2,1)}, bf16[2,256,256]{2,1,0:T(8,128)(2,1)S(1)}, bf16[2,256,256]{2,1,0:T(8,128)(2,1)S(1)}, f32[1,256]{1,0:T(1,128)S(1)}) custom-call(s32[2]{0:T(128)S(1)} %pad_add_fusion.place_ref, s32[1]{0:T(128)} %bitcast.5.first_ref, bf16[1024,256]{1,0:T(8,128)(2,1)S(1)} %bitcast.50, bf16[1024,256]{1,0:T(8,128)(2,1)S(1)} %bitcast.48, ...), custom_call_target="tpu_custom_call" | custom-call | flops 3087007744 | bytes 4194304 | tf_op jit(solution)/shard_map/time_attention/pallas_call | solution.py:445
  51.9 1.1 collective-permute-start.3
  53.0 2.8 %all-to-all-start.2 = ((bf16[32,32,256]{2,1,0:T(8,128)(2,1)}), bf16[32,32,256]{2,1,0:T(8,128)(2,1)S(1)}, u32[]{:S(2)}, u32[]{:S(2)}) async-start(bf16[32,32,256]{2,1,0:T(8,128)(2,1)} %bitcast.60), calls=%async_computation.2 | async-start | bytes 1048576 | tf_op jit(solution)/shard_map/all_to_all | solution.py:541
  56.0 1.7 %collective-permute-start.4 = (bf16[2,128,256]{2,1,0:T(8,128)(2,1)S(1)}, bf16[2,128,256]{2,1,0:T(8,128)(2,1)S(1)}, u32[]{:S(2)}, u32[]{:S(2)}) collective-permute-start(bf16[2,128,256]{2,1,0:T(8,128)(2,1)S(1)} %dynamic-slice_bitcast_fusion), channel_id=1, source_target_pairs={{0,4},{2,6},{4,0},{6,2},{8,12},{10,14},{12,8},{14,10},{16,20},{18,... | collective-permute-start | bytes 393224 | tf_op jit(solution)/shard_map/ppermute | solution.py:610
  57.6 7.6 %collective-permute-done.4 = bf16[2,128,256]{2,1,0:T(8,128)(2,1)S(1)} collective-permute-done((bf16[2,128,256]{2,1,0:T(8,128)(2,1)S(1)}, bf16[2,128,256]{2,1,0:T(8,128)(2,1)S(1)}, u32[]{:S(2)}, u32[]{:S(2)}) %collective-permute-start.4) | collective-permute-done | bytes 131104 | tf_op jit(solution)/shard_map/ppermute | solution.py:610
  65.3 2.2 %collective-permute-start.5 = (bf16[128,256]{1,0:T(8,128)(2,1)S(1)}, bf16[128,256]{1,0:T(8,128)(2,1)S(1)}, u32[]{:S(2)}, u32[]{:S(2)}) collective-permute-start(bf16[128,256]{1,0:T(8,128)(2,1)S(1)} %dynamic-slice_bitcast_fusion.1), channel_id=1, source_target_pairs={{0,1},{1,0},{2,3},{3,2},{4,5},{5,4},{6,7},{7,6},{8,9},{9,8},{10,11... | collective-permute-start | bytes 196616 | tf_op jit(solution)/shard_map/ppermute | solution.py:610
  67.5 3.2 %all-to-all-done.2 = bf16[32,32,256]{2,1,0:T(8,128)(2,1)S(1)} async-done(((bf16[32,32,256]{2,1,0:T(8,128)(2,1)}), bf16[32,32,256]{2,1,0:T(8,128)(2,1)S(1)}, u32[]{:S(2)}, u32[]{:S(2)}) %all-to-all-start.2) | async-done | bytes 524320 | tf_op jit(solution)/shard_map/all_to_all | solution.py:541
  70.7 6.2 %freq_backward.1 = (bf16[4,128,256]{2,1,0:T(8,128)(2,1)S(1)}, bf16[1,4,128,256]{3,2,1,0:T(8,128)(2,1)S(1)}, bf16[2,256,256]{2,1,0:T(8,128)(2,1)S(1)}, bf16[528,256]{1,0:T(8,128)(2,1)S(1)}, f32[16,256]{1,0:T(8,128)S(1)}) custom-call(s32[2]{0:T(128)S(1)} %pad_add_fusion.place_ref, bf16[2,4,128,256]{3,2,1,0:T(8,128)(2,1)} %bitcast.46, ...), custom_call_target="tpu_custom_call" | custom-call | flops 3221225472 | bytes 8388608 | tf_op jit(solution)/shard_map/freq_backward/pallas_call | solution.py:322
  76.9 1.1 collective-permute-start.2
  78.1 1.1 collective-permute-done.2.arrived_ref
  80.0 3.9 %all-to-all-start.3 = ((bf16[16,48,256]{2,1,0:T(8,128)(2,1)}), bf16[16,48,256]{2,1,0:T(8,128)(2,1)S(1)}, u32[]{:S(2)}, u32[]{:S(2)}) async-start(bf16[16,48,256]{2,1,0:T(8,128)(2,1)} %sums_by_peer.1), calls=%async_computation.3 | async-start | bytes 786432 | tf_op jit(solution)/shard_map/all_to_all | solution.py:615
  84.0 1.9 %collective-permute-start.1 = (bf16[4,128,256]{2,1,0:T(8,128)(2,1)S(1)}, bf16[4,128,256]{2,1,0:T(8,128)(2,1)S(1)}, u32[]{:S(2)}, u32[]{:S(2)}) collective-permute-start(bf16[4,128,256]{2,1,0:T(8,128)(2,1)S(1)} %bitcast.55), channel_id=1, source_target_pairs={{0,1},{1,0},{2,3},{3,2},{4,5},{5,4},{6,7},{7,6},{8,9},{9,8},{10,11... | collective-permute-start | bytes 786440 | tf_op jit(solution)/shard_map/ppermute | solution.py:558
  85.9 10.0 %collective-permute-done.1 = bf16[4,128,256]{2,1,0:T(8,128)(2,1)S(1)} collective-permute-done((bf16[4,128,256]{2,1,0:T(8,128)(2,1)S(1)}, bf16[4,128,256]{2,1,0:T(8,128)(2,1)S(1)}, u32[]{:S(2)}, u32[]{:S(2)}) %collective-permute-start.1) | collective-permute-done | bytes 262176 | tf_op jit(solution)/shard_map/ppermute | solution.py:558
  97.1 19.9 %all_to_all.25 = bf16[16,64,256]{2,1,0:T(8,128)(2,1)S(1)} all-to-all(bf16[16,64,256]{2,1,0:T(8,128)(2,1)S(1)} %broadcast_in_dim.2), channel_id=1, replica_groups={{0,1,4,5,8,9,12,13,16,17,20,21,24,25,28,29},{2,3,6,7,10,11,14,15,18,19,..., dimensions={0} | all-to-all | bytes 1048576 | tf_op jit(solution)/shard_map/all_to_all | solution.py:615
  117.1 1.2 fusion.3
  119.2 1.5 %maximum_convert_fusion = f32[8,256,256]{2,1,0:T(8,128)} fusion(bf16[4,256,256]{2,1,0:T(8,128)(2,1)S(1)} %bitcast.56, bf16[4,256,256]{2,1,0:T(8,128)(2,1)S(1)} %bitcast.57), kind=kLoop, calls=%fused_computation.6 | loop fusion | flops 1048576 | bytes 3145728 | tf_op jit(solution)/shard_map/convert_element_type | solution.py:651
  (37 shorter events, 5.2 us)
Async XLA Ops:
  0.6 4.1 %copy-start = (bf16[8,128,256]{2,1,0:T(8,128)(2,1)S(1)}, bf16[8,128,256]{2,1,0:T(8,128)(2,1)}, u32[]{:S(2)}) copy-start(bf16[8,128,256]{2,1,0:T(8,128)(2,1)} %param.5) | copy-start | bytes 1572868
  0.6 12.1 %copy-start.1 = (bf16[8,128,256]{2,1,0:T(8,128)(2,1)S(1)}, bf16[8,128,256]{2,1,0:T(8,128)(2,1)}, u32[]{:S(2)}) copy-start(bf16[8,128,256]{2,1,0:T(8,128)(2,1)} %param.4) | copy-start | bytes 1572868
  0.7 12.1 %copy-start.3 = (f32[2,256]{1,0:T(2,128)S(1)}, f32[2,256]{1,0:T(2,128)}, u32[]{:S(2)}) copy-start(f32[2,256]{1,0:T(2,128)} %gain_ref.5) | copy-start | bytes 6148
  1.7 11.0 %collective-permute-start = (bf16[4,128,256]{2,1,0:T(8,128)(2,1)S(1)}, bf16[4,128,256]{2,1,0:T(8,128)(2,1)S(1)}, u32[]{:S(2)}, u32[]{:S(2)}) collective-permute-start(bf16[4,128,256]{2,1,0:T(8,128)(2,1)S(1)} %bitcast.51), channel_id=1, source_target_pairs={{0,1},{1,0},{2,3},{3,2},{4,5},{5,4},{6,7},{7,6},{8,9},{9,8},{10,11... | collective-permute-start | bytes 786440 | tf_op jit(solution)/shard_map/ppermute | solution.py:558
  5.6 20.4 %all-to-all-start.1 = ((bf16[16,8,8,256]{3,2,1,0:T(8,128)(2,1)}), bf16[16,8,8,256]{3,2,1,0:T(8,128)(2,1)S(1)}, u32[]{:S(2)}, u32[]{:S(2)}) async-start(bf16[16,8,8,256]{3,2,1,0:T(8,128)(2,1)} %copy_bitcast_fusion), calls=%async_computation.1 | async-start | bytes 1048576 | tf_op jit(solution)/shard_map/all_to_all | solution.py:536
  12.7 7.7 %copy-start.2 = (bf16[4,128,256]{2,1,0:T(8,128)(2,1)}, bf16[4,128,256]{2,1,0:T(8,128)(2,1)S(1)}, u32[]{:S(2)}) copy-start(bf16[4,128,256]{2,1,0:T(8,128)(2,1)S(1)} %collective-permute-done) | copy-start | bytes 786436
  26.0 18.1 %all-to-all-start = ((bf16[32,32,256]{2,1,0:T(8,128)(2,1)}), bf16[32,32,256]{2,1,0:T(8,128)(2,1)S(1)}, u32[]{:S(2)}, u32[]{:S(2)}) async-start(bf16[32,32,256]{2,1,0:T(8,128)(2,1)} %bitcast.61), calls=%async_computation | async-start | bytes 1048576 | tf_op jit(solution)/shard_map/all_to_all | solution.py:541
  51.9 4.0 %collective-permute-start.3 = (bf16[2,256,256]{2,1,0:T(8,128)(2,1)S(1)}, bf16[2,256,256]{2,1,0:T(8,128)(2,1)S(1)}, u32[]{:S(2)}, u32[]{:S(2)}) collective-permute-start(bf16[2,256,256]{2,1,0:T(8,128)(2,1)S(1)} %get-tuple-element.42), channel_id=1, source_target_pairs={{0,2},{2,0},{4,6},{6,4},{8,10},{10,8},{12,14},{14,12},{16,18},{18,... | collective-permute-start | bytes 786440 | tf_op jit(solution)/shard_map/ppermute | solution.py:619
  53.0 17.7 %all-to-all-start.2 = ((bf16[32,32,256]{2,1,0:T(8,128)(2,1)}), bf16[32,32,256]{2,1,0:T(8,128)(2,1)S(1)}, u32[]{:S(2)}, u32[]{:S(2)}) async-start(bf16[32,32,256]{2,1,0:T(8,128)(2,1)} %bitcast.60), calls=%async_computation.2 | async-start | bytes 1048576 | tf_op jit(solution)/shard_map/all_to_all | solution.py:541
  56.0 9.2 %collective-permute-start.4 = (bf16[2,128,256]{2,1,0:T(8,128)(2,1)S(1)}, bf16[2,128,256]{2,1,0:T(8,128)(2,1)S(1)}, u32[]{:S(2)}, u32[]{:S(2)}) collective-permute-start(bf16[2,128,256]{2,1,0:T(8,128)(2,1)S(1)} %dynamic-slice_bitcast_fusion), channel_id=1, source_target_pairs={{0,4},{2,6},{4,0},{6,2},{8,12},{10,14},{12,8},{14,10},{16,20},{18,... | collective-permute-start | bytes 393224 | tf_op jit(solution)/shard_map/ppermute | solution.py:610
  65.3 12.8 %collective-permute-start.5 = (bf16[128,256]{1,0:T(8,128)(2,1)S(1)}, bf16[128,256]{1,0:T(8,128)(2,1)S(1)}, u32[]{:S(2)}, u32[]{:S(2)}) collective-permute-start(bf16[128,256]{1,0:T(8,128)(2,1)S(1)} %dynamic-slice_bitcast_fusion.1), channel_id=1, source_target_pairs={{0,1},{1,0},{2,3},{3,2},{4,5},{5,4},{6,7},{7,6},{8,9},{9,8},{10,11... | collective-permute-start | bytes 196616 | tf_op jit(solution)/shard_map/ppermute | solution.py:610
  76.9 2.3 %collective-permute-start.2 = (bf16[528,256]{1,0:T(8,128)(2,1)S(1)}, bf16[528,256]{1,0:T(8,128)(2,1)S(1)}, u32[]{:S(2)}, u32[]{:S(2)}) collective-permute-start(bf16[528,256]{1,0:T(8,128)(2,1)S(1)} %get-tuple-element.40), channel_id=1, source_target_pairs={{0,2},{2,0},{4,6},{6,4},{8,10},{10,8},{12,14},{14,12},{16,18},{18,... | collective-permute-start | bytes 811016 | tf_op jit(solution)/shard_map/ppermute | solution.py:624
  80.0 16.9 %all-to-all-start.3 = ((bf16[16,48,256]{2,1,0:T(8,128)(2,1)}), bf16[16,48,256]{2,1,0:T(8,128)(2,1)S(1)}, u32[]{:S(2)}, u32[]{:S(2)}) async-start(bf16[16,48,256]{2,1,0:T(8,128)(2,1)} %sums_by_peer.1), calls=%async_computation.3 | async-start | bytes 786432 | tf_op jit(solution)/shard_map/all_to_all | solution.py:615
  84.0 11.9 %collective-permute-start.1 = (bf16[4,128,256]{2,1,0:T(8,128)(2,1)S(1)}, bf16[4,128,256]{2,1,0:T(8,128)(2,1)S(1)}, u32[]{:S(2)}, u32[]{:S(2)}) collective-permute-start(bf16[4,128,256]{2,1,0:T(8,128)(2,1)S(1)} %bitcast.55), channel_id=1, source_target_pairs={{0,1},{1,0},{2,3},{3,2},{4,5},{5,4},{6,7},{7,6},{8,9},{9,8},{10,11... | collective-permute-start | bytes 786440 | tf_op jit(solution)/shard_map/ppermute | solution.py:558
  117.1 1.9 %collective-permute-start.6 = (bf16[16,64,256]{2,1,0:T(8,128)(2,1)S(1)}, bf16[16,64,256]{2,1,0:T(8,128)(2,1)S(1)}, u32[]{:S(2)}, u32[]{:S(2)}) collective-permute-start(bf16[16,64,256]{2,1,0:T(8,128)(2,1)S(1)} %all_to_all.25), channel_id=1, source_target_pairs={{0,2},{2,0},{4,6},{6,4},{8,10},{10,8},{12,14},{14,12},{16,18},{18,... | collective-permute-start | bytes 1572872 | tf_op jit(solution)/shard_map/ppermute | solution.py:643

commit v8 on v7

--- a/solution.py
+++ b/solution.py
@@ -20,6 +20,7 @@
 MIB = 1024 * 1024
 VMEM_LIMIT = 24 * MIB
 FORWARD_WEIGHT = 40
+PLACE_FLOPS = 10_000_000_000
 
 CONTRACT_LAST = (((1,), (1,)), ((), ()))
 CONTRACT_FIRST = (((0,), (0,)), ((), ()))
@@ -129,38 +130,54 @@
 
 
 def freq_forward_kernel(
-    place_ref, own_ref, others_ref, w_ref, gain_ref, q_ref, k_ref, v_ref, o_ref, p_ref, h_hbm,
-    hold, low, sem
+    place_ref, x_hbm, others_ref, w_ref, gain_ref,
+    q_hbm, k_hbm, v_hbm, o_hbm, p_hbm, h_hbm,
+    own_ref, q_ref, k_ref, v_ref, o_ref, p_ref, hold, h_low, load_sem, sems
 ):
-    step = pl.program_id(0)
-    freq, bins_dev, width = others_ref.shape[0] + 1, own_ref.shape[2], own_ref.shape[3]
-    bins_time = hold.shape[2] // pl.num_programs(0)
-    x = joined(own_ref.at[0, 0], others_ref.at[:, 0])
-    _, unit = norm_parts(x)
-    n = (unit * gain_ref[0:1, :]).astype(bf16)
+    frames, bins_dev, width = own_ref.shape
+    freq = others_ref.shape[0] + 1
+    bins_time = hold.shape[2] // frames
     scale = (width // HEADS) ** (-0.5)
-    q = dot(n, w_ref[0]).astype(bf16)
-    k = dot(n, w_ref[1]).astype(bf16)
-    v = dot(n, w_ref[2]).astype(bf16)
-    probs = head_probs(dot_nt(spread(q, scale), k), None)
-    o = own_channels(dot(stacked_low(probs), v), n.shape[0]).astype(bf16)
-    hidden = x + dot(o, w_ref[3])
-    q_ref[0] = q
-    k_ref[0] = k
-    v_ref[0] = v
-    o_ref[0] = o
-    for h in range(HEADS):
-        p_ref[0, h] = probs[h].astype(bf16)
-    rows = pl.ds(pl.multiple_of(step * bins_time, bins_time), bins_time)
-    for f in range(freq):
-        part = hidden[f * bins_dev : (f + 1) * bins_dev].reshape(-1, bins_time, width)
-        hold[:, slot_of(place_ref[0], f, freq), rows, :] = part
-
-    @pl.when(step == pl.num_programs(0) - 1)
-    def _():
-        low[...] = hold[...].astype(bf16)
-        copy = pltpu.make_async_copy(low, h_hbm, sem)
-        copy.start()
+    stores = []
+
+    def store(source, target):
+        stores.append(pltpu.make_async_copy(source, target, sems.at[len(stores)]))
+        stores[-1].start()
+
+    load = pltpu.make_async_copy(x_hbm.at[place_ref[0]], own_ref, load_sem)
+    load.start()
+    load.wait()
+    first = []
+    for f in range(frames):
+        _, unit = norm_parts(joined(own_ref.at[f], others_ref.at[:, f]))
+        n = (unit * gain_ref[0:1, :]).astype(bf16)
+        q = dot(n, w_ref[0]).astype(bf16)
+        k = dot(n, w_ref[1]).astype(bf16)
+        v = dot(n, w_ref[2]).astype(bf16)
+        q_ref[f] = q
+        k_ref[f] = k
+        v_ref[f] = v
+        first.append((v, dot_nt(spread(q, scale), k)))
+    store(q_ref, q_hbm)
+    store(k_ref, k_hbm)
+    store(v_ref, v_hbm)
+    second = []
+    for f, (v, scores) in enumerate(first):
+        low = stacked_low(head_probs(scores, None))
+        p_ref[f] = low.reshape(p_ref.shape[1:])
+        store(p_ref.at[f], p_hbm.at[f])
+        second.append(own_channels(dot(low, v), v.shape[0]).astype(bf16))
+    for f, o in enumerate(second):
+        o_ref[f] = o
+        hidden = joined(own_ref.at[f], others_ref.at[:, f]) + dot(o, w_ref[3])
+        rows = pl.ds(f * bins_time, bins_time)
+        for j in range(freq):
+            part = hidden[j * bins_dev : (j + 1) * bins_dev].reshape(-1, bins_time, width)
+            hold[:, slot_of(place_ref[0], j, freq), rows, :] = part
+    store(o_ref, o_hbm)
+    h_low[...] = hold[...].astype(bf16)
+    store(h_low, h_hbm)
+    for copy in stores:
         copy.wait()
 
 
@@ -179,44 +196,29 @@
     return pltpu.with_memory_space_constraint(array, pltpu.HBM)
 
 
-def frame_specs(freq, bins_dev, width, count=1):
-    own = pl.BlockSpec((1, count, bins_dev, width), lambda i, place: (place[0], i, 0, 0))
-    others = pl.BlockSpec((freq - 1, count, bins_dev, width), lambda i, place: (0, i, 0, 0))
-    rows = pl.BlockSpec((count, freq * bins_dev, width), lambda i, place: (i, 0, 0))
-    return own, others, rows
-
-
-def fixed(shape):
-    return pl.BlockSpec(shape, lambda i, place: (0,) * len(shape))
-
-
 def freq_forward(place, features, others, weights, gains, group):
     freq, frames, bins_dev, width = features.shape
     bins = freq * bins_dev
-    rows = frames * (bins_dev // group)
-    own_spec, others_spec, row_spec = frame_specs(freq, bins_dev, width)
-    rowshape = pltpu.HBM((frames, bins, width), bf16)
-    whole = (group, freq, rows, width)
+    whole = (group, freq, frames * (bins_dev // group), width)
+    probs = (frames, HEADS, bins, bins)
+    rows = (frames, bins, width)
     flops = frames * 2 * bins * (4 * width * width + 2 * HEADS * bins * width)
+    vmem = pl.BlockSpec(memory_space=pltpu.VMEM)
+    hbm = pl.BlockSpec(memory_space=pltpu.HBM)
     return pl.pallas_call(
         freq_forward_kernel,
-        grid_spec=pltpu.PrefetchScalarGridSpec(
-            num_scalar_prefetch=1,
-            grid=(frames,),
-            in_specs=[own_spec, others_spec, fixed(weights.shape), fixed(gains.shape)],
-            out_specs=[row_spec] * 4
-            + [
-                pl.BlockSpec((1, HEADS, bins, bins), lambda i, place: (i, 0, 0, 0)),
-                pl.BlockSpec(memory_space=pltpu.HBM),
-            ],
-            scratch_shapes=[
-                pltpu.VMEM(whole, f32),
-                pltpu.VMEM(whole, bf16),
-                pltpu.SemaphoreType.DMA,
-            ],
-        ),
-        out_shape=[rowshape] * 4
-        + [pltpu.HBM((frames, HEADS, bins, bins), bf16), pltpu.HBM(whole, bf16)],
+        in_specs=[pl.BlockSpec(memory_space=pltpu.SMEM), hbm, vmem, vmem, vmem],
+        out_specs=[hbm] * 6,
+        out_shape=[pltpu.HBM(rows, bf16)] * 4 + [pltpu.HBM(probs, bf16), pltpu.HBM(whole, bf16)],
+        scratch_shapes=[pltpu.VMEM((frames, bins_dev, width), bf16)]
+        + [pltpu.VMEM(rows, bf16)] * 4
+        + [
+            pltpu.VMEM(probs, bf16),
+            pltpu.VMEM(whole, f32),
+            pltpu.VMEM(whole, bf16),
+            pltpu.SemaphoreType.DMA,
+            pltpu.SemaphoreType.DMA((frames + 5,)),
+        ],
         compiler_params=pltpu.CompilerParams(vmem_limit_bytes=VMEM_LIMIT),
         cost_estimate=pl.CostEstimate(
             flops=flops * FORWARD_WEIGHT,
@@ -224,7 +226,7 @@
             transcendentals=frames * HEADS * bins * bins,
         ),
         name="freq_forward",
-    )(place, features, near(others), near(weights), gains)
+    )(place, far(features), near(others), near(weights), gains)
 
 
 def freq_backward_kernel(
@@ -465,6 +467,35 @@
     )(place, first, near(hidden), near(upstream), near(weights), gains)
 
 
+def place_kernel(place_ref, *refs):
+    *parts, out_hbm, sems = refs
+    freq = len(parts)
+    copies = [
+        pltpu.make_async_copy(part, out_hbm.at[lax.rem(place_ref[0] + j, freq)], sems.at[j])
+        for j, part in enumerate(parts)
+    ]
+    for copy in copies:
+        copy.start()
+    for copy in copies:
+        copy.wait()
+
+
+def place_frames(place, parts):
+    vmem = pl.BlockSpec(memory_space=pltpu.VMEM)
+    return pl.pallas_call(
+        place_kernel,
+        in_specs=[pl.BlockSpec(memory_space=pltpu.SMEM)] + [vmem] * len(parts),
+        out_specs=pl.BlockSpec(memory_space=pltpu.HBM),
+        out_shape=pltpu.HBM((len(parts),) + parts[0].shape, bf16),
+        scratch_shapes=[pltpu.SemaphoreType.DMA((len(parts),))],
+        compiler_params=pltpu.CompilerParams(vmem_limit_bytes=VMEM_LIMIT),
+        cost_estimate=pl.CostEstimate(
+            flops=PLACE_FLOPS, bytes_accessed=4 * parts[0].size, transcendentals=0
+        ),
+        name="place_frames",
+    )(place, *map(near, parts))
+
+
 def sums_kernel(kept_ref, arrived_ref, time_ref, gains_ref, out_ref):
     peers, _, width = out_ref.shape
     arrived = arrived_ref[...].astype(f32)
@@ -627,8 +658,8 @@
     )
     arrived = over_same(sums)
     returned = [grad_own] + [along_freq(grad_others[j - 1], -j) for j in range(1, freq)]
-    returned, arrived = lax.optimization_barrier((returned, arrived))
-    grad_input = jnp.roll(jnp.stack(returned), place[0], axis=0).reshape(features.shape)
+    grad_input = place_frames(place, returned).reshape(features.shape)
+    grad_input, arrived = lax.optimization_barrier((grad_input, arrived))
 
     inv_root = (total_frames * bins_dev * freq) ** (-0.5)
     summed = jnp.sum(arrived.astype(f32), axis=0) * inv_root

time: 121 us -> 119 us (0.983)
  waiting for transfers between devices: 42.6 us -> 47 us
  blocking collectives: 19.9 us -> 17.9 us
  other arithmetic: 3.71 us -> 2.49 us
    all_to_all x1, waiting for transfers between devices: 1.06 us -> 9.26 us  [over_same(): lax.all_to_all(blocks, ('tm', 'freq'), 0, 0, tiled=True, axis_index_group...]
    ppermute x2, waiting for transfers between devices: 9.98 us -> 2.34 us  [along_freq(): lax.ppermute(block, 'freq', [(i, (i + steps) % freq) for i in range(freq)])]
    all_to_all x1, waiting for transfers between devices: 5.63 us -> 9.11 us  [over_tm(): lax.all_to_all(blocks, 'tm', 0, 0, tiled=True, axis_index_groups=groups)]
    all_to_all x1, blocking collectives: 19.9 us -> 17.9 us  [over_same(): lax.all_to_all(blocks, ('tm', 'freq'), 0, 0, tiled=True, axis_index_group...]
    pallas_call x1 -> x2, Pallas kernels: 7.63 us -> 6.54 us  [the longest x1 5.18 us: freq_forward(): pl.pallas_call(freq_forward_kernel, in_specs=[pl.BlockSpec(memory_space=p...]
  transfers between devices with their start and end apart: 11 -> 11, of which waited for: 8 -> 8; matrix products, arithmetic and copies ran while one was open for 4% -> 2% of each run, Pallas kernels for 11% -> 11%
where the time goes in v8:
time: 119 us
  waiting for transfers between devices  47 us (39%)
  starting transfers between devices  25.8 us (22%)
  Pallas kernels  22.5 us (19%)
  blocking collectives  17.9 us (15%)
  other arithmetic  2.49 us (2%)
  local copies, waits for them, and re-layouts  2.14 us (2%)
    all_to_all x1, blocking collectives, over_same(): lax.all_to_all(blocks, ('tm', 'freq'), 0, 0, tiled=True, axis_index_group...  17.9 us
    all_to_all x2, waiting for transfers between devices, over_all(): lax.all_to_all(flat, ('tm', 'freq'), 0, 0, tiled=True).reshape(blocks.shape)  17.1 us
    all_to_all x1, waiting for transfers between devices, over_same(): lax.all_to_all(blocks, ('tm', 'freq'), 0, 0, tiled=True, axis_index_group...  9.26 us
    all_to_all x1, waiting for transfers between devices, over_tm(): lax.all_to_all(blocks, 'tm', 0, 0, tiled=True, axis_index_groups=groups)  9.11 us
    pallas_call x1, Pallas kernels, time_attention(): pl.pallas_call(functools.partial(time_kernel, bins, own_start, total), in...  7.78 us
    ppermute x2, waiting for transfers between devices, scattered(): came = lax.ppermute(sent, axis, [(d, d ^ 1 << k) for d in devices])  7.58 us
    pallas_call x1, Pallas kernels, freq_backward(): pl.pallas_call(freq_backward_kernel, in_specs=[pl.BlockSpec(memory_space=...  6.25 us
    all_to_all x2, starting transfers between devices, over_all(): lax.all_to_all(flat, ('tm', 'freq'), 0, 0, tiled=True).reshape(blocks.shape)  5.93 us
  transfers between devices with their start and end apart: 11, of which 8 were waited for; matrix products, arithmetic and copies ran while one was open for 2% of the time, Pallas kernels for 11%

profile of v8, /device:TPU:0, one launch (start us, length us, event | category | flops | bytes accessed | tf_op | source)
XLA Modules:
  0.0 118.7 jit_solution(1181511059207119350)
XLA Ops:
  0.7 1.1 pick_others.1
  1.8 3.0 %collective-permute-start = (bf16[4,128,256]{2,1,0:T(8,128)(2,1)S(1)}, bf16[4,128,256]{2,1,0:T(8,128)(2,1)S(1)}, u32[]{:S(2)}, u32[]{:S(2)}) collective-permute-start(bf16[4,128,256]{2,1,0:T(8,128)(2,1)S(1)} %bitcast.46), channel_id=1, source_target_pairs={{0,1},{1,0},{2,3},{3,2},{4,5},{5,4},{6,7},{7,6},{8,9},{9,8},{10,11... | collective-permute-start | bytes 786440 | tf_op jit(solution)/shard_map/ppermute | solution.py:589
  5.7 5.9 %all-to-all-start.1 = ((bf16[16,8,8,256]{3,2,1,0:T(8,128)(2,1)}), bf16[16,8,8,256]{3,2,1,0:T(8,128)(2,1)S(1)}, u32[]{:S(2)}, u32[]{:S(2)}) async-start(bf16[16,8,8,256]{3,2,1,0:T(8,128)(2,1)} %copy_bitcast_fusion), calls=%async_computation.1 | async-start | bytes 1048576 | tf_op jit(solution)/shard_map/all_to_all | solution.py:567
  11.7 5.2 %freq_forward.1 = (bf16[4,256,256]{2,1,0:T(8,128)(2,1)}, bf16[4,256,256]{2,1,0:T(8,128)(2,1)}, bf16[4,256,256]{2,1,0:T(8,128)(2,1)}, bf16[4,256,256]{2,1,0:T(8,1...) custom-call(s32[2]{0:T(128)S(1)} %pad_add_fusion.place_ref, ...), custom_call_target="tpu_custom_call" | custom-call | flops 64424509440 | bytes 2097152 | tf_op jit(solution)/shard_map/freq_forward/pallas_call | solution.py:208
  16.9 9.1 %all-to-all-done.1 = bf16[16,8,8,256]{3,2,1,0:T(8,128)(2,1)S(1)} async-done(((bf16[16,8,8,256]{3,2,1,0:T(8,128)(2,1)}), bf16[16,8,8,256]{3,2,1,0:T(8,128)(2,1)S(1)}, u32[]{:S(2)}, u32[]{:S(2)}) %all-to-all-start.1) | async-done | bytes 524320 | tf_op jit(solution)/shard_map/all_to_all | solution.py:567
  26.0 3.1 %all-to-all-start = ((bf16[32,32,256]{2,1,0:T(8,128)(2,1)}), bf16[32,32,256]{2,1,0:T(8,128)(2,1)S(1)}, u32[]{:S(2)}, u32[]{:S(2)}) async-start(bf16[32,32,256]{2,1,0:T(8,128)(2,1)} %bitcast.58), calls=%async_computation | async-start | bytes 1048576 | tf_op jit(solution)/shard_map/all_to_all | solution.py:572
  29.1 1.1 slice.23.w_ref
  30.2 13.9 %all-to-all-done = bf16[32,32,256]{2,1,0:T(8,128)(2,1)S(1)} async-done(((bf16[32,32,256]{2,1,0:T(8,128)(2,1)}), bf16[32,32,256]{2,1,0:T(8,128)(2,1)S(1)}, u32[]{:S(2)}, u32[]{:S(2)}) %all-to-all-start) | async-done | bytes 524320 | tf_op jit(solution)/shard_map/all_to_all | solution.py:572
  44.1 7.8 %time_attention.1 = (bf16[1024,256]{1,0:T(8,128)(2,1)}, bf16[2,256,256]{2,1,0:T(8,128)(2,1)S(1)}, bf16[2,256,256]{2,1,0:T(8,128)(2,1)S(1)}, f32[1,256]{1,0:T(1,128)S(1)}) custom-call(s32[2]{0:T(128)S(1)} %pad_add_fusion.place_ref, s32[1]{0:T(128)} %bitcast.5.first_ref, bf16[1024,256]{1,0:T(8,128)(2,1)S(1)} %bitcast.45, bf16[1024,256]{1,0:T(8,128)(2,1)S(1)} %bitcast.43, ...), custom_call_target="tpu_custom_call" | custom-call | flops 3087007744 | bytes 4194304 | tf_op jit(solution)/shard_map/time_attention/pallas_call | solution.py:447
  51.9 1.1 collective-permute-start.3
  53.0 2.9 %all-to-all-start.2 = ((bf16[32,32,256]{2,1,0:T(8,128)(2,1)}), bf16[32,32,256]{2,1,0:T(8,128)(2,1)S(1)}, u32[]{:S(2)}, u32[]{:S(2)}) async-start(bf16[32,32,256]{2,1,0:T(8,128)(2,1)} %bitcast.57), calls=%async_computation.2 | async-start | bytes 1048576 | tf_op jit(solution)/shard_map/all_to_all | solution.py:572
  56.0 1.7 %collective-permute-start.4 = (bf16[2,128,256]{2,1,0:T(8,128)(2,1)S(1)}, bf16[2,128,256]{2,1,0:T(8,128)(2,1)S(1)}, u32[]{:S(2)}, u32[]{:S(2)}) collective-permute-start(bf16[2,128,256]{2,1,0:T(8,128)(2,1)S(1)} %dynamic-slice_bitcast_fusion), channel_id=1, source_target_pairs={{0,4},{2,6},{4,0},{6,2},{8,12},{10,14},{12,8},{14,10},{16,20},{18,... | collective-permute-start | bytes 393224 | tf_op jit(solution)/shard_map/ppermute | solution.py:641
  57.7 7.6 %collective-permute-done.4 = bf16[2,128,256]{2,1,0:T(8,128)(2,1)S(1)} collective-permute-done((bf16[2,128,256]{2,1,0:T(8,128)(2,1)S(1)}, bf16[2,128,256]{2,1,0:T(8,128)(2,1)S(1)}, u32[]{:S(2)}, u32[]{:S(2)}) %collective-permute-start.4) | collective-permute-done | bytes 131104 | tf_op jit(solution)/shard_map/ppermute | solution.py:641
  65.3 2.2 %collective-permute-start.5 = (bf16[128,256]{1,0:T(8,128)(2,1)S(1)}, bf16[128,256]{1,0:T(8,128)(2,1)S(1)}, u32[]{:S(2)}, u32[]{:S(2)}) collective-permute-start(bf16[128,256]{1,0:T(8,128)(2,1)S(1)} %dynamic-slice_bitcast_fusion.1), channel_id=1, source_target_pairs={{0,1},{1,0},{2,3},{3,2},{4,5},{5,4},{6,7},{7,6},{8,9},{9,8},{10,11... | collective-permute-start | bytes 196616 | tf_op jit(solution)/shard_map/ppermute | solution.py:641
  67.6 3.2 %all-to-all-done.2 = bf16[32,32,256]{2,1,0:T(8,128)(2,1)S(1)} async-done(((bf16[32,32,256]{2,1,0:T(8,128)(2,1)}), bf16[32,32,256]{2,1,0:T(8,128)(2,1)S(1)}, u32[]{:S(2)}, u32[]{:S(2)}) %all-to-all-start.2) | async-done | bytes 524320 | tf_op jit(solution)/shard_map/all_to_all | solution.py:572
  70.7 6.2 %freq_backward.1 = (bf16[4,128,256]{2,1,0:T(8,128)(2,1)S(1)}, bf16[1,4,128,256]{3,2,1,0:T(8,128)(2,1)S(1)}, bf16[2,256,256]{2,1,0:T(8,128)(2,1)S(1)}, bf16[528,256]{1,0:T(8,128)(2,1)S(1)}, f32[16,256]{1,0:T(8,128)S(1)}) custom-call(s32[2]{0:T(128)S(1)} %pad_add_fusion.place_ref, bf16[2,4,128,256]{3,2,1,0:T(8,128)(2,1)} %bitcast.56, ...), custom_call_target="tpu_custom_call" | custom-call | flops 3221225472 | bytes 8388608 | tf_op jit(solution)/shard_map/freq_backward/pallas_call | solution.py:324
  77.0 1.1 collective-permute-start.2
  80.1 3.9 %all-to-all-start.3 = ((bf16[16,48,256]{2,1,0:T(8,128)(2,1)}), bf16[16,48,256]{2,1,0:T(8,128)(2,1)S(1)}, u32[]{:S(2)}, u32[]{:S(2)}) async-start(bf16[16,48,256]{2,1,0:T(8,128)(2,1)} %sums_by_peer.1), calls=%async_computation.3 | async-start | bytes 786432 | tf_op jit(solution)/shard_map/all_to_all | solution.py:646
  84.1 2.3 %collective-permute-done.1.refs_1_ = bf16[4,128,256]{2,1,0:T(8,128)(2,1)S(1)} collective-permute-done((bf16[4,128,256]{2,1,0:T(8,128)(2,1)S(1)}, bf16[4,128,256]{2,1,0:T(8,128)(2,1)S(1)}, u32[]{:S(2)}, u32[]{:S(2)}) %collective-permute-start.1) | collective-permute-done | bytes 262176 | tf_op jit(solution)/shard_map/ppermute | solution.py:589
  86.4 1.4 %place_frames.1 = bf16[2,4,128,256]{3,2,1,0:T(8,128)(2,1)} custom-call(s32[2]{0:T(128)S(1)} %pad_add_fusion.place_ref, bf16[4,128,256]{2,1,0:T(8,128)(2,1)S(1)} %get-tuple-element.36.refs_0_, bf16[4,128,256]{2,1,0:T(8,128)(2,1)S(1)} %collective-permute-done.1.refs_1_), custom_call_target="tpu_custom_call" | custom-call | flops 10000000000 | bytes 524288 | tf_op jit(solution)/shard_map/place_frames/pallas_call | solution.py:485
  87.8 9.3 %all-to-all-done.3 = bf16[16,48,256]{2,1,0:T(8,128)(2,1)S(1)} async-done(((bf16[16,48,256]{2,1,0:T(8,128)(2,1)}), bf16[16,48,256]{2,1,0:T(8,128)(2,1)S(1)}, u32[]{:S(2)}, u32[]{:S(2)}) %all-to-all-start.3) | async-done | bytes 393248 | tf_op jit(solution)/shard_map/all_to_all | solution.py:646
  97.2 17.9 %all_to_all.25 = bf16[16,64,256]{2,1,0:T(8,128)(2,1)S(1)} all-to-all(bf16[16,64,256]{2,1,0:T(8,128)(2,1)S(1)} %broadcast_in_dim.2), channel_id=1, replica_groups={{0,1,4,5,8,9,12,13,16,17,20,21,24,25,28,29},{2,3,6,7,10,11,14,15,18,19,..., dimensions={0} | all-to-all | bytes 1048576 | tf_op jit(solution)/shard_map/all_to_all | solution.py:646
  115.7 1.3 %collective-permute-done.6 = bf16[16,64,256]{2,1,0:T(8,128)(2,1)S(1)} collective-permute-done((bf16[16,64,256]{2,1,0:T(8,128)(2,1)S(1)}, bf16[16,64,256]{2,1,0:T(8,128)(2,1)S(1)}, u32[]{:S(2)}, u32[]{:S(2)}) %collective-permute-start.6) | collective-permute-done | bytes 524320 | tf_op jit(solution)/shard_map/ppermute | solution.py:674
  117.2 1.5 %maximum_convert_fusion = f32[8,256,256]{2,1,0:T(8,128)} fusion(bf16[4,256,256]{2,1,0:T(8,128)(2,1)S(1)} %bitcast.50, bf16[4,256,256]{2,1,0:T(8,128)(2,1)S(1)} %bitcast.51), kind=kLoop, calls=%fused_computation.2 | loop fusion | flops 1048576 | bytes 3145728 | tf_op jit(solution)/shard_map/convert_element_type | solution.py:682
  (37 shorter events, 4.1 us)
Async XLA Ops:
  0.6 4.2 %copy-start = (bf16[8,128,256]{2,1,0:T(8,128)(2,1)S(1)}, bf16[8,128,256]{2,1,0:T(8,128)(2,1)}, u32[]{:S(2)}) copy-start(bf16[8,128,256]{2,1,0:T(8,128)(2,1)} %param.5) | copy-start | bytes 1572868
  0.6 10.9 %copy-start.3 = (bf16[8,256,256]{2,1,0:T(8,128)(2,1)S(1)}, bf16[8,256,256]{2,1,0:T(8,128)(2,1)}, u32[]{:S(2)}) copy-start(bf16[8,256,256]{2,1,0:T(8,128)(2,1)} %param.6) | copy-start | bytes 3145732
  0.7 11.1 %copy-start.2 = (f32[2,256]{1,0:T(2,128)S(1)}, f32[2,256]{1,0:T(2,128)}, u32[]{:S(2)}) copy-start(f32[2,256]{1,0:T(2,128)} %gain_ref.5) | copy-start | bytes 6148
  1.8 10.0 %collective-permute-start = (bf16[4,128,256]{2,1,0:T(8,128)(2,1)S(1)}, bf16[4,128,256]{2,1,0:T(8,128)(2,1)S(1)}, u32[]{:S(2)}, u32[]{:S(2)}) collective-permute-start(bf16[4,128,256]{2,1,0:T(8,128)(2,1)S(1)} %bitcast.46), channel_id=1, source_target_pairs={{0,1},{1,0},{2,3},{3,2},{4,5},{5,4},{6,7},{7,6},{8,9},{9,8},{10,11... | collective-permute-start | bytes 786440 | tf_op jit(solution)/shard_map/ppermute | solution.py:589
  5.7 20.4 %all-to-all-start.1 = ((bf16[16,8,8,256]{3,2,1,0:T(8,128)(2,1)}), bf16[16,8,8,256]{3,2,1,0:T(8,128)(2,1)S(1)}, u32[]{:S(2)}, u32[]{:S(2)}) async-start(bf16[16,8,8,256]{3,2,1,0:T(8,128)(2,1)} %copy_bitcast_fusion), calls=%async_computation.1 | async-start | bytes 1048576 | tf_op jit(solution)/shard_map/all_to_all | solution.py:567
  11.7 5.2 %copy-start.1 = (bf16[4,128,256]{2,1,0:T(8,128)(2,1)}, bf16[4,128,256]{2,1,0:T(8,128)(2,1)S(1)}, u32[]{:S(2)}) copy-start(bf16[4,128,256]{2,1,0:T(8,128)(2,1)S(1)} %collective-permute-done) | copy-start | bytes 786436
  26.0 18.1 %all-to-all-start = ((bf16[32,32,256]{2,1,0:T(8,128)(2,1)}), bf16[32,32,256]{2,1,0:T(8,128)(2,1)S(1)}, u32[]{:S(2)}, u32[]{:S(2)}) async-start(bf16[32,32,256]{2,1,0:T(8,128)(2,1)} %bitcast.58), calls=%async_computation | async-start | bytes 1048576 | tf_op jit(solution)/shard_map/all_to_all | solution.py:572
  51.9 4.0 %collective-permute-start.3 = (bf16[2,256,256]{2,1,0:T(8,128)(2,1)S(1)}, bf16[2,256,256]{2,1,0:T(8,128)(2,1)S(1)}, u32[]{:S(2)}, u32[]{:S(2)}) collective-permute-start(bf16[2,256,256]{2,1,0:T(8,128)(2,1)S(1)} %get-tuple-element.41), channel_id=1, source_target_pairs={{0,2},{2,0},{4,6},{6,4},{8,10},{10,8},{12,14},{14,12},{16,18},{18,... | collective-permute-start | bytes 786440 | tf_op jit(solution)/shard_map/ppermute | solution.py:650
  53.0 17.7 %all-to-all-start.2 = ((bf16[32,32,256]{2,1,0:T(8,128)(2,1)}), bf16[32,32,256]{2,1,0:T(8,128)(2,1)S(1)}, u32[]{:S(2)}, u32[]{:S(2)}) async-start(bf16[32,32,256]{2,1,0:T(8,128)(2,1)} %bitcast.57), calls=%async_computation.2 | async-start | bytes 1048576 | tf_op jit(solution)/shard_map/all_to_all | solution.py:572
  56.0 9.2 %collective-permute-start.4 = (bf16[2,128,256]{2,1,0:T(8,128)(2,1)S(1)}, bf16[2,128,256]{2,1,0:T(8,128)(2,1)S(1)}, u32[]{:S(2)}, u32[]{:S(2)}) collective-permute-start(bf16[2,128,256]{2,1,0:T(8,128)(2,1)S(1)} %dynamic-slice_bitcast_fusion), channel_id=1, source_target_pairs={{0,4},{2,6},{4,0},{6,2},{8,12},{10,14},{12,8},{14,10},{16,20},{18,... | collective-permute-start | bytes 393224 | tf_op jit(solution)/shard_map/ppermute | solution.py:641
  65.3 13.6 %collective-permute-start.5 = (bf16[128,256]{1,0:T(8,128)(2,1)S(1)}, bf16[128,256]{1,0:T(8,128)(2,1)S(1)}, u32[]{:S(2)}, u32[]{:S(2)}) collective-permute-start(bf16[128,256]{1,0:T(8,128)(2,1)S(1)} %dynamic-slice_bitcast_fusion.1), channel_id=1, source_target_pairs={{0,1},{1,0},{2,3},{3,2},{4,5},{5,4},{6,7},{7,6},{8,9},{9,8},{10,11... | collective-permute-start | bytes 196616 | tf_op jit(solution)/shard_map/ppermute | solution.py:641
  77.0 2.3 %collective-permute-start.2 = (bf16[528,256]{1,0:T(8,128)(2,1)S(1)}, bf16[528,256]{1,0:T(8,128)(2,1)S(1)}, u32[]{:S(2)}, u32[]{:S(2)}) collective-permute-start(bf16[528,256]{1,0:T(8,128)(2,1)S(1)} %get-tuple-element.39), channel_id=1, source_target_pairs={{0,2},{2,0},{4,6},{6,4},{8,10},{10,8},{12,14},{14,12},{16,18},{18,... | collective-permute-start | bytes 811016 | tf_op jit(solution)/shard_map/ppermute | solution.py:655
  78.1 8.3 %collective-permute-start.1 = (bf16[4,128,256]{2,1,0:T(8,128)(2,1)S(1)}, bf16[4,128,256]{2,1,0:T(8,128)(2,1)S(1)}, u32[]{:S(2)}, u32[]{:S(2)}) collective-permute-start(bf16[4,128,256]{2,1,0:T(8,128)(2,1)S(1)} %bitcast.49), channel_id=1, source_target_pairs={{0,1},{1,0},{2,3},{3,2},{4,5},{5,4},{6,7},{7,6},{8,9},{9,8},{10,11... | collective-permute-start | bytes 786440 | tf_op jit(solution)/shard_map/ppermute | solution.py:589
  80.1 16.9 %all-to-all-start.3 = ((bf16[16,48,256]{2,1,0:T(8,128)(2,1)}), bf16[16,48,256]{2,1,0:T(8,128)(2,1)S(1)}, u32[]{:S(2)}, u32[]{:S(2)}) async-start(bf16[16,48,256]{2,1,0:T(8,128)(2,1)} %sums_by_peer.1), calls=%async_computation.3 | async-start | bytes 786432 | tf_op jit(solution)/shard_map/all_to_all | solution.py:646
  115.1 1.9 %collective-permute-start.6 = (bf16[16,64,256]{2,1,0:T(8,128)(2,1)S(1)}, bf16[16,64,256]{2,1,0:T(8,128)(2,1)S(1)}, u32[]{:S(2)}, u32[]{:S(2)}) collective-permute-start(bf16[16,64,256]{2,1,0:T(8,128)(2,1)S(1)} %all_to_all.25), channel_id=1, source_target_pairs={{0,2},{2,0},{4,6},{6,4},{8,10},{10,8},{12,14},{14,12},{16,18},{18,... | collective-permute-start | bytes 1572872 | tf_op jit(solution)/shard_map/ppermute | solution.py:674

commit v9 on v8

--- a/solution.py
+++ b/solution.py
@@ -390,27 +390,43 @@
         frame = first_ref[0] + key
         allowed = allowed & (frame >= 0) & (frame < total_frames)
 
-    together = max(n for n in (1, 2, 4) if bins % n == 0 and (n == 1 or n * span <= 512))
-
-    def some_bins(start):
-        places = [pl.ds(start + b, span, stride=bins) for b in range(together)]
-        first = []
-        for rows in places:
+    together = max(n for n in (1, 2) if bins % n == 0 and (n == 1 or n * span <= 512))
+
+    def products(start):
+        result = []
+        for b in range(together):
+            rows = pl.ds(start + b, span, stride=bins)
             q, k, v, grad_out = (get(ref, rows).astype(bf16) for ref in (q_s, k_s, v_s, go_s))
             out_spread = spread(grad_out, 1.0)
-            first.append((q, k, v, out_spread, dot_nt(spread(q, scale), k), dot_nt(out_spread, v)))
+            scores, grad_probs = dot_nt(spread(q, scale), k), dot_nt(out_spread, v)
+            result.append((rows, q, k, v, out_spread, scores, grad_probs))
+        return result
+
+    def cotangents(result):
         second = []
-        for q, k, v, out_spread, scores, grad_probs in first:
+        for *_, scores, grad_probs in result:
             probs = head_probs(scores, allowed)
             second.append((stacked_low(probs), head_grads(probs, grad_probs, scale)))
-        for rows, (q, k, v, out_spread, _, _), (low, grad_scores) in zip(places, first, second):
+        return second
+
+    def mix(result, second):
+        for (rows, q, k, v, out_spread, *_), (low, grad_scores) in zip(result, second):
             put(o_s, rows, own_channels(dot(low, v), span))
             put(gq_s, rows, own_channels(dot(grad_scores, k), span))
             put(gk_s, rows, dot_tn(grad_scores, spread(q, 1.0)))
             put(gv_s, rows, dot_tn(low, out_spread))
 
-    for start in range(0, bins, together):
-        some_bins(start)
+    starts = list(range(0, bins, together))
+    ahead = products(starts[0])
+    for i in range(len(starts)):
+        first, ahead = ahead, None
+        second = cotangents(first)
+        more = i + 1 < len(starts)
+        if more and together > 1:
+            ahead = products(starts[i + 1])
+        mix(first, second)
+        if more and together == 1:
+            ahead = products(starts[i + 1])
 
     dg_ref[...] = jnp.zeros_like(dg_ref)
     stores = []

time: 119 us -> 119 us (level)
  no operation moved by 1% of the time
where the time goes in v9:
time: 119 us
  waiting for transfers between devices  47 us (39%)
  starting transfers between devices  25.8 us (22%)
  Pallas kernels  22.5 us (19%)
  blocking collectives  17.9 us (15%)
  other arithmetic  2.49 us (2%)
  local copies, waits for them, and re-layouts  2.14 us (2%)
    all_to_all x1, blocking collectives, over_same(): lax.all_to_all(blocks, ('tm', 'freq'), 0, 0, tiled=True, axis_index_group...  17.9 us
    all_to_all x2, waiting for transfers between devices, over_all(): lax.all_to_all(flat, ('tm', 'freq'), 0, 0, tiled=True).reshape(blocks.shape)  17.1 us
    all_to_all x1, waiting for transfers between devices, over_same(): lax.all_to_all(blocks, ('tm', 'freq'), 0, 0, tiled=True, axis_index_group...  9.26 us
    all_to_all x1, waiting for transfers between devices, over_tm(): lax.all_to_all(blocks, 'tm', 0, 0, tiled=True, axis_index_groups=groups)  9.11 us
    pallas_call x1, Pallas kernels, time_attention(): pl.pallas_call(functools.partial(time_kernel, bins, own_start, total), in...  7.76 us
    ppermute x2, waiting for transfers between devices, scattered(): came = lax.ppermute(sent, axis, [(d, d ^ 1 << k) for d in devices])  7.58 us
    pallas_call x1, Pallas kernels, freq_backward(): pl.pallas_call(freq_backward_kernel, in_specs=[pl.BlockSpec(memory_space=...  6.25 us
    all_to_all x2, starting transfers between devices, over_all(): lax.all_to_all(flat, ('tm', 'freq'), 0, 0, tiled=True).reshape(blocks.shape)  5.93 us
  transfers between devices with their start and end apart: 11, of which 8 were waited for; matrix products, arithmetic and copies ran while one was open for 2% of the time, Pallas kernels for 11%

profile of v9, /device:TPU:0, one launch (start us, length us, event | category | flops | bytes accessed | tf_op | source)
XLA Modules:
  0.0 118.7 jit_solution(11693439018319057154)
XLA Ops:
  0.7 1.1 pick_others.1
  1.8 3.0 %collective-permute-start = (bf16[4,128,256]{2,1,0:T(8,128)(2,1)S(1)}, bf16[4,128,256]{2,1,0:T(8,128)(2,1)S(1)}, u32[]{:S(2)}, u32[]{:S(2)}) collective-permute-start(bf16[4,128,256]{2,1,0:T(8,128)(2,1)S(1)} %bitcast.46), channel_id=1, source_target_pairs={{0,1},{1,0},{2,3},{3,2},{4,5},{5,4},{6,7},{7,6},{8,9},{9,8},{10,11... | collective-permute-start | bytes 786440 | tf_op jit(solution)/shard_map/ppermute | solution.py:605
  5.7 5.9 %all-to-all-start.1 = ((bf16[16,8,8,256]{3,2,1,0:T(8,128)(2,1)}), bf16[16,8,8,256]{3,2,1,0:T(8,128)(2,1)S(1)}, u32[]{:S(2)}, u32[]{:S(2)}) async-start(bf16[16,8,8,256]{3,2,1,0:T(8,128)(2,1)} %copy_bitcast_fusion), calls=%async_computation.1 | async-start | bytes 1048576 | tf_op jit(solution)/shard_map/all_to_all | solution.py:583
  11.7 5.2 %freq_forward.1 = (bf16[4,256,256]{2,1,0:T(8,128)(2,1)}, bf16[4,256,256]{2,1,0:T(8,128)(2,1)}, bf16[4,256,256]{2,1,0:T(8,128)(2,1)}, bf16[4,256,256]{2,1,0:T(8,1...) custom-call(s32[2]{0:T(128)S(1)} %pad_add_fusion.place_ref, ...), custom_call_target="tpu_custom_call" | custom-call | flops 64424509440 | bytes 2097152 | tf_op jit(solution)/shard_map/freq_forward/pallas_call | solution.py:208
  16.9 9.1 %all-to-all-done.1 = bf16[16,8,8,256]{3,2,1,0:T(8,128)(2,1)S(1)} async-done(((bf16[16,8,8,256]{3,2,1,0:T(8,128)(2,1)}), bf16[16,8,8,256]{3,2,1,0:T(8,128)(2,1)S(1)}, u32[]{:S(2)}, u32[]{:S(2)}) %all-to-all-start.1) | async-done | bytes 524320 | tf_op jit(solution)/shard_map/all_to_all | solution.py:583
  26.0 3.1 %all-to-all-start = ((bf16[32,32,256]{2,1,0:T(8,128)(2,1)}), bf16[32,32,256]{2,1,0:T(8,128)(2,1)S(1)}, u32[]{:S(2)}, u32[]{:S(2)}) async-start(bf16[32,32,256]{2,1,0:T(8,128)(2,1)} %bitcast.58), calls=%async_computation | async-start | bytes 1048576 | tf_op jit(solution)/shard_map/all_to_all | solution.py:588
  29.1 1.1 slice.23.w_ref
  30.2 13.9 %all-to-all-done = bf16[32,32,256]{2,1,0:T(8,128)(2,1)S(1)} async-done(((bf16[32,32,256]{2,1,0:T(8,128)(2,1)}), bf16[32,32,256]{2,1,0:T(8,128)(2,1)S(1)}, u32[]{:S(2)}, u32[]{:S(2)}) %all-to-all-start) | async-done | bytes 524320 | tf_op jit(solution)/shard_map/all_to_all | solution.py:588
  44.1 7.8 %time_attention.1 = (bf16[1024,256]{1,0:T(8,128)(2,1)}, bf16[2,256,256]{2,1,0:T(8,128)(2,1)S(1)}, bf16[2,256,256]{2,1,0:T(8,128)(2,1)S(1)}, f32[1,256]{1,0:T(1,128)S(1)}) custom-call(s32[2]{0:T(128)S(1)} %pad_add_fusion.place_ref, s32[1]{0:T(128)} %bitcast.5.first_ref, bf16[1024,256]{1,0:T(8,128)(2,1)S(1)} %bitcast.45, bf16[1024,256]{1,0:T(8,128)(2,1)S(1)} %bitcast.43, ...), custom_call_target="tpu_custom_call" | custom-call | flops 3087007744 | bytes 4194304 | tf_op jit(solution)/shard_map/time_attention/pallas_call | solution.py:463
  51.9 1.1 collective-permute-start.3
  53.0 2.8 %all-to-all-start.2 = ((bf16[32,32,256]{2,1,0:T(8,128)(2,1)}), bf16[32,32,256]{2,1,0:T(8,128)(2,1)S(1)}, u32[]{:S(2)}, u32[]{:S(2)}) async-start(bf16[32,32,256]{2,1,0:T(8,128)(2,1)} %bitcast.57), calls=%async_computation.2 | async-start | bytes 1048576 | tf_op jit(solution)/shard_map/all_to_all | solution.py:588
  56.0 1.7 %collective-permute-start.4 = (bf16[2,128,256]{2,1,0:T(8,128)(2,1)S(1)}, bf16[2,128,256]{2,1,0:T(8,128)(2,1)S(1)}, u32[]{:S(2)}, u32[]{:S(2)}) collective-permute-start(bf16[2,128,256]{2,1,0:T(8,128)(2,1)S(1)} %dynamic-slice_bitcast_fusion), channel_id=1, source_target_pairs={{0,4},{2,6},{4,0},{6,2},{8,12},{10,14},{12,8},{14,10},{16,20},{18,... | collective-permute-start | bytes 393224 | tf_op jit(solution)/shard_map/ppermute | solution.py:657
  57.7 7.6 %collective-permute-done.4 = bf16[2,128,256]{2,1,0:T(8,128)(2,1)S(1)} collective-permute-done((bf16[2,128,256]{2,1,0:T(8,128)(2,1)S(1)}, bf16[2,128,256]{2,1,0:T(8,128)(2,1)S(1)}, u32[]{:S(2)}, u32[]{:S(2)}) %collective-permute-start.4) | collective-permute-done | bytes 131104 | tf_op jit(solution)/shard_map/ppermute | solution.py:657
  65.3 2.2 %collective-permute-start.5 = (bf16[128,256]{1,0:T(8,128)(2,1)S(1)}, bf16[128,256]{1,0:T(8,128)(2,1)S(1)}, u32[]{:S(2)}, u32[]{:S(2)}) collective-permute-start(bf16[128,256]{1,0:T(8,128)(2,1)S(1)} %dynamic-slice_bitcast_fusion.1), channel_id=1, source_target_pairs={{0,1},{1,0},{2,3},{3,2},{4,5},{5,4},{6,7},{7,6},{8,9},{9,8},{10,11... | collective-permute-start | bytes 196616 | tf_op jit(solution)/shard_map/ppermute | solution.py:657
  67.5 3.2 %all-to-all-done.2 = bf16[32,32,256]{2,1,0:T(8,128)(2,1)S(1)} async-done(((bf16[32,32,256]{2,1,0:T(8,128)(2,1)}), bf16[32,32,256]{2,1,0:T(8,128)(2,1)S(1)}, u32[]{:S(2)}, u32[]{:S(2)}) %all-to-all-start.2) | async-done | bytes 524320 | tf_op jit(solution)/shard_map/all_to_all | solution.py:588
  70.7 6.2 %freq_backward.1 = (bf16[4,128,256]{2,1,0:T(8,128)(2,1)S(1)}, bf16[1,4,128,256]{3,2,1,0:T(8,128)(2,1)S(1)}, bf16[2,256,256]{2,1,0:T(8,128)(2,1)S(1)}, bf16[528,256]{1,0:T(8,128)(2,1)S(1)}, f32[16,256]{1,0:T(8,128)S(1)}) custom-call(s32[2]{0:T(128)S(1)} %pad_add_fusion.place_ref, bf16[2,4,128,256]{3,2,1,0:T(8,128)(2,1)} %bitcast.56, ...), custom_call_target="tpu_custom_call" | custom-call | flops 3221225472 | bytes 8388608 | tf_op jit(solution)/shard_map/freq_backward/pallas_call | solution.py:324
  77.0 1.1 collective-permute-start.2
  80.1 3.9 %all-to-all-start.3 = ((bf16[16,48,256]{2,1,0:T(8,128)(2,1)}), bf16[16,48,256]{2,1,0:T(8,128)(2,1)S(1)}, u32[]{:S(2)}, u32[]{:S(2)}) async-start(bf16[16,48,256]{2,1,0:T(8,128)(2,1)} %sums_by_peer.1), calls=%async_computation.3 | async-start | bytes 786432 | tf_op jit(solution)/shard_map/all_to_all | solution.py:662
  84.0 2.3 %collective-permute-done.1.refs_1_ = bf16[4,128,256]{2,1,0:T(8,128)(2,1)S(1)} collective-permute-done((bf16[4,128,256]{2,1,0:T(8,128)(2,1)S(1)}, bf16[4,128,256]{2,1,0:T(8,128)(2,1)S(1)}, u32[]{:S(2)}, u32[]{:S(2)}) %collective-permute-start.1) | collective-permute-done | bytes 262176 | tf_op jit(solution)/shard_map/ppermute | solution.py:605
  86.4 1.4 %place_frames.1 = bf16[2,4,128,256]{3,2,1,0:T(8,128)(2,1)} custom-call(s32[2]{0:T(128)S(1)} %pad_add_fusion.place_ref, bf16[4,128,256]{2,1,0:T(8,128)(2,1)S(1)} %get-tuple-element.36.refs_0_, bf16[4,128,256]{2,1,0:T(8,128)(2,1)S(1)} %collective-permute-done.1.refs_1_), custom_call_target="tpu_custom_call" | custom-call | flops 10000000000 | bytes 524288 | tf_op jit(solution)/shard_map/place_frames/pallas_call | solution.py:501
  87.8 9.3 %all-to-all-done.3 = bf16[16,48,256]{2,1,0:T(8,128)(2,1)S(1)} async-done(((bf16[16,48,256]{2,1,0:T(8,128)(2,1)}), bf16[16,48,256]{2,1,0:T(8,128)(2,1)S(1)}, u32[]{:S(2)}, u32[]{:S(2)}) %all-to-all-start.3) | async-done | bytes 393248 | tf_op jit(solution)/shard_map/all_to_all | solution.py:662
  97.2 17.9 %all_to_all.25 = bf16[16,64,256]{2,1,0:T(8,128)(2,1)S(1)} all-to-all(bf16[16,64,256]{2,1,0:T(8,128)(2,1)S(1)} %broadcast_in_dim.2), channel_id=1, replica_groups={{0,1,4,5,8,9,12,13,16,17,20,21,24,25,28,29},{2,3,6,7,10,11,14,15,18,19,..., dimensions={0} | all-to-all | bytes 1048576 | tf_op jit(solution)/shard_map/all_to_all | solution.py:662
  115.7 1.3 %collective-permute-done.6 = bf16[16,64,256]{2,1,0:T(8,128)(2,1)S(1)} collective-permute-done((bf16[16,64,256]{2,1,0:T(8,128)(2,1)S(1)}, bf16[16,64,256]{2,1,0:T(8,128)(2,1)S(1)}, u32[]{:S(2)}, u32[]{:S(2)}) %collective-permute-start.6) | collective-permute-done | bytes 524320 | tf_op jit(solution)/shard_map/ppermute | solution.py:690
  117.2 1.5 %maximum_convert_fusion = f32[8,256,256]{2,1,0:T(8,128)} fusion(bf16[4,256,256]{2,1,0:T(8,128)(2,1)S(1)} %bitcast.50, bf16[4,256,256]{2,1,0:T(8,128)(2,1)S(1)} %bitcast.51), kind=kLoop, calls=%fused_computation.2 | loop fusion | flops 1048576 | bytes 3145728 | tf_op jit(solution)/shard_map/convert_element_type | solution.py:698
  (37 shorter events, 4.1 us)
Async XLA Ops:
  0.6 4.2 %copy-start = (bf16[8,128,256]{2,1,0:T(8,128)(2,1)S(1)}, bf16[8,128,256]{2,1,0:T(8,128)(2,1)}, u32[]{:S(2)}) copy-start(bf16[8,128,256]{2,1,0:T(8,128)(2,1)} %param.5) | copy-start | bytes 1572868
  0.6 10.9 %copy-start.3 = (bf16[8,256,256]{2,1,0:T(8,128)(2,1)S(1)}, bf16[8,256,256]{2,1,0:T(8,128)(2,1)}, u32[]{:S(2)}) copy-start(bf16[8,256,256]{2,1,0:T(8,128)(2,1)} %param.6) | copy-start | bytes 3145732
  0.7 11.1 %copy-start.2 = (f32[2,256]{1,0:T(2,128)S(1)}, f32[2,256]{1,0:T(2,128)}, u32[]{:S(2)}) copy-start(f32[2,256]{1,0:T(2,128)} %gain_ref.5) | copy-start | bytes 6148
  1.8 10.0 %collective-permute-start = (bf16[4,128,256]{2,1,0:T(8,128)(2,1)S(1)}, bf16[4,128,256]{2,1,0:T(8,128)(2,1)S(1)}, u32[]{:S(2)}, u32[]{:S(2)}) collective-permute-start(bf16[4,128,256]{2,1,0:T(8,128)(2,1)S(1)} %bitcast.46), channel_id=1, source_target_pairs={{0,1},{1,0},{2,3},{3,2},{4,5},{5,4},{6,7},{7,6},{8,9},{9,8},{10,11... | collective-permute-start | bytes 786440 | tf_op jit(solution)/shard_map/ppermute | solution.py:605
  5.7 20.4 %all-to-all-start.1 = ((bf16[16,8,8,256]{3,2,1,0:T(8,128)(2,1)}), bf16[16,8,8,256]{3,2,1,0:T(8,128)(2,1)S(1)}, u32[]{:S(2)}, u32[]{:S(2)}) async-start(bf16[16,8,8,256]{3,2,1,0:T(8,128)(2,1)} %copy_bitcast_fusion), calls=%async_computation.1 | async-start | bytes 1048576 | tf_op jit(solution)/shard_map/all_to_all | solution.py:583
  11.7 5.2 %copy-start.1 = (bf16[4,128,256]{2,1,0:T(8,128)(2,1)}, bf16[4,128,256]{2,1,0:T(8,128)(2,1)S(1)}, u32[]{:S(2)}) copy-start(bf16[4,128,256]{2,1,0:T(8,128)(2,1)S(1)} %collective-permute-done) | copy-start | bytes 786436
  26.0 18.1 %all-to-all-start = ((bf16[32,32,256]{2,1,0:T(8,128)(2,1)}), bf16[32,32,256]{2,1,0:T(8,128)(2,1)S(1)}, u32[]{:S(2)}, u32[]{:S(2)}) async-start(bf16[32,32,256]{2,1,0:T(8,128)(2,1)} %bitcast.58), calls=%async_computation | async-start | bytes 1048576 | tf_op jit(solution)/shard_map/all_to_all | solution.py:588
  51.9 4.0 %collective-permute-start.3 = (bf16[2,256,256]{2,1,0:T(8,128)(2,1)S(1)}, bf16[2,256,256]{2,1,0:T(8,128)(2,1)S(1)}, u32[]{:S(2)}, u32[]{:S(2)}) collective-permute-start(bf16[2,256,256]{2,1,0:T(8,128)(2,1)S(1)} %get-tuple-element.41), channel_id=1, source_target_pairs={{0,2},{2,0},{4,6},{6,4},{8,10},{10,8},{12,14},{14,12},{16,18},{18,... | collective-permute-start | bytes 786440 | tf_op jit(solution)/shard_map/ppermute | solution.py:666
  53.0 17.7 %all-to-all-start.2 = ((bf16[32,32,256]{2,1,0:T(8,128)(2,1)}), bf16[32,32,256]{2,1,0:T(8,128)(2,1)S(1)}, u32[]{:S(2)}, u32[]{:S(2)}) async-start(bf16[32,32,256]{2,1,0:T(8,128)(2,1)} %bitcast.57), calls=%async_computation.2 | async-start | bytes 1048576 | tf_op jit(solution)/shard_map/all_to_all | solution.py:588
  56.0 9.2 %collective-permute-start.4 = (bf16[2,128,256]{2,1,0:T(8,128)(2,1)S(1)}, bf16[2,128,256]{2,1,0:T(8,128)(2,1)S(1)}, u32[]{:S(2)}, u32[]{:S(2)}) collective-permute-start(bf16[2,128,256]{2,1,0:T(8,128)(2,1)S(1)} %dynamic-slice_bitcast_fusion), channel_id=1, source_target_pairs={{0,4},{2,6},{4,0},{6,2},{8,12},{10,14},{12,8},{14,10},{16,20},{18,... | collective-permute-start | bytes 393224 | tf_op jit(solution)/shard_map/ppermute | solution.py:657
  65.3 13.6 %collective-permute-start.5 = (bf16[128,256]{1,0:T(8,128)(2,1)S(1)}, bf16[128,256]{1,0:T(8,128)(2,1)S(1)}, u32[]{:S(2)}, u32[]{:S(2)}) collective-permute-start(bf16[128,256]{1,0:T(8,128)(2,1)S(1)} %dynamic-slice_bitcast_fusion.1), channel_id=1, source_target_pairs={{0,1},{1,0},{2,3},{3,2},{4,5},{5,4},{6,7},{7,6},{8,9},{9,8},{10,11... | collective-permute-start | bytes 196616 | tf_op jit(solution)/shard_map/ppermute | solution.py:657
  77.0 2.3 %collective-permute-start.2 = (bf16[528,256]{1,0:T(8,128)(2,1)S(1)}, bf16[528,256]{1,0:T(8,128)(2,1)S(1)}, u32[]{:S(2)}, u32[]{:S(2)}) collective-permute-start(bf16[528,256]{1,0:T(8,128)(2,1)S(1)} %get-tuple-element.39), channel_id=1, source_target_pairs={{0,2},{2,0},{4,6},{6,4},{8,10},{10,8},{12,14},{14,12},{16,18},{18,... | collective-permute-start | bytes 811016 | tf_op jit(solution)/shard_map/ppermute | solution.py:671
  78.1 8.3 %collective-permute-start.1 = (bf16[4,128,256]{2,1,0:T(8,128)(2,1)S(1)}, bf16[4,128,256]{2,1,0:T(8,128)(2,1)S(1)}, u32[]{:S(2)}, u32[]{:S(2)}) collective-permute-start(bf16[4,128,256]{2,1,0:T(8,128)(2,1)S(1)} %bitcast.49), channel_id=1, source_target_pairs={{0,1},{1,0},{2,3},{3,2},{4,5},{5,4},{6,7},{7,6},{8,9},{9,8},{10,11... | collective-permute-start | bytes 786440 | tf_op jit(solution)/shard_map/ppermute | solution.py:605
  80.1 16.9 %all-to-all-start.3 = ((bf16[16,48,256]{2,1,0:T(8,128)(2,1)}), bf16[16,48,256]{2,1,0:T(8,128)(2,1)S(1)}, u32[]{:S(2)}, u32[]{:S(2)}) async-start(bf16[16,48,256]{2,1,0:T(8,128)(2,1)} %sums_by_peer.1), calls=%async_computation.3 | async-start | bytes 786432 | tf_op jit(solution)/shard_map/all_to_all | solution.py:662
  115.1 1.9 %collective-permute-start.6 = (bf16[16,64,256]{2,1,0:T(8,128)(2,1)S(1)}, bf16[16,64,256]{2,1,0:T(8,128)(2,1)S(1)}, u32[]{:S(2)}, u32[]{:S(2)}) collective-permute-start(bf16[16,64,256]{2,1,0:T(8,128)(2,1)S(1)} %all_to_all.25), channel_id=1, source_target_pairs={{0,2},{2,0},{4,6},{6,4},{8,10},{10,8},{12,14},{14,12},{16,18},{18,... | collective-permute-start | bytes 1572872 | tf_op jit(solution)/shard_map/ppermute | solution.py:690
